TPU v7x, 128 devices: a whole 4x4x4 slice. The times are simulated.
128 devices in a mesh: section: 2 (over z_hi), dp: 16 (over y, z_lo, core), tensor: 4 (over x).
Axes of the slice: x: 4, y: 4, z: 4 (z_hi: 2, z_lo: 2; z = z_hi * 2 + z_lo), core: 2. Of those that a mesh axis runs over, the one named last changes fastest.
Arguments:
- features: bfloat16 [4, 8192, 1280], P('section', ('dp', 'tensor')), may hold values from -6 to 6
- layer_norm_gain: float32 [4, 1280], P('section'), may hold values from 0.1 to 1.9
- layer_norm_bias: float32 [4, 1280], P('section'), may hold values from -3 to 3
- proj_weight: bfloat16 [5120, 8192], P('section', 'tensor'), may hold values from -0.078125 to 0.078125
- cotangent: bfloat16 [16, 512, 8192], P('dp', 'section', 'tensor'), may hold values from -6 to 6
Outputs:
- projected: bfloat16 [16, 512, 8192], P('dp', 'section', 'tensor')
- weight_grad: bfloat16 [5120, 8192], P('section', 'tensor')
- hidden_state_gradient: bfloat16 [4, 8192, 1280], P('section', ('dp', 'tensor'))
All inputs are finite; a program needn't handle non-finite values.
Results may differ from a plain program's by a relative error of at most 0.022.
Values may be sent and summed in bfloat16 or wider, within the bound.
No kernel may reach another device: no remote copies, remote signals or barrier semaphores. Data moves between devices by JAX's collectives and lax.ppermute only.
A program may use at most 128 MiB of HBM per device.

v0:
```python
import jax
import jax.numpy as jnp
from jax import lax
from jax.sharding import PartitionSpec as P


def body(features, layer_norm_gain, layer_norm_bias, proj_weight, cotangent):
    x = features.astype(jnp.float32)
    mu = jnp.mean(x, axis=-1, keepdims=True)
    centered_rows = x - mu
    inverse_deviation = 1.0 / jnp.sqrt(
        jnp.mean(centered_rows * centered_rows, axis=-1, keepdims=True) + 1e-05
    )
    standardized_input = centered_rows * inverse_deviation
    norm_output = (
        standardized_input * layer_norm_gain[:, None, :] + layer_norm_bias[:, None, :]
    ).astype(jnp.bfloat16)
    taps_here, width = layer_norm_gain.shape
    out_cols = proj_weight.shape[1]
    weight = proj_weight.reshape(taps_here, width, out_cols)
    gathered = lax.all_gather(norm_output, "tensor", axis=1, tiled=True)
    rows = gathered
    projected = lax.psum_scatter(
        jnp.einsum("lrc,lco->ro", rows, weight, preferred_element_type=jnp.float32).astype(
            jnp.bfloat16
        ),
        "section",
        scatter_dimension=0,
        tiled=True,
    ).astype(jnp.float32)
    projected = projected.astype(jnp.bfloat16)[None]
    grads = lax.all_gather(cotangent, "section", axis=1, tiled=True)[0]
    partial_value = jnp.einsum("lrc,ro->lco", gathered, grads, preferred_element_type=jnp.float32)
    summed = lax.psum(partial_value.astype(jnp.bfloat16), "dp")
    weight_grad = summed.reshape(taps_here * width, out_cols)
    rows = grads
    dnorm = lax.psum_scatter(
        jnp.einsum("ro,lco->rlc", rows, weight, preferred_element_type=jnp.float32).astype(
            jnp.bfloat16
        ),
        "tensor",
        scatter_dimension=0,
        tiled=True,
    ).astype(jnp.float32)
    dnorm = jnp.transpose(dnorm, (1, 0, 2))
    gain_scaled = dnorm * layer_norm_gain[:, None, :]
    hidden_state_gradient = inverse_deviation * (
        gain_scaled
        - jnp.mean(gain_scaled, axis=-1, keepdims=True)
        - standardized_input * jnp.mean(gain_scaled * standardized_input, axis=-1, keepdims=True)
    )
    return (projected, weight_grad, hidden_state_gradient.astype(jnp.bfloat16))


def solution(mesh):
    return jax.shard_map(
        body,
        mesh=mesh,
        in_specs=(
            P("section", ("dp", "tensor"), None),
            P("section", None),
            P("section", None),
            P("section", "tensor"),
            P("dp", "section", "tensor"),
        ),
        out_specs=(
            P("dp", "section", "tensor"),
            P("section", "tensor"),
            P("section", ("dp", "tensor"), None),
        ),
        check_vma=False,
    )
```

profile of v0, /device:TPU:1, one launch (start us, length us, event | category | flops | bytes accessed | tf_op | source)
XLA Modules:
  0.0 435.6 jit_solution(10492214980139114581)
XLA Ops:
  7.2 0.0 all-gather.5.cloned.1.call-start
  7.2 0.7 all-gather.5.cloned.1.call-update
  7.9 0.0 reduce-scatter.5.cloned.1.call-start
  7.9 42.3 %all-gather.5.cloned.1.call-done = bf16[1,512,2048]{2,1,0:T(8,128)(2,1)} async-done(((bf16[1,256,2048]{2,1,0:T(8,128)(2,1)}), bf16[1,512,2048]{2,1,0:T(8,128)(2,1)}) %all-gather.5.cloned.1.call-update) | async-done | bytes 2097168 | tf_op jit(solution)/shard_map/all_gather | solution.py:32
  50.2 10.1 %convolution_convert_fusion.1 = bf16[512,2,1280]{2,0,1:T(8,128)(2,1)} fusion(bf16[2,1280,2048]{2,1,0:T(8,128)(2,1)} %bitcast.22, bf16[1,512,2048]{2,1,0:T(8,128)(2,1)} %all-gather.5.cloned.1.call-done), kind=kOutput, calls=%fused_computation.2 | convolution fusion | flops 5370019840 | bytes 15204352 | tf_op jit(solution)/shard_map/ro,lco->rlc/dot_general | solution.py:38
  60.3 0.0 reduce-scatter.5.cloned.1.call-update
  60.3 0.0 all-gather.3.cloned.1.call-start
  60.4 1.0 copy-done
  61.4 0.2 convert_reduce_fusion
  61.5 0.3 fusion.13
  61.9 31.8 %reduce-scatter.5.cloned.1.call-done = bf16[128,2,1280]{2,0,1:T(8,128)(2,1)} async-done(((bf16[512,2,1280]{2,0,1:T(8,128)(2,1)}), bf16[128,2,1280]{2,0,1:T(8,128)(2,1)}) %reduce-scatter.5.cloned.1.call-update) | async-done | bytes 655376 | tf_op jit(solution)/shard_map/reduce_scatter | solution.py:37
  93.6 1.5 bitcast_reduce_fusion
  95.2 2.7 fusion.12
  97.9 0.0 all-gather.3.cloned.1.call-update
  97.9 0.0 reduce-scatter.3.cloned.1.call-start
  98.0 34.9 %all-gather.3.cloned.1.call-done = bf16[2,512,1280]{2,1,0:T(8,128)(2,1)} async-done(((bf16[2,128,1280]{2,1,0:T(8,128)(2,1)}), bf16[2,512,1280]{2,1,0:T(8,128)(2,1)}) %all-gather.3.cloned.1.call-update) | async-done | bytes 2621456 | tf_op jit(solution)/shard_map/all_gather | solution.py:21
  132.9 11.3 %bitcast_convert_fusion = bf16[512,2048]{1,0:T(8,128)(2,1)} fusion(bf16[2,512,1280]{2,1,0:T(8,128)(2,1)} %all-gather.3.cloned.1.call-done, bf16[2,1280,2048]{2,1,0:T(8,128)(2,1)} %bitcast.23), kind=kOutput, calls=%fused_computation.1 | convolution fusion | flops 5369757696 | bytes 15204352 | tf_op jit(solution)/shard_map/lrc,lco->ro/dot_general | solution.py:24
  144.3 0.0 reduce-scatter.3.cloned.1.call-update
  144.3 0.0 all-reduce.2.cloned.1.call-start
  144.3 9.9 %convolution_convert_fusion = bf16[2,1280,2048]{2,1,0:T(8,128)(2,1)} fusion(bf16[2,512,1280]{2,1,0:T(8,128)(2,1)S(1)} %copy-done.3, bf16[1,512,2048]{2,1,0:T(8,128)(2,1)} %all-gather.5.cloned.1.call-done), kind=kOutput, calls=%fused_computation | convolution fusion | flops 5373952000 | bytes 15204352 | tf_op jit(solution)/shard_map/lrc,ro->lco/dot_general | solution.py:33
  154.3 0.0 all-reduce.2.cloned.1.call-update
  154.3 26.3 %reduce-scatter.3.cloned.1.call-done = bf16[256,2048]{1,0:T(8,128)(2,1)} async-done(((bf16[512,2048]{1,0:T(8,128)(2,1)}), bf16[256,2048]{1,0:T(8,128)(2,1)}) %reduce-scatter.3.cloned.1.call-update) | async-done | bytes 1048592 | tf_op jit(solution)/shard_map/reduce_scatter | solution.py:23
  180.6 238.3 %all-reduce.2.cloned.1.call-done = bf16[2560,2048]{1,0:T(8,128)(2,1)} async-done(((bf16[2560,2048]{1,0:T(8,128)(2,1)}), bf16[2560,2048]{1,0:T(8,128)(2,1)}) %all-reduce.2.cloned.1.call-update) | async-done | bytes 10485776 | tf_op jit(solution)/shard_map/psum | solution.py:34
  418.8 10.3 %copy.11 = bf16[2560,2048]{1,0:T(8,128)(2,1)} copy(bf16[2560,2048]{1,0:T(8,128)(2,1)} %all-reduce.2.cloned.1.call-done) | data formatting | bytes 20971520
  (10 shorter events, 0.0 us)
Async XLA Ops:
  7.2 43.0 %all-gather.5.cloned.1.call-start = ((), (), s32[]{:S(2)}) async-start(), calls=%async_computation.4 | async-start | bytes 3145728 | tf_op jit(solution)/shard_map/all_gather | solution.py:32
  7.9 85.7 %reduce-scatter.5.cloned.1.call-start = ((), (), s32[]{:S(2)}) async-start(), calls=%async_computation.6 | async-start | bytes 3276800 | tf_op jit(solution)/shard_map/reduce_scatter | solution.py:37
  60.3 1.1 copy-start
  60.3 33.4 %copy-start.1 = (f32[2,1280]{1,0:T(2,128)S(1)}, f32[2,1280]{1,0:T(2,128)}, u32[]{:S(2)}) copy-start(f32[2,1280]{1,0:T(2,128)} %param.6) | copy-start | bytes 30724
  60.3 34.9 %copy-start.2 = (f32[2,1280]{1,0:T(2,128)S(1)}, f32[2,1280]{1,0:T(2,128)}, u32[]{:S(2)}) copy-start(f32[2,1280]{1,0:T(2,128)} %param.7) | copy-start | bytes 30724
  60.3 72.6 %all-gather.3.cloned.1.call-start = ((), (), s32[]{:S(2)}) async-start(), calls=%async_computation.2 | async-start | bytes 3276800 | tf_op jit(solution)/shard_map/all_gather | solution.py:21
  97.9 82.6 %reduce-scatter.3.cloned.1.call-start = ((), (), s32[]{:S(2)}) async-start(), calls=%async_computation.3 | async-start | bytes 3145728 | tf_op jit(solution)/shard_map/reduce_scatter | solution.py:23
  132.9 11.4 %copy-start.3 = (bf16[2,512,1280]{2,1,0:T(8,128)(2,1)S(1)}, bf16[2,512,1280]{2,1,0:T(8,128)(2,1)}, u32[]{:S(2)}) copy-start(bf16[2,512,1280]{2,1,0:T(8,128)(2,1)} %all-gather.3.cloned.1.call-done) | copy-start | bytes 7864324
  144.3 274.6 %all-reduce.2.cloned.1.call-start = ((), (), s32[]{:S(2)}) async-start(), calls=%async_computation.5 | async-start | bytes 20971520 | tf_op jit(solution)/shard_map/psum | solution.py:34
Sparse Core Ops, SparseCore 0:
  9.7 40.5 all-gather.4
  60.4 33.1 reduce-scatter.4
  98.1 34.8 all-gather.2
  144.4 36.1 reduce-scatter.2
  183.7 235.1 all-reduce.1
where the time goes:
time: 436 us
  waiting for transfers between devices  374 us (86%)
  matrix products  31.3 us (7%)
  between operations  13.8 us (3%)
  local copies, waits for them, and re-layouts  11.3 us (3%)
  other arithmetic  4.75 us (1%)
    psum x1, waiting for transfers between devices, body(): summed = lax.psum(partial_value.astype(jnp.bfloat16), 'dp')  238 us
    all_gather x1, waiting for transfers between devices, body(): grads = lax.all_gather(cotangent, 'section', axis=1, tiled=True)[0]  42.3 us
    all_gather x1, waiting for transfers between devices, body(): gathered = lax.all_gather(norm_output, 'tensor', axis=1, tiled=True)  34.9 us
    reduce_scatter x1, waiting for transfers between devices, body(): lax.psum_scatter(jnp.einsum('ro,lco->rlc', rows, weight, preferred_elemen...  31.8 us
    reduce_scatter x1, waiting for transfers between devices, body(): lax.psum_scatter(jnp.einsum('lrc,lco->ro', rows, weight, preferred_elemen...  26.3 us
    dot_general x1, matrix products, body(): jnp.einsum('lrc,lco->ro', rows, weight, preferred_element_type=jnp.float32)  11.3 us
    unnamed x9, local copies, waits for them, and re-layouts  11.3 us
    dot_general x1, matrix products, body(): jnp.einsum('ro,lco->rlc', rows, weight, preferred_element_type=jnp.float32)  10.1 us
  transfers between devices with their start and end apart: 5, of which 5 were waited for; matrix products, arithmetic and copies ran while one was open for 2% of the time, Pallas kernels for 0%

commit v1 on v0

v1 whole, which is shorter than its diff:
```python
import jax
import jax.numpy as jnp
from jax import lax
from jax.experimental import pallas as pl
from jax.experimental.pallas import tpu as pltpu
from jax.sharding import PartitionSpec as P

F32 = jnp.float32
BF16 = jnp.bfloat16
VMEM_LIMIT = 48 * 1024 * 1024

ROW_CHUNKS = ((0, 512), (512, 768))


def dp_pairs(fy=lambda y: y, fz=lambda z: z, fc=lambda c: c):
    return [(i, fy(i // 4) * 4 + fz(i // 2 % 2) * 2 + fc(i % 2)) for i in range(16)]


Y1 = dp_pairs(fy=lambda y: y ^ 1)
Y3 = dp_pairs(fy=lambda y: y ^ 3)
ZLO = dp_pairs(fz=lambda z: z ^ 1)
CORE = dp_pairs(fc=lambda c: c ^ 1)
SECTION = [(0, 1), (1, 0)]
AROUND, SLOTS = 1, 5


def shift(step):
    return [(i, (i + step) % 4) for i in range(4)]


def swap(value, pairs, axis="dp"):
    return lax.ppermute(value, axis, pairs)


def index_vector():
    s, d, x = lax.axis_index("section"), lax.axis_index("dp"), lax.axis_index("tensor")
    y = d // 4
    slots = [(t // 2 ^ s) * 2 + t % 2 for t in (x, (x + 1) % 4, (x + 3) % 4, (x + 2) % 4)]
    return jnp.stack([d % 2, y, y ^ 1, y ^ 2, y ^ 3, *slots]).astype(jnp.int32)


def call(kernel, index, operands, in_specs, out_shapes, out_specs, grid, flops=0, scratch=(), aliases=None):
    read = sum(a.size * a.dtype.itemsize for a in operands)
    written = sum(a.size * a.dtype.itemsize for a in out_shapes)
    return pl.pallas_call(
        kernel,
        grid_spec=pltpu.PrefetchScalarGridSpec(
            num_scalar_prefetch=1,
            grid=grid,
            in_specs=in_specs,
            out_specs=out_specs,
            scratch_shapes=scratch,
        ),
        out_shape=out_shapes,
        input_output_aliases=aliases or {},
        compiler_params=pltpu.CompilerParams(vmem_limit_bytes=VMEM_LIMIT),
        cost_estimate=pl.CostEstimate(flops=flops, bytes_accessed=read + written, transcendentals=0),
    )(index, *operands)


def full(array):
    return pl.BlockSpec(array.shape, lambda *_: (0,) * len(array.shape))


def out(*shape, dtype=BF16):
    return jax.ShapeDtypeStruct(shape, dtype)


def dot(a, b, contract=(1, 0)):
    return lax.dot_general(a, b, (((contract[0],), (contract[1],)), ((), ())), preferred_element_type=F32)


def moments(value):
    mean = jnp.mean(value, axis=-1, keepdims=True)
    centered = value - mean
    inverse = 1.0 / jnp.sqrt(jnp.mean(centered * centered, axis=-1, keepdims=True) + 1e-05)
    return centered * inverse, inverse


def normalize(index, features, theirs, gain, bias):
    _, rows, width = features.shape

    def kernel(index_ref, own_ref, theirs_ref, gain_ref, bias_ref, *outs):
        c = index_ref[0]
        gain, bias = gain_ref[pl.ds(c, 1)], bias_ref[pl.ds(c, 1)]
        for k, value in enumerate((own_ref[0], theirs_ref[...])):
            standard, _ = moments(value.astype(F32))
            normed = (standard * gain + bias).astype(BF16)
            for (start, size), out_ref in zip(ROW_CHUNKS, outs):
                out_ref[k] = normed[:, start : start + size]

    shapes = [out(2, rows, size) for _, size in ROW_CHUNKS]
    return call(
        kernel,
        index,
        [features, theirs, gain, bias],
        [pl.BlockSpec((1, rows, width), lambda i, idx: (idx[0], 0, 0)), full(theirs), full(gain), full(bias)],
        shapes,
        [full(s) for s in shapes],
        (1,),
    )


def normalize_backward(index, features, theirs, gain, parts):
    _, rows, width = features.shape

    def kernel(index_ref, own_ref, theirs_ref, gain_ref, *refs):
        gain = gain_ref[pl.ds(index_ref[0], 1)]
        for k, value in enumerate((own_ref[0], theirs_ref[...])):
            standard, inverse = moments(value.astype(F32))
            total = refs[0][k].astype(F32)
            for ref in refs[1:-1]:
                total = total + ref[k].astype(F32)
            scaled = total * gain
            hidden = inverse * (
                scaled
                - jnp.mean(scaled, axis=-1, keepdims=True)
                - standard * jnp.mean(scaled * standard, axis=-1, keepdims=True)
            )
            refs[-1][k] = hidden.astype(BF16)

    shape = out(2, rows, width)
    return call(
        kernel,
        index,
        [features, theirs, gain, *parts],
        [pl.BlockSpec((1, rows, width), lambda i, idx: (idx[0], 0, 0)), full(theirs), full(gain)]
        + [full(p) for p in parts],
        [shape],
        [full(shape)],
        (1,),
    )[0]


def transpose_pieces(index_ref, pieces, scratch):
    for n, piece in enumerate(pieces):
        for k in range(2):
            at = pl.multiple_of((4 * k + index_ref[SLOTS + n]) * 128, 128)
            scratch[:, pl.ds(at, 128)] = piece[k].T


def weight_grad_blocks(index, pieces, grads, blocks, wanted):
    rows = pieces[0].shape[2]
    half = rows // 2
    part = grads[0].shape[1] // 4
    steps = len(blocks)

    def kernel(index_ref, *refs):
        ins, gs = refs[:4], refs[4:8]
        outs, scratch = refs[8:-1], refs[-1]
        step = pl.program_id(0)

        @pl.when(step == 0)
        def _():
            transpose_pieces(index_ref, ins, scratch)

        for k, block in enumerate(blocks):
            @pl.when(step == k)
            def _(block=block):
                for which, out_ref in zip(wanted, outs):
                    h, held, dtype = which
                    if block not in held:
                        continue
                    mine = scratch[h * half : (h + 1) * half]
                    total = dot(mine[:, :256], gs[0][...])
                    for p in range(1, 4):
                        total = total + dot(mine[:, 256 * p : 256 * (p + 1)], gs[p][...])
                    out_ref[...] = total.astype(dtype)

    def pick(values):
        def index_map(i, idx):
            result = jnp.int32(values[0])
            for k in range(1, steps):
                result = jnp.where(i >= k, jnp.int32(values[k]), result)
            return (0, result)

        return index_map

    out_specs = []
    for h, held, _ in wanted:
        place, last = [], 0
        for block in blocks:
            if block in held:
                last = held.index(block)
            place.append(last)
        out_specs.append(pl.BlockSpec((half, part), pick(place)))
    shapes = [out(half, len(held) * part, dtype=dtype) for _, held, dtype in wanted]
    return call(
        kernel,
        index,
        [*pieces, *grads],
        [full(p) for p in pieces] + [pl.BlockSpec((256, part), pick(blocks))] * 4,
        shapes,
        out_specs,
        (steps,),
        flops=2 * 1024 * half * part * sum(len(held) for _, held, _ in wanted),
        scratch=[pltpu.VMEM((rows, 1024), BF16)],
    )


def row_gradients(index, grads, proj_weight):
    part = grads[0].shape[1] // 4
    width = proj_weight.shape[0] // 2

    def kernel(index_ref, *refs):
        gs, w, outs, acc = refs[:4], refs[4], refs[5:9], refs[9]
        step = pl.program_id(0)
        for p in range(4):
            rows = slice(256 * p, 256 * (p + 1))
            value = dot(gs[p][...], w[...], (1, 1))

            @pl.when(step == 0)
            def _():
                acc[rows] = value

            @pl.when(step > 0)
            def _():
                acc[rows] = acc[rows] + value

        @pl.when(step == 3)
        def _():
            for n, out_ref in enumerate(outs):
                for k in range(2):
                    at = pl.multiple_of((4 * k + index_ref[SLOTS + n]) * 128, 128)
                    out_ref[k] = acc[pl.ds(at, 128)].astype(BF16)

    shapes = [out(2, 128, width)] * 4
    return call(
        kernel,
        index,
        [*grads, proj_weight],
        [pl.BlockSpec((256, part), lambda i, idx: (0, i))] * 4
        + [pl.BlockSpec((width, part), lambda i, idx: (idx[0], idx[AROUND + i]))],
        shapes,
        [full(s) for s in shapes],
        (4,),
        flops=2 * 1024 * width * part * 4,
        scratch=[pltpu.VMEM((1024, width), F32)],
    )


def project(index, chunks, proj_weight):
    width, cols = proj_weight.shape[0] // 2, proj_weight.shape[1]
    part = cols // 4
    count = len(chunks)

    def kernel(index_ref, *refs):
        ins, w, own, other, scratch = refs[: 4 * count], refs[-4], refs[-3], refs[-2], refs[-1]

        @pl.when(pl.program_id(0) == 0)
        def _():
            for m, (start, size) in enumerate(ROW_CHUNKS):
                for n in range(4):
                    for k in range(2):
                        at = pl.multiple_of((4 * k + index_ref[SLOTS + n]) * 128, 128)
                        scratch[pl.ds(at, 128), start : start + size] = ins[4 * m + n][k]

        own[...] = dot(scratch[:512], w[...]).astype(BF16)
        other[...] = dot(scratch[512:], w[...]).astype(BF16)

    operands = [piece for chunk in chunks for piece in chunk]
    shapes = [out(512, cols)] * 2
    return call(
        kernel,
        index,
        [*operands, proj_weight],
        [full(p) for p in operands] + [pl.BlockSpec((width, part), lambda i, idx: (idx[0], i))],
        shapes,
        [pl.BlockSpec((512, part), lambda i, idx: (0, i))] * 2,
        (4,),
        flops=2 * 1024 * width * cols,
        scratch=[pltpu.VMEM((1024, width), BF16)],
    )


def place(index, pieces, start, size, width, cols, into):
    half, part = size // 2, cols // 4
    count = len(pieces)

    def kernel(index_ref, *refs):
        sources, result, sems = refs[:count], refs[-2], refs[-1]
        c = index_ref[0]
        at = [pl.ds(pl.multiple_of(index_ref[AROUND + j] * part, part), part) for j in range(4)]
        left, right, every = slice(0, part), slice(part, 2 * part), slice(None)
        copies = []
        for k, tap in enumerate((c, 1 - c)):
            a = pl.ds(pl.multiple_of(tap * width + start, 128), half)
            b = pl.ds(pl.multiple_of(tap * width + start + half, 128), half)
            for n, src, dst in (
                (0, (slice(0, half), every), (a, at[0])),
                (0, (slice(half, size), every), (b, at[0])),
                (1, (every, every), (a, at[3])),
                (2, (every, every), (b, at[1])),
                (3, (every, left), (a, at[1])),
                (3, (every, right), (a, at[2])),
                (4, (every, left), (b, at[3])),
                (4, (every, right), (b, at[2])),
            ):
                copies.append(
                    pltpu.make_async_copy(sources[5 * k + n].at[src], result.at[dst], sems.at[len(copies)])
                )
        for copy in copies:
            copy.start()
        for copy in copies:
            copy.wait()

    anywhere = pl.BlockSpec(memory_space=pl.ANY)
    operands = list(pieces) + ([] if into is None else [into])
    return call(
        kernel,
        index,
        operands,
        [full(p) for p in pieces] + ([] if into is None else [anywhere]),
        [out(2 * width, cols)],
        [anywhere],
        (1,),
        scratch=[pltpu.SemaphoreType.DMA((16,))],
        aliases={} if into is None else {count + 1: 0},
    )[0]


def body(features, layer_norm_gain, layer_norm_bias, proj_weight, cotangent):
    index = index_vector()
    c = index[0]
    width = layer_norm_gain.shape[1]
    cols = proj_weight.shape[1]
    part = cols // 4

    mine = jnp.concatenate(
        [lax.dynamic_slice(cotangent[0], (0, index[AROUND + j] * part), (256, part)) for j in range(4)], axis=1
    )
    away = swap(mine, SECTION, "section")
    grads = [mine, away, swap(mine, CORE), swap(away, CORE)]

    theirs = swap(lax.dynamic_index_in_dim(features, 1 - c, 0, keepdims=False), CORE)
    gathered = [
        [mine] + [swap(mine, shift(k), "tensor") for k in (-1, 1, 2)]
        for mine in normalize(index, features, theirs, layer_norm_gain, layer_norm_bias)
    ]

    weight_grad = None
    for (r0, size), pieces in zip(ROW_CHUNKS, gathered):
        half = size // 2
        send_a, send_b = weight_grad_blocks(
            index, pieces, grads, (1, 2, 3), ((0, (1, 2), BF16), (1, (2, 3), BF16))
        )
        got_a, got_b = swap(send_a, Y1), swap(send_b, Y3)
        next_a, next_b, keep_a, keep_b = weight_grad_blocks(
            index, pieces, grads, (3, 1, 0), ((0, (3,), F32), (1, (1,), F32), (0, (0,), F32), (1, (0,), F32))
        )
        next_a = (next_a + got_a[:, part:].astype(F32)).astype(BF16)
        next_b = (next_b + got_b[:, :part].astype(F32)).astype(BF16)
        more_a, more_b = swap(next_a, Y3), swap(next_b, Y1)
        keep_a = keep_a + got_a[:, :part].astype(F32) + more_a.astype(F32)
        keep_b = keep_b + got_b[:, part:].astype(F32) + more_b.astype(F32)
        keep = lax.optimization_barrier(jnp.concatenate([keep_a, keep_b], axis=0).astype(BF16))
        done = (keep.astype(F32) + swap(keep, ZLO).astype(F32)).astype(BF16)
        done_a, done_b = done[:half], done[half:]
        second_a, second_b = swap(done_a, Y3), swap(done_b, Y1)
        last_a = swap(jnp.concatenate([done_a, second_a], axis=1), Y1)
        last_b = swap(jnp.concatenate([done_b, second_b], axis=1), Y3)
        ours = [done, second_a, second_b, last_a, last_b]
        weight_grad = place(
            index, ours + [swap(m, CORE) for m in ours], r0, size, width, cols, weight_grad
        )

    parts = row_gradients(index, grads, proj_weight)
    parts = [parts[0]] + [swap(p, shift(k), "tensor") for p, k in zip(parts[1:], (1, -1, 2))]
    hidden = normalize_backward(index, features, theirs, layer_norm_gain, parts)
    ours, back = hidden[0], swap(hidden[1], CORE)
    hidden = jnp.where(c == 0, jnp.stack([ours, back]), jnp.stack([back, ours]))

    own, other = project(index, gathered, proj_weight)
    other = swap(other, CORE)
    back = swap((own[256:].astype(F32) + other[256:].astype(F32)).astype(BF16), SECTION, "section")
    projected = own[:256].astype(F32) + other[:256].astype(F32) + back.astype(F32)
    return (projected.astype(BF16)[None], weight_grad, hidden)


def solution(mesh):
    return jax.shard_map(
        body,
        mesh=mesh,
        in_specs=(
            P("section", ("dp", "tensor"), None),
            P("section", None),
            P("section", None),
            P("section", "tensor"),
            P("dp", "section", "tensor"),
        ),
        out_specs=(
            P("dp", "section", "tensor"),
            P("section", "tensor"),
            P("section", ("dp", "tensor"), None),
        ),
        check_vma=False,
    )
```

time: 436 us -> 231 us (0.53)
  waiting for transfers between devices: 374 us -> 84.2 us
  starting transfers between devices: 0.2 us -> 66.3 us
  Pallas kernels: 0 us -> 54.5 us
  matrix products: 31.3 us -> 0 us
  between operations: 13.8 us -> 1.31 us
  other arithmetic: 4.75 us -> 12.9 us
    psum x1 -> x0, waiting for transfers between devices: 238 us -> none  [body(): summed = lax.psum(partial_value.astype(jnp.bfloat16), 'dp')]
    ppermute x0 -> x44, waiting for transfers between devices: none -> 84.2 us  [swap(): return lax.ppermute(value, axis, pairs)]
    all_gather x2 -> x0, waiting for transfers between devices: 77.2 us -> none  [the longest x1 42.3 us: body(): grads = lax.all_gather(cotangent, 'section', axis=1, tiled=True)[0]]
    ppermute x0 -> x44, starting transfers between devices: none -> 66.3 us  [swap(): return lax.ppermute(value, axis, pairs)]
    reduce_scatter x2 -> x0, waiting for transfers between devices: 58 us -> none  [the longest x1 31.8 us: body(): lax.psum_scatter(jnp.einsum('ro,lco->rlc', rows, weight, preferred_elemen...]
    pallas_call x0 -> x10, Pallas kernels: none -> 54.5 us  [call(): pl.pallas_call(kernel, grid_spec=pltpu.PrefetchScalarGridSpec(num_scalar_...]
    dot_general x3 -> x0, matrix products: 31.3 us -> none  [the longest x1 11.3 us: body(): jnp.einsum('lrc,lco->ro', rows, weight, preferred_element_type=jnp.float32)]
    unnamed x9 -> x56, local copies, waits for them, and re-layouts: 11.3 us -> 6.91 us
  transfers between devices with their start and end apart: 5 -> 44, of which waited for: 5 -> 13; matrix products, arithmetic and copies ran while one was open for 2% -> 7% of each run, Pallas kernels for 0% -> 22%
where the time goes in v1:
time: 231 us; the launch traced here: 230 us
  waiting for transfers between devices  84.2 us (36%)
  starting transfers between devices  66.3 us (29%)
  Pallas kernels  54.5 us (24%)
  other arithmetic  12.9 us (6%)
  local copies, waits for them, and re-layouts  10.9 us (5%)
    ppermute x44, waiting for transfers between devices, swap(): return lax.ppermute(value, axis, pairs)  84.2 us
    ppermute x44, starting transfers between devices, swap(): return lax.ppermute(value, axis, pairs)  66.3 us
    pallas_call x10, Pallas kernels, call(): pl.pallas_call(kernel, grid_spec=pltpu.PrefetchScalarGridSpec(num_scalar_...  54.5 us
    unnamed x56, local copies, waits for them, and re-layouts  6.91 us
  transfers between devices with their start and end apart: 44, of which 13 were waited for; matrix products, arithmetic and copies ran while one was open for 7% of the time, Pallas kernels for 22%

profile of v1, /device:TPU:1, one launch (start us, length us, event | category | flops | bytes accessed | tf_op | source)
XLA Modules:
  0.0 230.1 jit_solution(6157536889790877230)
XLA Ops:
  2.1 4.5 %collective-permute-start.9 = (bf16[256,2048]{1,0:T(8,128)(2,1)S(1)}, bf16[256,2048]{1,0:T(8,128)(2,1)S(1)}, u32[]{:S(2)}, u32[]{:S(2)}) collective-permute-start(bf16[256,2048]{1,0:T(8,128)(2,1)S(1)} %pad_maximum_fusion.refs_4_.refs_0_), channel_id=1, source_target_pairs={{0,64},{64,0},{1,65},{65,1},{2,66},{66,2},{3,67},{67,3},{4,68},{68... | collective-permute-start | bytes 3145736 | tf_op jit(solution)/shard_map/ppermute | solution.py:32
  7.6 21.9 %collective-permute-done.9.refs_5_.refs_1_ = bf16[256,2048]{1,0:T(8,128)(2,1)S(1)} collective-permute-done((bf16[256,2048]{1,0:T(8,128)(2,1)S(1)}, bf16[256,2048]{1,0:T(8,128)(2,1)S(1)}, u32[]{:S(2)}, u32[]{:S(2)}) %collective-permute-start.9) | collective-permute-done | bytes 1048608 | tf_op jit(solution)/shard_map/ppermute | solution.py:32
  41.9 3.8 %collective-permute-done.3.refs_3_ = bf16[2,128,512]{2,1,0:T(8,128)(2,1)S(1)} collective-permute-done((bf16[2,128,512]{2,1,0:T(8,128)(2,1)S(1)}, bf16[2,128,512]{2,1,0:T(8,128)(2,1)S(1)}, u32[]{:S(2)}, u32[]{:S(2)}) %collective-permute-start.3) | collective-permute-done | bytes 262176 | tf_op jit(solution)/shard_map/ppermute | solution.py:32
  48.5 3.9 %collective-permute-done.2.refs_2_ = bf16[2,128,512]{2,1,0:T(8,128)(2,1)S(1)} collective-permute-done((bf16[2,128,512]{2,1,0:T(8,128)(2,1)S(1)}, bf16[2,128,512]{2,1,0:T(8,128)(2,1)S(1)}, u32[]{:S(2)}, u32[]{:S(2)}) %collective-permute-start.2) | collective-permute-done | bytes 262176 | tf_op jit(solution)/shard_map/ppermute | solution.py:32
  55.0 3.9 %shard_map.81 = (bf16[256,1024]{1,0:T(8,128)(2,1)S(1)}, bf16[256,1024]{1,0:T(8,128)(2,1)S(1)}) custom-call(s32[9]{0:T(128)S(1)} %stack.49.index_ref, bf16[2,128,512]{2,1,0:T(8,128)(2,1)S(1)} %get-tuple-element.23.refs_0_, bf16[2,128,512]{2,1,0:T(8,128)(2,1)S(1)} %collective-permute-done.1.refs_1_, bf16[2,128,512]{2,1,0:T(8,128)(2,1)S(1)} %collective-permute-done.2.refs_2_, ...), custom_call_target="tpu_custom_call" | custom-call | flops 1073741824 | bytes 6291456 | tf_op jit(solution)/shard_map/pallas_call | solution.py:45
  62.3 6.5 %collective-permute-done.5.refs_6_.refs_2_ = bf16[2,128,768]{2,1,0:T(8,128)(2,1)S(1)} collective-permute-done((bf16[2,128,768]{2,1,0:T(8,128)(2,1)S(1)}, bf16[2,128,768]{2,1,0:T(8,128)(2,1)S(1)}, u32[]{:S(2)}, u32[]{:S(2)}) %collective-permute-start.5) | collective-permute-done | bytes 393248 | tf_op jit(solution)/shard_map/ppermute | solution.py:32
  68.8 5.3 %shard_map.79 = (bf16[384,1024]{1,0:T(8,128)(2,1)S(1)}, bf16[384,1024]{1,0:T(8,128)(2,1)}) custom-call(s32[9]{0:T(128)S(1)} %stack.49.index_ref, bf16[2,128,768]{2,1,0:T(8,128)(2,1)S(1)} %get-tuple-element.24.refs_4_.refs_0_, bf16[2,128,768]{2,1,0:T(8,128)(2,1)S(1)} %collective-permute-done.4.refs_5_.refs_1_, ...), custom_call_target="tpu_custom_call" | custom-call | flops 1610612736 | bytes 7340032 | tf_op jit(solution)/shard_map/pallas_call | solution.py:45
  76.8 15.2 %shard_map.84 = (bf16[2,128,1280]{2,1,0:T(8,128)(2,1)S(1)}, bf16[2,128,1280]{2,1,0:T(8,128)(2,1)}, bf16[2,128,1280]{2,1,0:T(8,128)(2,1)}, bf16[2,128,1280]{2,1,0:T(8,128)(2,1)}) custom-call(s32[9]{0:T(128)S(1)} %stack.49.index_ref, bf16[256,2048]{1,0:T(8,128)(2,1)S(1)} %pad_maximum_fusion.refs_4_.refs_0_, ...), custom_call_target="tpu_custom_call" | custom-call | flops 5368709120 | bytes 17301504 | tf_op jit(solution)/shard_map/pallas_call | solution.py:45
  93.2 9.1 %shard_map.77 = (bf16[512,2048]{1,0:T(8,128)(2,1)S(1)}, bf16[512,2048]{1,0:T(8,128)(2,1)}) custom-call(s32[9]{0:T(128)S(1)} %stack.49.index_ref, bf16[2,128,512]{2,1,0:T(8,128)(2,1)S(1)} %get-tuple-element.23.refs_0_, bf16[2,128,512]{2,1,0:T(8,128)(2,1)S(1)} %collective-permute-done.1.refs_1_, bf16[2,128,512]{2,1,0:T(8,128)(2,1)S(1)} %collective-permute-done.2.refs_2_, ...), custom_call_target="tpu_custom_call" | custom-call | flops 5368709120 | bytes 17301504 | tf_op jit(solution)/shard_map/pallas_call | solution.py:45
  109.3 4.9 %shard_map.78 = (f32[384,512]{1,0:T(8,128)S(1)}, f32[384,512]{1,0:T(8,128)S(1)}, f32[384,512]{1,0:T(8,128)S(1)}, f32[384,512]{1,0:T(8,128)S(1)}) custom-call(s32[9]{0:T(128)S(1)} %stack.49.index_ref, bf16[2,128,768]{2,1,0:T(8,128)(2,1)S(1)} %copy-done.12, bf16[2,128,768]{2,1,0:T(8,128)(2,1)S(1)} %copy-done.18, bf16[2,128,768]{2,1,0:T(8,128)(2,1)S(1)} %copy-done.16, ...), custom_call_target="tpu_custom_call" | custom-call | flops 1610612736 | bytes 8912896 | tf_op jit(solution)/shard_map/pallas_call | solution.py:45
  115.1 4.2 %shard_map.80 = (f32[256,512]{1,0:T(8,128)S(1)}, f32[256,512]{1,0:T(8,128)S(1)}, f32[256,512]{1,0:T(8,128)S(1)}, f32[256,512]{1,0:T(8,128)S(1)}) custom-call(s32[9]{0:T(128)S(1)} %stack.49.index_ref, bf16[2,128,512]{2,1,0:T(8,128)(2,1)S(1)} %get-tuple-element.23.refs_0_, bf16[2,128,512]{2,1,0:T(8,128)(2,1)S(1)} %collective-permute-done.1.refs_1_, ...), custom_call_target="tpu_custom_call" | custom-call | flops 1073741824 | bytes 7340032 | tf_op jit(solution)/shard_map/pallas_call | solution.py:45
  127.0 5.5 %collective-permute-done.12 = bf16[384,1024]{1,0:T(8,128)(2,1)S(1)} collective-permute-done((bf16[384,1024]{1,0:T(8,128)(2,1)S(1)}, bf16[384,1024]{1,0:T(8,128)(2,1)S(1)}, u32[]{:S(2)}, u32[]{:S(2)}) %collective-permute-start.12) | collective-permute-done | bytes 786464 | tf_op jit(solution)/shard_map/ppermute | solution.py:32
  132.8 5.3 %collective-permute-done.29 = bf16[256,512]{1,0:T(8,128)(2,1)S(1)} collective-permute-done((bf16[256,512]{1,0:T(8,128)(2,1)S(1)}, bf16[256,512]{1,0:T(8,128)(2,1)S(1)}, u32[]{:S(2)}, u32[]{:S(2)}) %collective-permute-start.29) | collective-permute-done | bytes 262176 | tf_op jit(solution)/shard_map/ppermute | solution.py:32
  139.5 7.0 %collective-permute-done.15 = bf16[384,512]{1,0:T(8,128)(2,1)S(1)} collective-permute-done((bf16[384,512]{1,0:T(8,128)(2,1)S(1)}, bf16[384,512]{1,0:T(8,128)(2,1)S(1)}, u32[]{:S(2)}, u32[]{:S(2)}) %collective-permute-start.15) | collective-permute-done | bytes 393248 | tf_op jit(solution)/shard_map/ppermute | solution.py:32
  149.7 3.4 %collective-permute-start.8 = (bf16[256,2048]{1,0:T(8,128)(2,1)S(1)}, bf16[256,2048]{1,0:T(8,128)(2,1)S(1)}, u32[]{:S(2)}, u32[]{:S(2)}) collective-permute-start(bf16[256,2048]{1,0:T(8,128)(2,1)S(1)} %add_convert_fusion.1), channel_id=1, source_target_pairs={{0,64},{64,0},{1,65},{65,1},{2,66},{66,2},{3,67},{67,3},{4,68},{68... | collective-permute-start | bytes 3145736 | tf_op jit(solution)/shard_map/ppermute | solution.py:32
  154.0 12.7 %collective-permute-done.16 = bf16[768,512]{1,0:T(8,128)(2,1)S(1)} collective-permute-done((bf16[768,512]{1,0:T(8,128)(2,1)S(1)}, bf16[768,512]{1,0:T(8,128)(2,1)S(1)}, u32[]{:S(2)}, u32[]{:S(2)}) %collective-permute-start.16) | collective-permute-done | bytes 786464 | tf_op jit(solution)/shard_map/ppermute | solution.py:32
  168.5 6.7 %collective-permute-start.43 = (bf16[128,1280]{1,0:T(8,128)(2,1)S(1)}, bf16[128,1280]{1,0:T(8,128)(2,1)S(1)}, u32[]{:S(2)}, u32[]{:S(2)}) collective-permute-start(bf16[128,1280]{1,0:T(8,128)(2,1)S(1)} %get-tuple-element.50), channel_id=1, source_target_pairs={{0,4},{4,0},{8,12},{12,8},{16,20},{20,16},{24,28},{28,24},{32,36},... | collective-permute-start | bytes 983048 | tf_op jit(solution)/shard_map/ppermute | solution.py:32
  180.6 11.4 %collective-permute-done.8 = bf16[256,2048]{1,0:T(8,128)(2,1)S(1)} collective-permute-done((bf16[256,2048]{1,0:T(8,128)(2,1)S(1)}, bf16[256,2048]{1,0:T(8,128)(2,1)S(1)}, u32[]{:S(2)}, u32[]{:S(2)}) %collective-permute-start.8) | collective-permute-done | bytes 1048608 | tf_op jit(solution)/shard_map/ppermute | solution.py:32
  192.1 4.0 %collective-permute-start.37 = (bf16[256,512]{1,0:T(8,128)(2,1)S(1)}, bf16[256,512]{1,0:T(8,128)(2,1)S(1)}, u32[]{:S(2)}, u32[]{:S(2)}) collective-permute-start(bf16[256,512]{1,0:T(8,128)(2,1)S(1)} %collective-permute-done.32.refs_2_), channel_id=1, source_target_pairs={{0,4},{4,0},{8,12},{12,8},{16,20},{20,16},{24,28},{28,24},{32,36},... | collective-permute-start | bytes 786440 | tf_op jit(solution)/shard_map/ppermute | solution.py:32
  203.1 6.0 %collective-permute-start.24 = (bf16[384,1024]{1,0:T(8,128)(2,1)}, bf16[384,1024]{1,0:T(8,128)(2,1)S(1)}, u32[]{:S(2)}, u32[]{:S(2)}) collective-permute-start(bf16[384,1024]{1,0:T(8,128)(2,1)} %collective-permute-done.19.refs_3_), channel_id=1, source_target_pairs={{0,4},{4,0},{8,12},{12,8},{16,20},{20,16},{24,28},{28,24},{32,36},... | collective-permute-start | bytes 2359304 | tf_op jit(solution)/shard_map/ppermute | solution.py:32
  209.3 4.2 %collective-permute-start.25 = (bf16[384,1024]{1,0:T(8,128)(2,1)}, bf16[384,1024]{1,0:T(8,128)(2,1)S(1)}, u32[]{:S(2)}, u32[]{:S(2)}) collective-permute-start(bf16[384,1024]{1,0:T(8,128)(2,1)} %collective-permute-done.20.refs_4_), channel_id=1, source_target_pairs={{0,4},{4,0},{8,12},{12,8},{16,20},{20,16},{24,28},{28,24},{32,36},... | collective-permute-start | bytes 2359304 | tf_op jit(solution)/shard_map/ppermute | solution.py:32
  216.3 3.4 %fusion = bf16[1,256,2048]{2,1,0:T(8,128)(2,1)} fusion(bf16[256,2048]{1,0:T(8,128)(2,1)} %copy-done.19, bf16[512,2048]{1,0:T(8,128)(2,1)} %collective-permute-done.7, bf16[512,2048]{1,0:T(8,128)(2,1)} %copy-done.6), kind=kLoop, calls=%fused_computation.3 | loop fusion | flops 3145728 | bytes 4194304 | tf_op jit(solution)/shard_map/broadcast_in_dim | solution.py:377
  219.7 4.3 %shard_map.82.refs_10_ = bf16[2560,2048]{1,0:T(8,128)(2,1)} custom-call(s32[9]{0:T(128)S(1)} %stack.49.index_ref, bf16[512,512]{1,0:T(8,128)(2,1)S(1)} %add_convert_fusion.3.refs_0_, bf16[256,512]{1,0:T(8,128)(2,1)S(1)} %collective-permute-done.31.refs_1_, bf16[256,512]{1,0:T(8,128)(2,1)S(1)} %collective-permute-done.32.refs_2_, ...), custom_call_target="tpu_custom_call" | custom-call | bytes 14680064 | tf_op jit(solution)/shard_map/pallas_call | solution.py:45
  225.0 4.9 %shard_map.83 = bf16[2560,2048]{1,0:T(8,128)(2,1)} custom-call(s32[9]{0:T(128)S(1)} %stack.49.index_ref, bf16[768,512]{1,0:T(8,128)(2,1)S(1)} %add_convert_fusion.2.refs_0_, bf16[384,512]{1,0:T(8,128)(2,1)S(1)} %collective-permute-done.17.refs_1_, bf16[384,512]{1,0:T(8,128)(2,1)S(1)} %collective-permute-done.18.refs_2_, ...), custom_call_target="tpu_custom_call", output_to_operand_aliasing={{}: (11, {})} | custom-call | bytes 27262976 | tf_op jit(solution)/shard_map/pallas_call | solution.py:45
  (156 shorter events, 66.6 us)
Async XLA Ops:
  2.1 27.4 %collective-permute-start.9 = (bf16[256,2048]{1,0:T(8,128)(2,1)S(1)}, bf16[256,2048]{1,0:T(8,128)(2,1)S(1)}, u32[]{:S(2)}, u32[]{:S(2)}) collective-permute-start(bf16[256,2048]{1,0:T(8,128)(2,1)S(1)} %pad_maximum_fusion.refs_4_.refs_0_), channel_id=1, source_target_pairs={{0,64},{64,0},{1,65},{65,1},{2,66},{66,2},{3,67},{67,3},{4,68},{68... | collective-permute-start | bytes 3145736 | tf_op jit(solution)/shard_map/ppermute | solution.py:32
  6.6 48.4 %collective-permute-start.10 = (bf16[256,2048]{1,0:T(8,128)(2,1)S(1)}, bf16[256,2048]{1,0:T(8,128)(2,1)S(1)}, u32[]{:S(2)}, u32[]{:S(2)}) collective-permute-start(bf16[256,2048]{1,0:T(8,128)(2,1)S(1)} %pad_maximum_fusion.refs_4_.refs_0_), channel_id=1, source_target_pairs={{0,4},{4,0},{8,12},{12,8},{16,20},{20,16},{24,28},{28,24},{32,36},... | collective-permute-start | bytes 3145736 | tf_op jit(solution)/shard_map/ppermute | solution.py:32
  29.5 25.5 %collective-permute-start.11 = (bf16[256,2048]{1,0:T(8,128)(2,1)S(1)}, bf16[256,2048]{1,0:T(8,128)(2,1)}, u32[]{:S(2)}, u32[]{:S(2)}) collective-permute-start(bf16[256,2048]{1,0:T(8,128)(2,1)S(1)} %collective-permute-done.9.refs_5_.refs_1_), channel_id=1, source_target_pairs={{0,4},{4,0},{8,12},{12,8},{16,20},{20,16},{24,28},{28,24},{32,36},... | collective-permute-start | bytes 3145736 | tf_op jit(solution)/shard_map/ppermute | solution.py:32
  59.0 44.7 %collective-permute-start.26 = (bf16[256,1024]{1,0:T(8,128)(2,1)S(1)}, bf16[256,1024]{1,0:T(8,128)(2,1)S(1)}, u32[]{:S(2)}, u32[]{:S(2)}) collective-permute-start(bf16[256,1024]{1,0:T(8,128)(2,1)S(1)} %get-tuple-element.34), channel_id=1, source_target_pairs={{0,16},{4,20},{8,24},{12,28},{16,0},{20,4},{24,8},{28,12},{32,48},... | collective-permute-start | bytes 1572872 | tf_op jit(solution)/shard_map/ppermute | solution.py:32
  60.4 53.8 %collective-permute-start.28 = (bf16[256,1024]{1,0:T(8,128)(2,1)S(1)}, bf16[256,1024]{1,0:T(8,128)(2,1)S(1)}, u32[]{:S(2)}, u32[]{:S(2)}) collective-permute-start(bf16[256,1024]{1,0:T(8,128)(2,1)S(1)} %get-tuple-element.37), channel_id=1, source_target_pairs={{0,48},{4,52},{8,56},{12,60},{16,32},{20,36},{24,40},{28,44},{32,1... | collective-permute-start | bytes 1572872 | tf_op jit(solution)/shard_map/ppermute | solution.py:32
  74.0 52.6 %collective-permute-start.14 = (bf16[384,1024]{1,0:T(8,128)(2,1)}, bf16[384,1024]{1,0:T(8,128)(2,1)S(1)}, u32[]{:S(2)}, u32[]{:S(2)}) collective-permute-start(bf16[384,1024]{1,0:T(8,128)(2,1)} %get-tuple-element.31), channel_id=1, source_target_pairs={{0,48},{4,52},{8,56},{12,60},{16,32},{20,36},{24,40},{28,44},{32,1... | collective-permute-start | bytes 2359304 | tf_op jit(solution)/shard_map/ppermute | solution.py:32
  91.9 28.5 %collective-permute-start.40 = (bf16[2,128,1280]{2,1,0:T(8,128)(2,1)}, bf16[2,128,1280]{2,1,0:T(8,128)(2,1)S(1)}, u32[]{:S(2)}, u32[]{:S(2)}) collective-permute-start(bf16[2,128,1280]{2,1,0:T(8,128)(2,1)} %get-tuple-element.40), channel_id=1, source_target_pairs={{0,1},{1,2},{2,3},{3,0},{4,5},{5,6},{6,7},{7,4},{8,9},{9,10},{10,1... | collective-permute-start | bytes 1966088 | tf_op jit(solution)/shard_map/ppermute | solution.py:32
  102.3 21.0 %collective-permute-start.41 = (bf16[2,128,1280]{2,1,0:T(8,128)(2,1)}, bf16[2,128,1280]{2,1,0:T(8,128)(2,1)S(1)}, u32[]{:S(2)}, u32[]{:S(2)}) collective-permute-start(bf16[2,128,1280]{2,1,0:T(8,128)(2,1)} %get-tuple-element.41), channel_id=1, source_target_pairs={{0,3},{1,0},{2,1},{3,2},{4,7},{5,4},{6,5},{7,6},{8,11},{9,8},{10,9... | collective-permute-start | bytes 1966088 | tf_op jit(solution)/shard_map/ppermute | solution.py:32
  103.8 21.2 %collective-permute-start.42 = (bf16[2,128,1280]{2,1,0:T(8,128)(2,1)}, bf16[2,128,1280]{2,1,0:T(8,128)(2,1)S(1)}, u32[]{:S(2)}, u32[]{:S(2)}) collective-permute-start(bf16[2,128,1280]{2,1,0:T(8,128)(2,1)} %get-tuple-element.42), channel_id=1, source_target_pairs={{0,2},{1,3},{2,0},{3,1},{4,6},{5,7},{6,4},{7,5},{8,10},{9,11},{10,... | collective-permute-start | bytes 1966088 | tf_op jit(solution)/shard_map/ppermute | solution.py:32
  115.1 17.4 %collective-permute-start.12 = (bf16[384,1024]{1,0:T(8,128)(2,1)S(1)}, bf16[384,1024]{1,0:T(8,128)(2,1)S(1)}, u32[]{:S(2)}, u32[]{:S(2)}) collective-permute-start(bf16[384,1024]{1,0:T(8,128)(2,1)S(1)} %get-tuple-element.28), channel_id=1, source_target_pairs={{0,16},{4,20},{8,24},{12,28},{16,0},{20,4},{24,8},{28,12},{32,48},... | collective-permute-start | bytes 2359304 | tf_op jit(solution)/shard_map/ppermute | solution.py:32
  120.4 27.6 %collective-permute-start.7 = (bf16[512,2048]{1,0:T(8,128)(2,1)}, bf16[512,2048]{1,0:T(8,128)(2,1)}, u32[]{:S(2)}, u32[]{:S(2)}) collective-permute-start(bf16[512,2048]{1,0:T(8,128)(2,1)} %get-tuple-element.26), channel_id=1, source_target_pairs={{0,4},{4,0},{8,12},{12,8},{16,20},{20,16},{24,28},{28,24},{32,36},... | collective-permute-start | bytes 6291464 | tf_op jit(solution)/shard_map/ppermute | solution.py:32
  126.8 19.7 %collective-permute-start.15 = (bf16[384,512]{1,0:T(8,128)(2,1)S(1)}, bf16[384,512]{1,0:T(8,128)(2,1)S(1)}, u32[]{:S(2)}, u32[]{:S(2)}) collective-permute-start(bf16[384,512]{1,0:T(8,128)(2,1)S(1)} %add_convert_fusion.5), channel_id=1, source_target_pairs={{0,16},{4,20},{8,24},{12,28},{16,0},{20,4},{24,8},{28,12},{32,48},... | collective-permute-start | bytes 1179656 | tf_op jit(solution)/shard_map/ppermute | solution.py:32
  147.0 19.7 %collective-permute-start.16 = (bf16[768,512]{1,0:T(8,128)(2,1)S(1)}, bf16[768,512]{1,0:T(8,128)(2,1)S(1)}, u32[]{:S(2)}, u32[]{:S(2)}) collective-permute-start(bf16[768,512]{1,0:T(8,128)(2,1)S(1)} %pad_maximum_fusion.1), channel_id=1, source_target_pairs={{0,8},{4,12},{8,0},{12,4},{16,24},{20,28},{24,16},{28,20},{32,40},... | collective-permute-start | bytes 2359304 | tf_op jit(solution)/shard_map/ppermute | solution.py:32
  149.7 42.3 %collective-permute-start.8 = (bf16[256,2048]{1,0:T(8,128)(2,1)S(1)}, bf16[256,2048]{1,0:T(8,128)(2,1)S(1)}, u32[]{:S(2)}, u32[]{:S(2)}) collective-permute-start(bf16[256,2048]{1,0:T(8,128)(2,1)S(1)} %add_convert_fusion.1), channel_id=1, source_target_pairs={{0,64},{64,0},{1,65},{65,1},{2,66},{66,2},{3,67},{67,3},{4,68},{68... | collective-permute-start | bytes 3145736 | tf_op jit(solution)/shard_map/ppermute | solution.py:32
  153.5 21.8 %collective-permute-start.31 = (bf16[256,512]{1,0:T(8,128)(2,1)S(1)}, bf16[256,512]{1,0:T(8,128)(2,1)S(1)}, u32[]{:S(2)}, u32[]{:S(2)}) collective-permute-start(bf16[256,512]{1,0:T(8,128)(2,1)S(1)} %get-tuple-element.52), channel_id=1, source_target_pairs={{0,48},{4,52},{8,56},{12,60},{16,32},{20,36},{24,40},{28,44},{32,1... | collective-permute-start | bytes 786440 | tf_op jit(solution)/shard_map/ppermute | solution.py:32
  175.3 16.8 %collective-permute-start.35 = (bf16[512,512]{1,0:T(8,128)(2,1)S(1)}, bf16[512,512]{1,0:T(8,128)(2,1)S(1)}, u32[]{:S(2)}, u32[]{:S(2)}) collective-permute-start(bf16[512,512]{1,0:T(8,128)(2,1)S(1)} %add_convert_fusion.3.refs_0_), channel_id=1, source_target_pairs={{0,4},{4,0},{8,12},{12,8},{16,20},{20,16},{24,28},{28,24},{32,36},... | collective-permute-start | bytes 1572872 | tf_op jit(solution)/shard_map/ppermute | solution.py:32
  175.5 20.6 %collective-permute-start.33 = (bf16[256,1024]{1,0:T(8,128)(2,1)S(1)}, bf16[256,1024]{1,0:T(8,128)(2,1)}, u32[]{:S(2)}, u32[]{:S(2)}) collective-permute-start(bf16[256,1024]{1,0:T(8,128)(2,1)S(1)} %pad_maximum_fusion.5), channel_id=1, source_target_pairs={{0,16},{4,20},{8,24},{12,28},{16,0},{20,4},{24,8},{28,12},{32,48},... | collective-permute-start | bytes 1572872 | tf_op jit(solution)/shard_map/ppermute | solution.py:32
  177.8 20.1 %collective-permute-start.34 = (bf16[256,1024]{1,0:T(8,128)(2,1)S(1)}, bf16[256,1024]{1,0:T(8,128)(2,1)}, u32[]{:S(2)}, u32[]{:S(2)}) collective-permute-start(bf16[256,1024]{1,0:T(8,128)(2,1)S(1)} %pad_maximum_fusion.6), channel_id=1, source_target_pairs={{0,48},{4,52},{8,56},{12,60},{16,32},{20,36},{24,40},{28,44},{32,1... | collective-permute-start | bytes 1572872 | tf_op jit(solution)/shard_map/ppermute | solution.py:32
  180.6 22.5 %collective-permute-start.19 = (bf16[384,1024]{1,0:T(8,128)(2,1)}, bf16[384,1024]{1,0:T(8,128)(2,1)}, u32[]{:S(2)}, u32[]{:S(2)}) collective-permute-start(bf16[384,1024]{1,0:T(8,128)(2,1)} %pad_maximum_fusion.2), channel_id=1, source_target_pairs={{0,16},{4,20},{8,24},{12,28},{16,0},{20,4},{24,8},{28,12},{32,48},... | collective-permute-start | bytes 2359304 | tf_op jit(solution)/shard_map/ppermute | solution.py:32
  192.0 17.3 %collective-permute-start.20 = (bf16[384,1024]{1,0:T(8,128)(2,1)}, bf16[384,1024]{1,0:T(8,128)(2,1)}, u32[]{:S(2)}, u32[]{:S(2)}) collective-permute-start(bf16[384,1024]{1,0:T(8,128)(2,1)} %pad_maximum_fusion.3), channel_id=1, source_target_pairs={{0,48},{4,52},{8,56},{12,60},{16,32},{20,36},{24,40},{28,44},{32,1... | collective-permute-start | bytes 2359304 | tf_op jit(solution)/shard_map/ppermute | solution.py:32
  196.1 19.6 %collective-permute-start.38 = (bf16[256,1024]{1,0:T(8,128)(2,1)}, bf16[256,1024]{1,0:T(8,128)(2,1)}, u32[]{:S(2)}, u32[]{:S(2)}) collective-permute-start(bf16[256,1024]{1,0:T(8,128)(2,1)} %collective-permute-done.33.refs_3_), channel_id=1, source_target_pairs={{0,4},{4,0},{8,12},{12,8},{16,20},{20,16},{24,28},{28,24},{32,36},... | collective-permute-start | bytes 1572872 | tf_op jit(solution)/shard_map/ppermute | solution.py:32
  197.9 17.8 %collective-permute-start.39 = (bf16[256,1024]{1,0:T(8,128)(2,1)}, bf16[256,1024]{1,0:T(8,128)(2,1)}, u32[]{:S(2)}, u32[]{:S(2)}) collective-permute-start(bf16[256,1024]{1,0:T(8,128)(2,1)} %collective-permute-done.34.refs_4_), channel_id=1, source_target_pairs={{0,4},{4,0},{8,12},{12,8},{16,20},{20,16},{24,28},{28,24},{32,36},... | collective-permute-start | bytes 1572872 | tf_op jit(solution)/shard_map/ppermute | solution.py:32
  200.3 23.7 %collective-permute-start.21 = (bf16[768,512]{1,0:T(8,128)(2,1)S(1)}, bf16[768,512]{1,0:T(8,128)(2,1)S(1)}, u32[]{:S(2)}, u32[]{:S(2)}) collective-permute-start(bf16[768,512]{1,0:T(8,128)(2,1)S(1)} %add_convert_fusion.2.refs_0_), channel_id=1, source_target_pairs={{0,4},{4,0},{8,12},{12,8},{16,20},{20,16},{24,28},{28,24},{32,36},... | collective-permute-start | bytes 2359304 | tf_op jit(solution)/shard_map/ppermute | solution.py:32
  203.1 20.9 %collective-permute-start.24 = (bf16[384,1024]{1,0:T(8,128)(2,1)}, bf16[384,1024]{1,0:T(8,128)(2,1)S(1)}, u32[]{:S(2)}, u32[]{:S(2)}) collective-permute-start(bf16[384,1024]{1,0:T(8,128)(2,1)} %collective-permute-done.19.refs_3_), channel_id=1, source_target_pairs={{0,4},{4,0},{8,12},{12,8},{16,20},{20,16},{24,28},{28,24},{32,36},... | collective-permute-start | bytes 2359304 | tf_op jit(solution)/shard_map/ppermute | solution.py:32
  (48 other events, 662.5 us)

commit v2 on v0

v2 whole, which is shorter than its diff:
```python
import jax
import jax.numpy as jnp
from jax import lax
from jax.experimental import pallas as pl
from jax.experimental.pallas import tpu as pltpu
from jax.sharding import PartitionSpec as P

F32 = jnp.float32
BF16 = jnp.bfloat16
VMEM_LIMIT = 20 * 1024 * 1024

ROW_CHUNKS = ((0, 640), (640, 640))


def dp_pairs(fy=lambda y: y, fz=lambda z: z, fc=lambda c: c):
    return [(i, fy(i // 4) * 4 + fz(i // 2 % 2) * 2 + fc(i % 2)) for i in range(16)]


Y1 = dp_pairs(fy=lambda y: y ^ 1)
Y3 = dp_pairs(fy=lambda y: y ^ 3)
ZLO = dp_pairs(fz=lambda z: z ^ 1)
CORE = dp_pairs(fc=lambda c: c ^ 1)
SECTION = [(0, 1), (1, 0)]
AROUND, SLOT_OF, SLOTS = 1, 5, 9


def shift(step):
    return [(i, (i + step) % 4) for i in range(4)]


def swap(value, pairs, axis="dp"):
    return lax.ppermute(value, axis, pairs)


ANY = pl.BlockSpec(memory_space=pl.ANY)
HBM = pl.BlockSpec(memory_space=pltpu.HBM)


class Copies:
    def __init__(self, sems):
        self.sems, self.all = sems, []

    def start(self, *pairs):
        copies = []
        for source, target in pairs:
            copies.append(pltpu.make_async_copy(source, target, self.sems.at[len(self.all)]))
            copies[-1].start()
            self.all.append(copies[-1])
        return copies


def wait(*groups):
    for group in groups:
        for copy in group:
            copy.wait()


def prepare(features, cotangent):
    _, rows, width = features.shape
    _, tokens, cols = cotangent.shape
    part = cols // 4

    def kernel(features_hbm, cotangent_hbm, theirs_out, mine_out, index_out, theirs, mine, sems):
        s, d = lax.axis_index("section"), lax.axis_index("dp")
        y, c = d // 4, d % 2
        around = (y, y + 1 - 2 * (y % 2), (y + 2) % 4, 3 - y)
        copies = Copies(sems)
        first = copies.start((features_hbm.at[1 - c], theirs))
        blocks = []
        for n, j in enumerate(around):
            at = pl.ds(pl.multiple_of(j * part, part), part)
            blocks.append(copies.start((cotangent_hbm.at[0, :, at], mine.at[:, n * part : (n + 1) * part])))
        index_out[0] = c
        for n, j in enumerate(around):
            index_out[AROUND + n] = j
        for t in range(4):
            index_out[SLOT_OF + t] = (s if t < 2 else 1 - s) * 2 + t % 2
        x = lax.axis_index("tensor")
        for n, t in enumerate((x, (x + 1) % 4, (x + 3) % 4, (x + 2) % 4)):
            index_out[SLOTS + n] = ((t // 2 + s) % 2) * 2 + t % 2
        wait(first)
        second = copies.start((theirs, theirs_out))
        for n, block in enumerate(blocks):
            wait(block)
            here = (slice(None), slice(n * part, (n + 1) * part))
            second += copies.start((mine.at[here], mine_out.at[here]))
        wait(second)

    return pl.pallas_call(
        kernel,
        in_specs=[HBM, HBM],
        out_specs=[ANY, ANY, pl.BlockSpec(memory_space=pltpu.SMEM)],
        out_shape=[out(rows, width), out(tokens, cols), out(13, dtype=jnp.int32)],
        scratch_shapes=[
            pltpu.VMEM((rows, width), BF16),
            pltpu.VMEM((tokens, cols), BF16),
            pltpu.SemaphoreType.DMA((10,)),
        ],
        compiler_params=pltpu.CompilerParams(vmem_limit_bytes=VMEM_LIMIT),
        cost_estimate=pl.CostEstimate(flops=1, bytes_accessed=1, transcendentals=0),
    )(features, cotangent)


def sums(*wanted, stack=False):
    flat = [(a, at) for terms in wanted for a, at in terms]
    shapes = [out(*jax.eval_shape(lambda a, at=terms[0][1]: a[at], terms[0][0]).shape) for terms in wanted]
    count = len(flat)
    made = [out(len(shapes) * shapes[0].shape[0], *shapes[0].shape[1:])] if stack else shapes

    def kernel(*refs):
        ins, outs = refs[:count], refs[count : count + len(made)]
        held, results, sems = refs[count + len(made) : -1 - len(wanted)], refs[-1 - len(wanted) : -1], refs[-1]
        if stack:
            rows = shapes[0].shape[0]
            outs = [outs[0].at[n * rows : (n + 1) * rows] for n in range(len(shapes))]
        copies = Copies(sems)
        arrived = [copies.start((ref.at[at], to)) for ref, (_, at), to in zip(ins, flat, held)]
        done, n = [], 0
        for terms, result, out_ref in zip(wanted, results, outs):
            total = None
            for _ in terms:
                wait(arrived[n])
                value = held[n][...].astype(F32)
                total = value if total is None else total + value
                n += 1
            result[...] = total.astype(BF16)
            done += copies.start((result, out_ref))
        wait(done)

    held_shapes = [s for terms, s in zip(wanted, shapes) for _ in terms]
    return pl.pallas_call(
        kernel,
        in_specs=[ANY] * count,
        out_specs=[ANY] * len(made),
        out_shape=made,
        scratch_shapes=[
            *(pltpu.VMEM(s.shape, BF16) for s in held_shapes),
            *(pltpu.VMEM(s.shape, BF16) for s in shapes),
            pltpu.SemaphoreType.DMA((count + len(shapes),)),
        ],
        compiler_params=pltpu.CompilerParams(vmem_limit_bytes=VMEM_LIMIT),
        cost_estimate=pl.CostEstimate(flops=1, bytes_accessed=1, transcendentals=0),
    )(*(a for a, _ in flat))


def call(kernel, index, operands, in_specs, out_shapes, out_specs, grid, scratch=(), aliases=None):
    return pl.pallas_call(
        kernel,
        grid_spec=pltpu.PrefetchScalarGridSpec(
            num_scalar_prefetch=1,
            grid=grid,
            in_specs=in_specs,
            out_specs=out_specs,
            scratch_shapes=scratch,
        ),
        out_shape=out_shapes,
        input_output_aliases=aliases or {},
        compiler_params=pltpu.CompilerParams(vmem_limit_bytes=VMEM_LIMIT),
        cost_estimate=pl.CostEstimate(flops=1, bytes_accessed=1, transcendentals=0),
    )(index, *operands)


def full(array):
    return pl.BlockSpec(array.shape, lambda *_: (0,) * len(array.shape))


def out(*shape, dtype=BF16):
    return jax.ShapeDtypeStruct(shape, dtype)


def dot(a, b, contract=(1, 0)):
    return lax.dot_general(a, b, (((contract[0],), (contract[1],)), ((), ())), preferred_element_type=F32)


def moments(value):
    mean = jnp.mean(value, axis=-1, keepdims=True)
    centered = value - mean
    inverse = 1.0 / jnp.sqrt(jnp.mean(centered * centered, axis=-1, keepdims=True) + 1e-05)
    return centered * inverse, inverse


def normalize(index, features, theirs, gain, bias):
    _, rows, width = features.shape

    def kernel(index_ref, own_hbm, theirs_any, gain_hbm, bias_hbm, *refs):
        outs, (held, scale, normed, sems) = refs[:-4], refs[-4:]
        c = index_ref[0]
        copies = Copies(sems)
        first = copies.start((gain_hbm, scale.at[0]), (bias_hbm, scale.at[1]))
        arrived = [copies.start((own_hbm.at[c], held.at[0])), copies.start((theirs_any, held.at[1]))]
        wait(first)
        gain, bias = scale[0, pl.ds(c, 1)], scale[1, pl.ds(c, 1)]
        done = []
        for k in range(2):
            wait(arrived[k])
            standard, _ = moments(held[k].astype(F32))
            normed[k] = (standard * gain + bias).astype(BF16)
            for (start, size), out_ref in zip(ROW_CHUNKS, outs):
                done += copies.start((normed.at[k, :, start : start + size], out_ref.at[k]))
        wait(done)

    shapes = [out(2, rows, size) for _, size in ROW_CHUNKS]
    return call(
        kernel,
        index,
        [features, theirs, gain, bias],
        [HBM, ANY, HBM, HBM],
        shapes,
        [ANY] * len(shapes),
        (1,),
        scratch=[
            pltpu.VMEM((2, rows, width), BF16),
            pltpu.VMEM((2, *gain.shape), F32),
            pltpu.VMEM((2, rows, width), BF16),
            pltpu.SemaphoreType.DMA((8,)),
        ],
    )


def normalize_backward(index, features, theirs, gain, parts):
    _, rows, width = features.shape

    def kernel(index_ref, own_ref, theirs_ref, gain_ref, *refs):
        gain = gain_ref[pl.ds(index_ref[0], 1)]
        for k, value in enumerate((own_ref[0], theirs_ref[...])):
            standard, inverse = moments(value.astype(F32))
            total = refs[0][k].astype(F32)
            for ref in refs[1:-1]:
                total = total + ref[k].astype(F32)
            scaled = total * gain
            hidden = inverse * (
                scaled
                - jnp.mean(scaled, axis=-1, keepdims=True)
                - standard * jnp.mean(scaled * standard, axis=-1, keepdims=True)
            )
            refs[-1][k] = hidden.astype(BF16)

    shape = out(2, rows, width)
    return call(
        kernel,
        index,
        [features, theirs, gain, *parts],
        [pl.BlockSpec((1, rows, width), lambda i, idx: (idx[0], 0, 0)), full(theirs), full(gain)]
        + [full(p) for p in parts],
        [shape],
        [full(shape)],
        (1,),
    )[0]


def weight_grad_blocks(index, normed, grads, wanted):
    rows = normed[0].shape[-1]
    stacked = len(normed) == 1
    count = len(normed)
    half = rows // 2
    part = grads[0].shape[1] // 4
    shapes = [out(half, blocks * part, dtype=dtype) for _, _, blocks, dtype in wanted]

    def kernel(index_ref, *refs):
        normed_hbm, gs, outs = refs[:count], refs[count : count + 4], refs[count + 4 : count + 4 + len(wanted)]
        held, turned, grad, *results, sems = refs[count + 4 + len(wanted) :]
        copies = Copies(sems)
        rows_in = {}
        for t in range(4):
            for k in range(2):
                source = normed_hbm[0].at[t, k] if stacked else normed_hbm[t].at[k]
                rows_in[t, k] = copies.start((source, held.at[t, k]))
        grads_in = {}
        for j in (2, 1, 3, 0):
            for n in range(4):
                source = gs[n].at[:, j * part : (j + 1) * part]
                target = grad.at[256 * n : 256 * (n + 1), j * part : (j + 1) * part]
                grads_in.setdefault(j, []).extend(copies.start((source, target)))
        for t in range(4):
            for k in range(2):
                wait(rows_in[t, k])
                at = pl.multiple_of((4 * k + index_ref[(SLOT_OF if stacked else SLOTS) + t]) * 128, 128)
                turned[:, pl.ds(at, 128)] = held[t, k].T
        copies_out = []
        for (h, first, blocks, dtype), out_ref, result in zip(wanted, outs, results):
            for j in range(first, first + blocks):
                wait(grads_in.pop(j, []))
            mine = turned[h * half : (h + 1) * half]
            result[...] = dot(mine, grad[:, first * part : (first + blocks) * part]).astype(dtype)
            for k in range(blocks):
                where = (slice(None), slice(k * part, (k + 1) * part))
                copies_out += copies.start((result.at[where], out_ref.at[where]))
        wait(copies_out)

    return call(
        kernel,
        index,
        [*normed, *grads],
        [ANY] * (count + 4),
        shapes,
        [ANY] * len(shapes),
        (1,),
        scratch=[
            pltpu.VMEM((4, *normed[0].shape[-3:]), BF16),
            pltpu.VMEM((rows, 1024), BF16),
            pltpu.VMEM((1024, 4 * part), BF16),
            *(pltpu.VMEM(s.shape, s.dtype) for s in shapes),
            pltpu.SemaphoreType.DMA((24 + sum(blocks for _, _, blocks, _ in wanted),)),
        ],
    )


def row_gradients(index, grads, proj_weight):
    cols = proj_weight.shape[1]
    part = cols // 4
    width = proj_weight.shape[0] // 2
    tile = 256

    def kernel(index_ref, *refs):
        gs, w, result, held, acc, sems = refs[:4], refs[4], refs[5:9], refs[9], refs[10], refs[11]

        @pl.when(pl.program_id(0) == 0)
        def _():
            copies = Copies(sems)
            for j in range(4):
                at = pl.multiple_of(index_ref[AROUND + j] * part, part)
                for n in range(4):
                    source = gs[n].at[:, j * part : (j + 1) * part]
                    copies.start((source, held.at[256 * n : 256 * (n + 1), pl.ds(at, part)]))
            wait(copies.all)

        acc[...] = dot(held[...], w[...], (1, 1)).astype(BF16)
        for t in range(4):
            for k in range(2):
                at = pl.multiple_of((4 * k + index_ref[SLOTS + t]) * 128, 128)
                result[t][k] = acc[pl.ds(at, 128)]

    shapes = [out(2, 128, width)] * 4
    return call(
        kernel,
        index,
        [*grads, proj_weight],
        [ANY] * 4 + [pl.BlockSpec((tile, cols), lambda i, idx: (idx[0] * (width // tile) + i, 0))],
        shapes,
        [pl.BlockSpec((2, 128, tile), lambda i, idx: (0, 0, i))] * 4,
        (width // tile,),
        scratch=[pltpu.VMEM((1024, cols), BF16), pltpu.VMEM((1024, tile), BF16), pltpu.SemaphoreType.DMA((16,))],
    )


def project(index, chunks, proj_weight):
    width, cols = proj_weight.shape[0] // 2, proj_weight.shape[1]
    flat = [piece for chunk in chunks for piece in chunk]
    count = len(flat)
    part = cols // 4

    def kernel(index_ref, *refs):
        ins, w_hbm, own, other = refs[:count], refs[count], refs[count + 1], refs[count + 2]
        held, w, result, sems = refs[count + 3 :]
        copies = Copies(sems)
        base = index_ref[0] * width

        def weights(i):
            pairs = []
            for k in range(4):
                rows = pl.ds(pl.multiple_of(base + k * (width // 4), width // 4), width // 4)
                here = slice(i * part, (i + 1) * part)
                pairs.append((w_hbm.at[rows, here], w.at[k * (width // 4) : (k + 1) * (width // 4), here]))
            return copies.start(*pairs)

        weights_in = [weights(0)]
        rows_in = []
        for m, (first, size) in enumerate(ROW_CHUNKS):
            pieces = ins[sum(len(chunk) for chunk in chunks[:m]) :][: len(chunks[m])]
            for t in range(4):
                for k in range(2):
                    stacked = len(pieces) == 1
                    slot = index_ref[(SLOT_OF if stacked else SLOTS) + t]
                    at = pl.multiple_of((4 * k + slot) * 128, 128)
                    source = pieces[0].at[t, k] if stacked else pieces[t].at[k]
                    rows_in += copies.start((source, held.at[pl.ds(at, 128), first : first + size]))
        weights_in += [weights(i) for i in range(1, 4)]
        wait(rows_in)
        copies_out = []
        for i in range(4):
            wait(weights_in[i])
            here = slice(i * part, (i + 1) * part)
            for rows, target in ((slice(512, 1024), other), (slice(0, 512), own)):
                result[rows, here] = dot(held[rows], w[:, here]).astype(BF16)
                copies_out += copies.start((result.at[rows, here], target.at[:, here]))
        wait(copies_out)

    shapes = [out(512, cols)] * 2
    return call(
        kernel,
        index,
        [*flat, proj_weight],
        [ANY] * (count + 1),
        shapes,
        [ANY] * 2,
        (1,),
        scratch=[
            pltpu.VMEM((1024, width), BF16),
            pltpu.VMEM((width, cols), BF16),
            pltpu.VMEM((1024, cols), BF16),
            pltpu.SemaphoreType.DMA((24 + 8 * len(chunks),)),
        ],
    )


EVERY = slice(None)


def add_first(next_a, next_b, got_a, got_b):
    part = next_a.shape[1]
    left, right = (EVERY, slice(0, part)), (EVERY, slice(part, 2 * part))
    return sums([(next_a, (EVERY, EVERY)), (got_a, right)], [(next_b, (EVERY, EVERY)), (got_b, left)])


def add_second(keep_a, keep_b, got_a, got_b, more_a, more_b):
    part = keep_a.shape[1]
    whole, left, right = (EVERY, EVERY), (EVERY, slice(0, part)), (EVERY, slice(part, 2 * part))
    return sums(
        [(keep_a, whole), (got_a, left), (more_a, whole)],
        [(keep_b, whole), (got_b, right), (more_b, whole)],
        stack=True,
    )[0]


def add_third(keep, other):
    half = keep.shape[0] // 2
    top, bottom = (slice(0, half), EVERY), (slice(half, 2 * half), EVERY)
    return sums([(keep, top), (other, top)], [(keep, bottom), (other, bottom)])


def join(left_a, left_b, right_a, right_b):
    half, part = left_a.shape

    def kernel(*refs):
        ins, outs, held, sems = refs[:4], refs[4:7], refs[7], refs[8]
        copies = Copies(sems)
        arrived = [
            copies.start((ref, held.at[n % 2, :, (n // 2) * part : (n // 2 + 1) * part])) for n, ref in enumerate(ins)
        ]
        done = []
        for n in range(2):
            wait(arrived[n], arrived[n + 2])
            done += copies.start((held.at[n], outs[n]), (held.at[n], outs[2].at[n * half : (n + 1) * half]))
        wait(done)

    return pl.pallas_call(
        kernel,
        in_specs=[ANY] * 4,
        out_specs=[ANY] * 3,
        out_shape=[out(half, 2 * part), out(half, 2 * part), out(2 * half, 2 * part)],
        scratch_shapes=[pltpu.VMEM((2, half, 2 * part), BF16), pltpu.SemaphoreType.DMA((8,))],
        compiler_params=pltpu.CompilerParams(vmem_limit_bytes=VMEM_LIMIT),
        cost_estimate=pl.CostEstimate(flops=1, bytes_accessed=1, transcendentals=0),
    )(left_a, left_b, right_a, right_b)


def place(index, pieces, start, width, cols, into):
    part = cols // 4
    half = next(size for first, size in ROW_CHUNKS if first == start) // 2
    arrays = []
    for piece in pieces:
        if not any(piece[0] is a for a in arrays):
            arrays.append(piece[0])
    which = [next(k for k, a in enumerate(arrays) if a is piece[0]) for piece in pieces]
    count = len(arrays)

    def kernel(index_ref, *refs):
        sources, result = refs[:count], refs[-3]
        held, sems = refs[-2], refs[-1]
        copies = Copies(sems)
        blocks = (slice(0, part), slice(part, 2 * part))
        arrived = [
            [copies.start((sources[k].at[row : row + half, b], held.at[n, :, b])) for b in blocks]
            for n, (k, (_, row, _, _, _)) in enumerate(zip(which, pieces))
        ]
        placed = []
        for n, (_, _, other, h, js) in enumerate(pieces):
            tap = 1 - index_ref[0] if other else index_ref[0]
            rows = pl.ds(pl.multiple_of(tap * width + start + h * half, 64), half)
            for b, j, ready in zip(blocks, js, arrived[n]):
                wait(ready)
                at = pl.ds(pl.multiple_of(index_ref[AROUND + j] * part, part), part)
                placed += copies.start((held.at[n, :, b], result.at[rows, at]))
        wait(placed)

    operands = arrays + ([] if into is None else [into])
    return call(
        kernel,
        index,
        operands,
        [ANY] * len(operands),
        [out(2 * width, cols)],
        [ANY],
        (1,),
        scratch=[pltpu.VMEM((len(pieces), half, 2 * part), BF16), pltpu.SemaphoreType.DMA((4 * len(pieces),))],
        aliases={} if into is None else {count + 1: 0},
    )[0]


class Phases:
    def __init__(self):
        self.here, self.away = {}, {}

    def __getitem__(self, name):
        return self.here[name]

    def __setitem__(self, name, value):
        self.here[name] = value

    def send(self, name, source, pairs, axis="dp"):
        self.away[name] = swap(self.here[source], pairs, axis)

    def land(self, *names):
        for name in names:
            self.here[name] = self.away.pop(name)

    def end(self, *drop):
        for name in drop:
            del self.here[name]
        self.here = lax.optimization_barrier(self.here)


def body(features, layer_norm_gain, layer_norm_bias, proj_weight, cotangent):
    width = layer_norm_gain.shape[1]
    cols = proj_weight.shape[1]
    half = ROW_CHUNKS[0][1] // 2
    wanted = (
        (0, 1, 2, BF16),
        (1, 2, 2, BF16),
        (0, 3, 1, BF16),
        (1, 1, 1, BF16),
        (0, 0, 1, BF16),
        (1, 0, 1, BF16),
    )
    v = Phases()

    def near(n):
        return [v["n%d" % n], *(v["x%d%d" % (n, k)] for k in (1, 3, 2))]

    def grads():
        return [v["mine"], v["away"], v["mine_c"], v["away_c"]]

    def products(t):
        names = "send_a", "send_b", "next_a", "next_b", "keep_a", "keep_b"
        for name, value in zip(names, weight_grad_blocks(v["index"], near(t), grads(), wanted)):
            v[name + str(t)] = value

    def spread(t):
        v["a%d" % t], v["b%d" % t], v["ab%d" % t] = join(*(v[n + str(t)] for n in ("da", "db", "ga", "gb")))

    def finish(t, early, late):
        pieces = []
        if early:
            for name, other in (("ab%d", False), ("ab%d_c", True)):
                array = v[name % t]
                pieces += [(array, 0, other, 0, (0, 3)), (array, half, other, 1, (0, 1))]
        if late:
            for name, other in (("l%s%d", False), ("l%s%d_c", True)):
                pieces += [(v[name % ("a", t)], 0, other, 0, (1, 2)), (v[name % ("b", t)], 0, other, 1, (3, 2))]
        v["weight_grad"] = place(v["index"], pieces, ROW_CHUNKS[t][0], width, cols, v.here.get("weight_grad"))

    v["theirs"], v["mine"], v["index"] = prepare(features, cotangent)
    v.end()

    v.send("away", "mine", SECTION, "section")
    v.send("rows", "theirs", CORE)
    v.send("mine_c", "mine", CORE)
    v.land("rows")
    v["n0"], v["n1"] = normalize(v["index"], features, v["rows"], layer_norm_gain, layer_norm_bias)
    v.land("mine_c")
    v.end("theirs")

    for k in (1, 3, 2):
        v.send("x0%d" % k, "n0", shift(-k), "tensor")
    v.land("x01", "x03", "x02", "away")
    v.end()

    v.send("away_c", "away", CORE)
    v.land("away_c")
    v.end()

    v.send("x11", "n1", shift(-1), "tensor")
    v.send("x13", "n1", shift(-3), "tensor")
    products(0)
    v.land("x11", "x13")
    v.end()

    v.send("got_a0", "send_a0", Y1)
    v.send("got_b0", "send_b0", Y3)
    v.send("x12", "n1", shift(-2), "tensor")
    for k, part in zip((0, 1, 3, 2), row_gradients(v["index"], grads(), proj_weight)):
        v["r%d" % k] = part
    v.land("got_a0", "got_b0", "x12")
    v.end("send_a0", "send_b0")

    v["n_a0"], v["n_b0"] = add_first(v["next_a0"], v["next_b0"], v["got_a0"], v["got_b0"])
    v.end("next_a0", "next_b0")

    v.send("more_a0", "n_a0", Y3)
    v.send("more_b0", "n_b0", Y1)
    products(1)
    v.land("more_a0", "more_b0")
    v.end("n_a0", "n_b0", "mine", "away", "mine_c", "away_c")

    v["keep0"] = add_second(*(v[n + "0"] for n in ("keep_a", "keep_b", "got_a", "got_b", "more_a", "more_b")))
    v.end("keep_a0", "keep_b0", "got_a0", "got_b0", "more_a0", "more_b0")

    v.send("got_a1", "send_a1", Y1)
    v.send("got_b1", "send_b1", Y3)
    v.send("other0", "keep0", ZLO)
    v.send("s2", "r2", shift(2), "tensor")
    v["own"], v["other"] = project(v["index"], [near(0), near(1)], proj_weight)
    v.land("got_a1", "got_b1", "other0", "s2")
    v.end("r2", "send_a1", "send_b1", "x01", "x03", "x02", "x11", "x13", "x12", "n0", "n1")

    v["n_a1"], v["n_b1"] = add_first(v["next_a1"], v["next_b1"], v["got_a1"], v["got_b1"])
    v["da0"], v["db0"] = add_third(v["keep0"], v["other0"])
    v.end("next_a1", "next_b1", "keep0", "other0")

    v.send("more_a1", "n_a1", Y3)
    v.send("more_b1", "n_b1", Y1)
    v.send("ga0", "da0", Y3)
    v.send("gb0", "db0", Y1)
    v.send("other_c", "other", CORE)
    v.land("more_a1", "more_b1", "ga0", "gb0", "other_c")
    v.end("n_a1", "n_b1", "other")

    v["keep1"] = add_second(*(v[n + "1"] for n in ("keep_a", "keep_b", "got_a", "got_b", "more_a", "more_b")))
    spread(0)
    v.end("keep_a1", "keep_b1", "got_a1", "got_b1", "more_a1", "more_b1", "da0", "db0", "ga0", "gb0")

    v.send("other1", "keep1", ZLO)
    v.send("la0", "a0", Y1)
    v.send("lb0", "b0", Y3)
    v.send("s1", "r1", shift(1), "tensor")
    v.send("s3", "r3", shift(3), "tensor")
    rows = [slice(128 * n, 128 * (n + 1)) for n in range(4)]
    v["up0"], v["up1"] = sums(*([(v["own"], (r, EVERY)), (v["other_c"], (r, EVERY))] for r in rows[2:]))
    v.land("other1", "la0", "lb0", "s1", "s3")
    v.end("a0", "b0", "r1", "r3")

    v["da1"], v["db1"] = add_third(v["keep1"], v["other1"])
    v.end("keep1", "other1")

    v.send("ga1", "da1", Y3)
    v.send("gb1", "db1", Y1)
    v.send("back0", "up0", SECTION, "section")
    v.send("ab0_c", "ab0", CORE)
    v.send("la0_c", "la0", CORE)
    hidden = normalize_backward(
        v["index"], features, v["rows"], layer_norm_gain, [v["r0"], v["s1"], v["s3"], v["s2"]]
    )
    v["ours"], v["hidden"] = hidden[0], hidden[1]
    v.land("ga1", "gb1", "ab0_c", "la0_c", "back0")
    v.end("up0", "r0", "s1", "s3", "s2")

    spread(1)
    v.end("da1", "db1", "ga1", "gb1")

    v.send("la1", "a1", Y1)
    v.send("lb1", "b1", Y3)
    v.send("ab1_c", "ab1", CORE)
    v.send("back1", "up1", SECTION, "section")
    v.send("lb0_c", "lb0", CORE)
    v.land("lb0_c")
    finish(0, True, True)
    v.land("ab1_c")
    finish(1, True, False)
    v.land("la1", "lb1", "back1")
    v.end("a1", "b1", "ab0", "ab0_c", "ab1", "ab1_c", "la0", "lb0", "la0_c", "lb0_c", "up1")

    v.send("la1_c", "la1", CORE)
    v.send("lb1_c", "lb1", CORE)
    v.send("hidden_c", "hidden", CORE)
    v["projected"] = sums(
        *([(v["own"], (r, EVERY)), (v["other_c"], (r, EVERY)), (v[b], (EVERY, EVERY))] for r, b in zip(rows, ("back0", "back1"))),
        stack=True,
    )[0]
    v.land("la1_c", "lb1_c", "hidden_c")
    v.end("own", "other_c", "back0", "back1", "hidden")
    finish(1, False, True)
    v["result"] = jnp.where(
        v["index"][0] == 0, jnp.stack([v["ours"], v["hidden_c"]]), jnp.stack([v["hidden_c"], v["ours"]])
    )
    return (v["projected"][None], v["weight_grad"], v["result"])


def solution(mesh):
    return jax.shard_map(
        body,
        mesh=mesh,
        in_specs=(
            P("section", ("dp", "tensor"), None),
            P("section", None),
            P("section", None),
            P("section", "tensor"),
            P("dp", "section", "tensor"),
        ),
        out_specs=(
            P("dp", "section", "tensor"),
            P("section", "tensor"),
            P("section", ("dp", "tensor"), None),
        ),
        check_vma=False,
    )
```

time: 436 us -> 184 us (0.42)
  waiting for transfers between devices: 374 us -> 64.7 us
  Pallas kernels: 0 us -> 55.8 us
  starting transfers between devices: 0.2 us -> 53.8 us
  matrix products: 31.3 us -> 0 us
  between operations: 13.8 us -> 1.16 us
    psum x1 -> x0, waiting for transfers between devices: 238 us -> none  [body(): summed = lax.psum(partial_value.astype(jnp.bfloat16), 'dp')]
    all_gather x2 -> x0, waiting for transfers between devices: 77.2 us -> none  [the longest x1 42.3 us: body(): grads = lax.all_gather(cotangent, 'section', axis=1, tiled=True)[0]]
    ppermute x0 -> x41, waiting for transfers between devices: none -> 64.7 us  [swap(): return lax.ppermute(value, axis, pairs)]
    reduce_scatter x2 -> x0, waiting for transfers between devices: 58 us -> none  [the longest x1 31.8 us: body(): lax.psum_scatter(jnp.einsum('ro,lco->rlc', rows, weight, preferred_elemen...]
    pallas_call x0 -> x20, Pallas kernels: none -> 55.8 us  [the longest x9 45 us: call(): pl.pallas_call(kernel, grid_spec=pltpu.PrefetchScalarGridSpec(num_scalar_...]
    ppermute x0 -> x41, starting transfers between devices: none -> 53.8 us  [swap(): return lax.ppermute(value, axis, pairs)]
    dot_general x3 -> x0, matrix products: 31.3 us -> none  [the longest x1 11.3 us: body(): jnp.einsum('lrc,lco->ro', rows, weight, preferred_element_type=jnp.float32)]
    unnamed x9 -> x20, local copies, waits for them, and re-layouts: 11.3 us -> 7.72 us
  transfers between devices with their start and end apart: 5 -> 41, of which waited for: 5 -> 20; matrix products, arithmetic and copies ran while one was open for 2% -> 0% of each run, Pallas kernels for 0% -> 24%
where the time goes in v2:
time: 184 us
  waiting for transfers between devices  64.7 us (35%)
  Pallas kernels  55.8 us (30%)
  starting transfers between devices  53.8 us (29%)
  local copies, waits for them, and re-layouts  7.76 us (4%)
    ppermute x41, waiting for transfers between devices, swap(): return lax.ppermute(value, axis, pairs)  64.7 us
    ppermute x41, starting transfers between devices, swap(): return lax.ppermute(value, axis, pairs)  53.8 us
    pallas_call x9, Pallas kernels, call(): pl.pallas_call(kernel, grid_spec=pltpu.PrefetchScalarGridSpec(num_scalar_...  45 us
    unnamed x20, local copies, waits for them, and re-layouts  7.72 us
    pallas_call x8, Pallas kernels, sums(): pl.pallas_call(kernel, in_specs=[ANY] * count, out_specs=[ANY] * len(made...  7.62 us
  transfers between devices with their start and end apart: 41, of which 20 were waited for; matrix products, arithmetic and copies ran while one was open for 0% of the time, Pallas kernels for 24%

profile of v2, /device:TPU:1, one launch (start us, length us, event | category | flops | bytes accessed | tf_op | source)
XLA Modules:
  0.0 184.2 jit_solution(2173169451459148119)
XLA Ops:
  5.6 3.7 %collective-permute-start = (bf16[256,2048]{1,0:T(8,128)(2,1)S(1)}, bf16[256,2048]{1,0:T(8,128)(2,1)S(1)}, u32[]{:S(2)}, u32[]{:S(2)}) collective-permute-start(bf16[256,2048]{1,0:T(8,128)(2,1)S(1)} %get-tuple-element.426.refs_4_.refs_0_), channel_id=1, source_target_pairs={{0,64},{64,0},{1,65},{65,1},{2,66},{66,2},{3,67},{67,3},{4,68},{68... | collective-permute-start | bytes 3145736 | tf_op jit(solution)/shard_map/ppermute | solution.py:32
  15.2 2.5 %collective-permute-start.4 = (bf16[2,128,640]{2,1,0:T(8,128)(2,1)S(1)}, bf16[2,128,640]{2,1,0:T(8,128)(2,1)S(1)}, u32[]{:S(2)}, u32[]{:S(2)}) collective-permute-start(bf16[2,128,640]{2,1,0:T(8,128)(2,1)S(1)} %get-tuple-element.482.refs_0_), channel_id=1, source_target_pairs={{0,2},{1,3},{2,0},{3,1},{4,6},{5,7},{6,4},{7,5},{8,10},{9,11},{10,... | collective-permute-start | bytes 983048 | tf_op jit(solution)/shard_map/ppermute | solution.py:32
  18.8 14.0 %collective-permute-done.refs_5_.refs_1_ = bf16[256,2048]{1,0:T(8,128)(2,1)S(1)} collective-permute-done((bf16[256,2048]{1,0:T(8,128)(2,1)S(1)}, bf16[256,2048]{1,0:T(8,128)(2,1)S(1)}, u32[]{:S(2)}, u32[]{:S(2)}) %collective-permute-start) | collective-permute-done | bytes 1048608 | tf_op jit(solution)/shard_map/ppermute | solution.py:32
  33.5 2.3 %collective-permute-done.6.refs_7_.refs_3_ = bf16[256,2048]{1,0:T(8,128)(2,1)S(1)} collective-permute-done((bf16[256,2048]{1,0:T(8,128)(2,1)S(1)}, bf16[256,2048]{1,0:T(8,128)(2,1)S(1)}, u32[]{:S(2)}, u32[]{:S(2)}) %collective-permute-start.6) | collective-permute-done | bytes 1048608 | tf_op jit(solution)/shard_map/ppermute | solution.py:32
  38.5 8.1 %shard_map.78 = (bf16[320,1024]{1,0:T(8,128)(2,1)S(1)}, bf16[320,1024]{1,0:T(8,128)(2,1)S(1)}, bf16[320,512]{1,0:T(8,128)(2,1)S(1)}, bf16[320,512]{1,0:T(8,128)(...) custom-call(s32[13]{0:T(128)S(1)} %get-tuple-element.645.index_ref, ...), custom_call_target="tpu_custom_call" | custom-call | flops 1 | bytes 1 | tf_op jit(solution)/shard_map/pallas_call | solution.py:147
  51.4 4.0 %copy-done = bf16[2560,2048]{1,0:T(8,128)(2,1)S(1)} copy-done((bf16[2560,2048]{1,0:T(8,128)(2,1)S(1)}, bf16[2560,2048]{1,0:T(8,128)(2,1)}, u32[]{:S(2)}) %copy-start) | copy-done | bytes 10485784
  55.4 8.2 %shard_map.79 = (bf16[2,128,1280]{2,1,0:T(8,128)(2,1)S(1)}, bf16[2,128,1280]{2,1,0:T(8,128)(2,1)S(1)}, bf16[2,128,1280]{2,1,0:T(8,128)(2,1)S(1)}, bf16[2,128,1280]{2,1,0:T(8,128)(2,1)S(1)}) custom-call(s32[13]{0:T(128)S(1)} %get-tuple-element.645.index_ref, bf16[256,2048]{1,0:T(8,128)(2,1)S(1)} %get-tuple-element.426.refs_4_.refs_0_, ...), custom_call_target="tpu_custom_call" | custom-call | flops 1 | bytes 1 | tf_op jit(solution)/shard_map/pallas_call | solution.py:147
  64.9 2.0 %collective-permute-start.12 = (bf16[320,512]{1,0:T(8,128)(2,1)S(1)}, bf16[320,512]{1,0:T(8,128)(2,1)S(1)}, u32[]{:S(2)}, u32[]{:S(2)}) collective-permute-start(bf16[320,512]{1,0:T(8,128)(2,1)S(1)} %get-tuple-element.433), channel_id=1, source_target_pairs={{0,48},{4,52},{8,56},{12,60},{16,32},{20,36},{24,40},{28,44},{32,1... | collective-permute-start | bytes 983048 | tf_op jit(solution)/shard_map/ppermute | solution.py:32
  66.9 8.1 %shard_map.81 = (bf16[320,1024]{1,0:T(8,128)(2,1)S(1)}, bf16[320,1024]{1,0:T(8,128)(2,1)S(1)}, bf16[320,512]{1,0:T(8,128)(2,1)S(1)}, bf16[320,512]{1,0:T(8,128)(...) custom-call(s32[13]{0:T(128)S(1)} %get-tuple-element.645.index_ref, ...), custom_call_target="tpu_custom_call" | custom-call | flops 1 | bytes 1 | tf_op jit(solution)/shard_map/pallas_call | solution.py:147
  80.6 9.3 %shard_map.83 = (bf16[512,2048]{1,0:T(8,128)(2,1)S(1)}, bf16[512,2048]{1,0:T(8,128)(2,1)S(1)}) custom-call(s32[13]{0:T(128)S(1)} %get-tuple-element.645.index_ref, bf16[2,128,640]{2,1,0:T(8,128)(2,1)S(1)} %get-tuple-element.482.refs_0_, bf16[2,128,640]{2,1,0:T(8,128)(2,1)S(1)} %collective-permute-done.3.refs_1_, ...), custom_call_target="tpu_custom_call" | custom-call | flops 1 | bytes 1 | tf_op jit(solution)/shard_map/pallas_call | solution.py:147
  90.0 2.1 %collective-permute-done.15.refs_3_.refs_4_ = bf16[320,1024]{1,0:T(8,128)(2,1)S(1)} collective-permute-done((bf16[320,1024]{1,0:T(8,128)(2,1)S(1)}, bf16[320,1024]{1,0:T(8,128)(2,1)S(1)}, u32[]{:S(2)}, u32[]{:S(2)}) %collective-permute-start.15) | collective-permute-done | bytes 655392 | tf_op jit(solution)/shard_map/ppermute | solution.py:32
  94.5 4.3 %collective-permute-start.22 = (bf16[512,2048]{1,0:T(8,128)(2,1)S(1)}, bf16[512,2048]{1,0:T(8,128)(2,1)S(1)}, u32[]{:S(2)}, u32[]{:S(2)}) collective-permute-start(bf16[512,2048]{1,0:T(8,128)(2,1)S(1)} %get-tuple-element.526), channel_id=1, source_target_pairs={{0,4},{4,0},{8,12},{12,8},{16,20},{20,16},{24,28},{28,24},{32,36},... | collective-permute-start | bytes 6291464 | tf_op jit(solution)/shard_map/ppermute | solution.py:32
  102.3 6.9 %collective-permute-done.20.refs_2_ = bf16[320,512]{1,0:T(8,128)(2,1)S(1)} collective-permute-done((bf16[320,512]{1,0:T(8,128)(2,1)S(1)}, bf16[320,512]{1,0:T(8,128)(2,1)S(1)}, u32[]{:S(2)}, u32[]{:S(2)}) %collective-permute-start.20) | collective-permute-done | bytes 327712 | tf_op jit(solution)/shard_map/ppermute | solution.py:32
  109.6 6.7 %collective-permute-done.18.refs_2_ = bf16[320,512]{1,0:T(8,128)(2,1)S(1)} collective-permute-done((bf16[320,512]{1,0:T(8,128)(2,1)S(1)}, bf16[320,512]{1,0:T(8,128)(2,1)S(1)}, u32[]{:S(2)}, u32[]{:S(2)}) %collective-permute-start.18) | collective-permute-done | bytes 327712 | tf_op jit(solution)/shard_map/ppermute | solution.py:32
  120.6 2.6 %collective-permute-start.27 = (bf16[2,128,1280]{2,1,0:T(8,128)(2,1)S(1)}, bf16[2,128,1280]{2,1,0:T(8,128)(2,1)S(1)}, u32[]{:S(2)}, u32[]{:S(2)}) collective-permute-start(bf16[2,128,1280]{2,1,0:T(8,128)(2,1)S(1)} %get-tuple-element.565), channel_id=1, source_target_pairs={{0,3},{1,0},{2,1},{3,2},{4,7},{5,4},{6,5},{7,6},{8,11},{9,8},{10,9... | collective-permute-start | bytes 1966088 | tf_op jit(solution)/shard_map/ppermute | solution.py:32
  124.8 9.1 %collective-permute-done.23.refs_2_ = bf16[320,1024]{1,0:T(8,128)(2,1)S(1)} collective-permute-done((bf16[320,1024]{1,0:T(8,128)(2,1)S(1)}, bf16[320,1024]{1,0:T(8,128)(2,1)S(1)}, u32[]{:S(2)}, u32[]{:S(2)}) %collective-permute-start.23) | collective-permute-done | bytes 655392 | tf_op jit(solution)/shard_map/ppermute | solution.py:32
  138.5 2.7 %collective-permute-start.28 = (bf16[640,1024]{1,0:T(8,128)(2,1)S(1)}, bf16[640,1024]{1,0:T(8,128)(2,1)S(1)}, u32[]{:S(2)}, u32[]{:S(2)}) collective-permute-start(bf16[640,1024]{1,0:T(8,128)(2,1)S(1)} %get-tuple-element.629.refs_0_), channel_id=1, source_target_pairs={{0,4},{4,0},{8,12},{12,8},{16,20},{20,16},{24,28},{28,24},{32,36},... | collective-permute-start | bytes 3932168 | tf_op jit(solution)/shard_map/ppermute | solution.py:32
  141.3 3.0 %collective-permute-start.29 = (bf16[128,2048]{1,0:T(8,128)(2,1)S(1)}, bf16[128,2048]{1,0:T(8,128)(2,1)S(1)}, u32[]{:S(2)}, u32[]{:S(2)}) collective-permute-start(bf16[128,2048]{1,0:T(8,128)(2,1)S(1)} %get-tuple-element.586), channel_id=1, source_target_pairs={{0,64},{64,0},{1,65},{65,1},{2,66},{66,2},{3,67},{67,3},{4,68},{68... | collective-permute-start | bytes 1572872 | tf_op jit(solution)/shard_map/ppermute | solution.py:32
  147.4 6.7 %collective-permute-done.30.refs_2_ = bf16[320,512]{1,0:T(8,128)(2,1)S(1)} collective-permute-done((bf16[320,512]{1,0:T(8,128)(2,1)S(1)}, bf16[320,512]{1,0:T(8,128)(2,1)S(1)}, u32[]{:S(2)}, u32[]{:S(2)}) %collective-permute-start.30) | collective-permute-done | bytes 327712 | tf_op jit(solution)/shard_map/ppermute | solution.py:32
  160.3 3.0 %collective-permute-start.33 = (bf16[128,2048]{1,0:T(8,128)(2,1)S(1)}, bf16[128,2048]{1,0:T(8,128)(2,1)S(1)}, u32[]{:S(2)}, u32[]{:S(2)}) collective-permute-start(bf16[128,2048]{1,0:T(8,128)(2,1)S(1)} %get-tuple-element.620), channel_id=1, source_target_pairs={{0,64},{64,0},{1,65},{65,1},{2,66},{66,2},{3,67},{67,3},{4,68},{68... | collective-permute-start | bytes 1572872 | tf_op jit(solution)/shard_map/ppermute | solution.py:32
  163.3 3.5 %shard_map.92.refs_2_ = bf16[2560,2048]{1,0:T(8,128)(2,1)} custom-call(s32[13]{0:T(128)S(1)} %get-tuple-element.645.index_ref, bf16[640,1024]{1,0:T(8,128)(2,1)S(1)} %get-tuple-element.629.refs_0_, bf16[640,1024]{1,0:T(8,128)(2,1)S(1)} %collective-permute-done.28.refs_1_, bf16[320,1024]{1,0:T(8,128)(2,1)S(1)} %collective-permute-done.23.refs_2_, ...), custom_call_target="tpu_custom_call" | custom-call | flops 1 | bytes 1 | tf_op jit(solution)/shard_map/pallas_call | solution.py:147
  166.8 2.4 %shard_map.93.refs_4_ = bf16[2560,2048]{1,0:T(8,128)(2,1)} custom-call(s32[13]{0:T(128)S(1)} %get-tuple-element.645.index_ref, bf16[640,1024]{1,0:T(8,128)(2,1)S(1)} %get-tuple-element.628.refs_0_, bf16[640,1024]{1,0:T(8,128)(2,1)S(1)} %collective-permute-done.36.refs_1_, bf16[2560,2048]{1,0:T(8,128)(2,1)} %shard_map.92.refs_2_), custom_call_target="tpu_custom_call", output_to_operand_aliasing={{}: (3, {})} | custom-call | flops 1 | bytes 1 | tf_op jit(solution)/shard_map/pallas_call | solution.py:147
  169.2 5.1 %collective-permute-done.33.refs_5_ = bf16[128,2048]{1,0:T(8,128)(2,1)S(1)} collective-permute-done((bf16[128,2048]{1,0:T(8,128)(2,1)S(1)}, bf16[128,2048]{1,0:T(8,128)(2,1)S(1)}, u32[]{:S(2)}, u32[]{:S(2)}) %collective-permute-start.33) | collective-permute-done | bytes 524320 | tf_op jit(solution)/shard_map/ppermute | solution.py:32
  181.6 2.3 %shard_map.95 = bf16[2560,2048]{1,0:T(8,128)(2,1)} custom-call(s32[13]{0:T(128)S(1)} %get-tuple-element.645.index_ref, bf16[320,1024]{1,0:T(8,128)(2,1)S(1)} %collective-permute-done.34.refs_0_, bf16[320,1024]{1,0:T(8,128)(2,1)S(1)} %collective-permute-done.35.refs_1_, ...), custom_call_target="tpu_custom_call", output_to_operand_aliasing={{}: (5, {})} | custom-call | flops 1 | bytes 1 | tf_op jit(solution)/shard_map/pallas_call | solution.py:147
  (101 shorter events, 60.7 us)
Async XLA Ops:
  5.6 27.1 %collective-permute-start = (bf16[256,2048]{1,0:T(8,128)(2,1)S(1)}, bf16[256,2048]{1,0:T(8,128)(2,1)S(1)}, u32[]{:S(2)}, u32[]{:S(2)}) collective-permute-start(bf16[256,2048]{1,0:T(8,128)(2,1)S(1)} %get-tuple-element.426.refs_4_.refs_0_), channel_id=1, source_target_pairs={{0,64},{64,0},{1,65},{65,1},{2,66},{66,2},{3,67},{67,3},{4,68},{68... | collective-permute-start | bytes 3145736 | tf_op jit(solution)/shard_map/ppermute | solution.py:32
  13.9 18.8 %collective-permute-start.5 = (bf16[2,128,640]{2,1,0:T(8,128)(2,1)S(1)}, bf16[2,128,640]{2,1,0:T(8,128)(2,1)S(1)}, u32[]{:S(2)}, u32[]{:S(2)}) collective-permute-start(bf16[2,128,640]{2,1,0:T(8,128)(2,1)S(1)} %get-tuple-element.482.refs_0_), channel_id=1, source_target_pairs={{0,1},{1,2},{2,3},{3,0},{4,5},{5,6},{6,7},{7,4},{8,9},{9,10},{10,1... | collective-permute-start | bytes 983048 | tf_op jit(solution)/shard_map/ppermute | solution.py:32
  15.2 17.6 %collective-permute-start.4 = (bf16[2,128,640]{2,1,0:T(8,128)(2,1)S(1)}, bf16[2,128,640]{2,1,0:T(8,128)(2,1)S(1)}, u32[]{:S(2)}, u32[]{:S(2)}) collective-permute-start(bf16[2,128,640]{2,1,0:T(8,128)(2,1)S(1)} %get-tuple-element.482.refs_0_), channel_id=1, source_target_pairs={{0,2},{1,3},{2,0},{3,1},{4,6},{5,7},{6,4},{7,5},{8,10},{9,11},{10,... | collective-permute-start | bytes 983048 | tf_op jit(solution)/shard_map/ppermute | solution.py:32
  17.6 15.1 %collective-permute-start.3 = (bf16[2,128,640]{2,1,0:T(8,128)(2,1)S(1)}, bf16[2,128,640]{2,1,0:T(8,128)(2,1)S(1)}, u32[]{:S(2)}, u32[]{:S(2)}) collective-permute-start(bf16[2,128,640]{2,1,0:T(8,128)(2,1)S(1)} %get-tuple-element.482.refs_0_), channel_id=1, source_target_pairs={{0,3},{1,0},{2,1},{3,2},{4,7},{5,4},{6,5},{7,6},{8,11},{9,8},{10,9... | collective-permute-start | bytes 983048 | tf_op jit(solution)/shard_map/ppermute | solution.py:32
  46.6 16.9 %collective-permute-start.9 = (bf16[320,1024]{1,0:T(8,128)(2,1)S(1)}, bf16[320,1024]{1,0:T(8,128)(2,1)S(1)}, u32[]{:S(2)}, u32[]{:S(2)}) collective-permute-start(bf16[320,1024]{1,0:T(8,128)(2,1)S(1)} %get-tuple-element.371), channel_id=1, source_target_pairs={{0,16},{4,20},{8,24},{12,28},{16,0},{20,4},{24,8},{28,12},{32,48},... | collective-permute-start | bytes 1966088 | tf_op jit(solution)/shard_map/ppermute | solution.py:32
  48.0 16.2 %collective-permute-start.10 = (bf16[320,1024]{1,0:T(8,128)(2,1)S(1)}, bf16[320,1024]{1,0:T(8,128)(2,1)S(1)}, u32[]{:S(2)}, u32[]{:S(2)}) collective-permute-start(bf16[320,1024]{1,0:T(8,128)(2,1)S(1)} %get-tuple-element.372), channel_id=1, source_target_pairs={{0,48},{4,52},{8,56},{12,60},{16,32},{20,36},{24,40},{28,44},{32,1... | collective-permute-start | bytes 1966088 | tf_op jit(solution)/shard_map/ppermute | solution.py:32
  49.9 13.7 %collective-permute-start.11 = (bf16[2,128,640]{2,1,0:T(8,128)(2,1)S(1)}, bf16[2,128,640]{2,1,0:T(8,128)(2,1)S(1)}, u32[]{:S(2)}, u32[]{:S(2)}) collective-permute-start(bf16[2,128,640]{2,1,0:T(8,128)(2,1)S(1)} %get-tuple-element.486.refs_0_.refs_4_), channel_id=1, source_target_pairs={{0,2},{1,3},{2,0},{3,1},{4,6},{5,7},{6,4},{7,5},{8,10},{9,11},{10,... | collective-permute-start | bytes 983048 | tf_op jit(solution)/shard_map/ppermute | solution.py:32
  76.1 13.9 %collective-permute-start.14 = (bf16[320,1024]{1,0:T(8,128)(2,1)S(1)}, bf16[320,1024]{1,0:T(8,128)(2,1)S(1)}, u32[]{:S(2)}, u32[]{:S(2)}) collective-permute-start(bf16[320,1024]{1,0:T(8,128)(2,1)S(1)} %get-tuple-element.474), channel_id=1, source_target_pairs={{0,16},{4,20},{8,24},{12,28},{16,0},{20,4},{24,8},{28,12},{32,48},... | collective-permute-start | bytes 1966088 | tf_op jit(solution)/shard_map/ppermute | solution.py:32
  77.7 14.5 %collective-permute-start.15 = (bf16[320,1024]{1,0:T(8,128)(2,1)S(1)}, bf16[320,1024]{1,0:T(8,128)(2,1)S(1)}, u32[]{:S(2)}, u32[]{:S(2)}) collective-permute-start(bf16[320,1024]{1,0:T(8,128)(2,1)S(1)} %get-tuple-element.475), channel_id=1, source_target_pairs={{0,48},{4,52},{8,56},{12,60},{16,32},{20,36},{24,40},{28,44},{32,1... | collective-permute-start | bytes 1966088 | tf_op jit(solution)/shard_map/ppermute | solution.py:32
  78.5 14.5 %collective-permute-start.17 = (bf16[2,128,1280]{2,1,0:T(8,128)(2,1)S(1)}, bf16[2,128,1280]{2,1,0:T(8,128)(2,1)S(1)}, u32[]{:S(2)}, u32[]{:S(2)}) collective-permute-start(bf16[2,128,1280]{2,1,0:T(8,128)(2,1)S(1)} %get-tuple-element.496), channel_id=1, source_target_pairs={{0,2},{1,3},{2,0},{3,1},{4,6},{5,7},{6,4},{7,5},{8,10},{9,11},{10,... | collective-permute-start | bytes 1966088 | tf_op jit(solution)/shard_map/ppermute | solution.py:32
  94.5 22.1 %collective-permute-start.22 = (bf16[512,2048]{1,0:T(8,128)(2,1)S(1)}, bf16[512,2048]{1,0:T(8,128)(2,1)S(1)}, u32[]{:S(2)}, u32[]{:S(2)}) collective-permute-start(bf16[512,2048]{1,0:T(8,128)(2,1)S(1)} %get-tuple-element.526), channel_id=1, source_target_pairs={{0,4},{4,0},{8,12},{12,8},{16,20},{20,16},{24,28},{28,24},{32,36},... | collective-permute-start | bytes 6291464 | tf_op jit(solution)/shard_map/ppermute | solution.py:32
  100.7 15.6 %collective-permute-start.18 = (bf16[320,512]{1,0:T(8,128)(2,1)S(1)}, bf16[320,512]{1,0:T(8,128)(2,1)S(1)}, u32[]{:S(2)}, u32[]{:S(2)}) collective-permute-start(bf16[320,512]{1,0:T(8,128)(2,1)S(1)} %get-tuple-element.533.refs_0_), channel_id=1, source_target_pairs={{0,48},{4,52},{8,56},{12,60},{16,32},{20,36},{24,40},{28,44},{32,1... | collective-permute-start | bytes 983048 | tf_op jit(solution)/shard_map/ppermute | solution.py:32
  101.5 15.2 %collective-permute-start.19 = (bf16[320,512]{1,0:T(8,128)(2,1)S(1)}, bf16[320,512]{1,0:T(8,128)(2,1)S(1)}, u32[]{:S(2)}, u32[]{:S(2)}) collective-permute-start(bf16[320,512]{1,0:T(8,128)(2,1)S(1)} %get-tuple-element.534.refs_1_), channel_id=1, source_target_pairs={{0,16},{4,20},{8,24},{12,28},{16,0},{20,4},{24,8},{28,12},{32,48},... | collective-permute-start | bytes 983048 | tf_op jit(solution)/shard_map/ppermute | solution.py:32
  118.8 15.1 %collective-permute-start.23 = (bf16[320,1024]{1,0:T(8,128)(2,1)S(1)}, bf16[320,1024]{1,0:T(8,128)(2,1)S(1)}, u32[]{:S(2)}, u32[]{:S(2)}) collective-permute-start(bf16[320,1024]{1,0:T(8,128)(2,1)S(1)} %get-tuple-element.557), channel_id=1, source_target_pairs={{0,16},{4,20},{8,24},{12,28},{16,0},{20,4},{24,8},{28,12},{32,48},... | collective-permute-start | bytes 1966088 | tf_op jit(solution)/shard_map/ppermute | solution.py:32
  119.2 16.3 %collective-permute-start.24 = (bf16[320,1024]{1,0:T(8,128)(2,1)S(1)}, bf16[320,1024]{1,0:T(8,128)(2,1)S(1)}, u32[]{:S(2)}, u32[]{:S(2)}) collective-permute-start(bf16[320,1024]{1,0:T(8,128)(2,1)S(1)} %get-tuple-element.558), channel_id=1, source_target_pairs={{0,48},{4,52},{8,56},{12,60},{16,32},{20,36},{24,40},{28,44},{32,1... | collective-permute-start | bytes 1966088 | tf_op jit(solution)/shard_map/ppermute | solution.py:32
  120.5 16.3 %collective-permute-start.26 = (bf16[2,128,1280]{2,1,0:T(8,128)(2,1)S(1)}, bf16[2,128,1280]{2,1,0:T(8,128)(2,1)S(1)}, u32[]{:S(2)}, u32[]{:S(2)}) collective-permute-start(bf16[2,128,1280]{2,1,0:T(8,128)(2,1)S(1)} %get-tuple-element.563), channel_id=1, source_target_pairs={{0,1},{1,2},{2,3},{3,0},{4,5},{5,6},{6,7},{7,4},{8,9},{9,10},{10,1... | collective-permute-start | bytes 1966088 | tf_op jit(solution)/shard_map/ppermute | solution.py:32
  120.6 16.2 %collective-permute-start.27 = (bf16[2,128,1280]{2,1,0:T(8,128)(2,1)S(1)}, bf16[2,128,1280]{2,1,0:T(8,128)(2,1)S(1)}, u32[]{:S(2)}, u32[]{:S(2)}) collective-permute-start(bf16[2,128,1280]{2,1,0:T(8,128)(2,1)S(1)} %get-tuple-element.565), channel_id=1, source_target_pairs={{0,3},{1,0},{2,1},{3,2},{4,7},{5,4},{6,5},{7,6},{8,11},{9,8},{10,9... | collective-permute-start | bytes 1966088 | tf_op jit(solution)/shard_map/ppermute | solution.py:32
  123.2 14.5 %collective-permute-start.25 = (bf16[640,512]{1,0:T(8,128)(2,1)S(1)}, bf16[640,512]{1,0:T(8,128)(2,1)S(1)}, u32[]{:S(2)}, u32[]{:S(2)}) collective-permute-start(bf16[640,512]{1,0:T(8,128)(2,1)S(1)} %shard_map.87.refs_0_.refs_2_), channel_id=1, source_target_pairs={{0,8},{4,12},{8,0},{12,4},{16,24},{20,28},{24,16},{28,20},{32,40},... | collective-permute-start | bytes 1966088 | tf_op jit(solution)/shard_map/ppermute | solution.py:32
  138.5 17.4 %collective-permute-start.28 = (bf16[640,1024]{1,0:T(8,128)(2,1)S(1)}, bf16[640,1024]{1,0:T(8,128)(2,1)S(1)}, u32[]{:S(2)}, u32[]{:S(2)}) collective-permute-start(bf16[640,1024]{1,0:T(8,128)(2,1)S(1)} %get-tuple-element.629.refs_0_), channel_id=1, source_target_pairs={{0,4},{4,0},{8,12},{12,8},{16,20},{20,16},{24,28},{28,24},{32,36},... | collective-permute-start | bytes 3932168 | tf_op jit(solution)/shard_map/ppermute | solution.py:32
  141.3 14.7 %collective-permute-start.32 = (bf16[320,1024]{1,0:T(8,128)(2,1)S(1)}, bf16[320,1024]{1,0:T(8,128)(2,1)S(1)}, u32[]{:S(2)}, u32[]{:S(2)}) collective-permute-start(bf16[320,1024]{1,0:T(8,128)(2,1)S(1)} %collective-permute-done.23.refs_2_), channel_id=1, source_target_pairs={{0,4},{4,0},{8,12},{12,8},{16,20},{20,16},{24,28},{28,24},{32,36},... | collective-permute-start | bytes 1966088 | tf_op jit(solution)/shard_map/ppermute | solution.py:32
  141.3 14.6 %collective-permute-start.29 = (bf16[128,2048]{1,0:T(8,128)(2,1)S(1)}, bf16[128,2048]{1,0:T(8,128)(2,1)S(1)}, u32[]{:S(2)}, u32[]{:S(2)}) collective-permute-start(bf16[128,2048]{1,0:T(8,128)(2,1)S(1)} %get-tuple-element.586), channel_id=1, source_target_pairs={{0,64},{64,0},{1,65},{65,1},{2,66},{66,2},{3,67},{67,3},{4,68},{68... | collective-permute-start | bytes 1572872 | tf_op jit(solution)/shard_map/ppermute | solution.py:32
  158.4 15.9 %collective-permute-start.34 = (bf16[320,1024]{1,0:T(8,128)(2,1)S(1)}, bf16[320,1024]{1,0:T(8,128)(2,1)S(1)}, u32[]{:S(2)}, u32[]{:S(2)}) collective-permute-start(bf16[320,1024]{1,0:T(8,128)(2,1)S(1)} %get-tuple-element.623), channel_id=1, source_target_pairs={{0,16},{4,20},{8,24},{12,28},{16,0},{20,4},{24,8},{28,12},{32,48},... | collective-permute-start | bytes 1966088 | tf_op jit(solution)/shard_map/ppermute | solution.py:32
  159.2 16.8 %collective-permute-start.35 = (bf16[320,1024]{1,0:T(8,128)(2,1)S(1)}, bf16[320,1024]{1,0:T(8,128)(2,1)S(1)}, u32[]{:S(2)}, u32[]{:S(2)}) collective-permute-start(bf16[320,1024]{1,0:T(8,128)(2,1)S(1)} %get-tuple-element.624), channel_id=1, source_target_pairs={{0,48},{4,52},{8,56},{12,60},{16,32},{20,36},{24,40},{28,44},{32,1... | collective-permute-start | bytes 1966088 | tf_op jit(solution)/shard_map/ppermute | solution.py:32
  160.3 14.0 %collective-permute-start.33 = (bf16[128,2048]{1,0:T(8,128)(2,1)S(1)}, bf16[128,2048]{1,0:T(8,128)(2,1)S(1)}, u32[]{:S(2)}, u32[]{:S(2)}) collective-permute-start(bf16[128,2048]{1,0:T(8,128)(2,1)S(1)} %get-tuple-element.620), channel_id=1, source_target_pairs={{0,64},{64,0},{1,65},{65,1},{2,66},{66,2},{3,67},{67,3},{4,68},{68... | collective-permute-start | bytes 1572872 | tf_op jit(solution)/shard_map/ppermute | solution.py:32
  (27 other events, 245.4 us)

commit v3 on v0

v3 whole, which is shorter than its diff:
```python
import jax
import jax.numpy as jnp
from jax import lax
from jax.experimental import pallas as pl
from jax.experimental.pallas import tpu as pltpu
from jax.sharding import PartitionSpec as P

F32 = jnp.float32
BF16 = jnp.bfloat16
VMEM_LIMIT = 20 * 1024 * 1024

ROW_CHUNKS = ((0, 640), (640, 640))


def dp_pairs(fy=lambda y: y, fz=lambda z: z, fc=lambda c: c):
    return [(i, fy(i // 4) * 4 + fz(i // 2 % 2) * 2 + fc(i % 2)) for i in range(16)]


Y1 = dp_pairs(fy=lambda y: y ^ 1)
Y3 = dp_pairs(fy=lambda y: y ^ 3)
ZLO = dp_pairs(fz=lambda z: z ^ 1)
CORE = dp_pairs(fc=lambda c: c ^ 1)
SECTION = [(0, 1), (1, 0)]
AROUND, SLOT_OF, SLOTS = 1, 5, 9


def shift(step):
    return [(i, (i + step) % 4) for i in range(4)]


def swap(value, pairs, axis="dp"):
    return lax.ppermute(value, axis, pairs)


ANY = pl.BlockSpec(memory_space=pl.ANY)
VMEM = pl.BlockSpec(memory_space=pltpu.VMEM)
SMEM = pl.BlockSpec(memory_space=pltpu.SMEM)


class Copies:
    def __init__(self, sems):
        self.sems, self.all = sems, []

    def start(self, *pairs):
        copies = []
        for source, target in pairs:
            copies.append(pltpu.make_async_copy(source, target, self.sems.at[len(self.all)]))
            copies[-1].start()
            self.all.append(copies[-1])
        return copies


def wait(*groups):
    for group in groups:
        for copy in group:
            copy.wait()


def call(kernel, operands, in_specs, out_shapes, out_specs, scratch=(), aliases=None):
    return pl.pallas_call(
        kernel,
        in_specs=in_specs,
        out_specs=out_specs,
        out_shape=out_shapes,
        scratch_shapes=scratch,
        input_output_aliases=aliases or {},
        compiler_params=pltpu.CompilerParams(vmem_limit_bytes=VMEM_LIMIT),
        cost_estimate=pl.CostEstimate(flops=1, bytes_accessed=1, transcendentals=0),
    )(*operands)


def prepare(features, cotangent, gain, bias):
    _, rows, width = features.shape
    _, tokens, cols = cotangent.shape
    part = cols // 4

    def kernel(features, cotangent, gain, bias, ours_out, theirs_out, mine_out, scale_out, index_out, sems):
        s, d, x = lax.axis_index("section"), lax.axis_index("dp"), lax.axis_index("tensor")
        y, c = d // 4, d % 2
        around = (y, y + 1 - 2 * (y % 2), (y + 2) % 4, 3 - y)
        copies = Copies(sems)
        copies.start((features.at[c], ours_out), (features.at[1 - c], theirs_out))
        for n, j in enumerate(around):
            at = pl.ds(pl.multiple_of(j * part, part), part)
            copies.start((cotangent.at[0, :, at], mine_out.at[:, n * part : (n + 1) * part]))
        index_out[0] = c
        for n, j in enumerate(around):
            index_out[AROUND + n] = j
        for t in range(4):
            index_out[SLOT_OF + t] = (s if t < 2 else 1 - s) * 2 + t % 2
        for n, t in enumerate((x, (x + 1) % 4, (x + 3) % 4, (x + 2) % 4)):
            index_out[SLOTS + n] = ((t // 2 + s) % 2) * 2 + t % 2
        scale_out[0:1] = gain[pl.ds(c, 1)]
        scale_out[1:2] = bias[pl.ds(c, 1)]
        wait(copies.all)

    return call(
        kernel,
        [features, cotangent, gain, bias],
        [ANY, ANY, VMEM, VMEM],
        [out(rows, width), out(rows, width), out(tokens, cols), out(2, width, dtype=F32), out(13, dtype=jnp.int32)],
        [VMEM, VMEM, VMEM, VMEM, SMEM],
        [pltpu.SemaphoreType.DMA((6,))],
    )


def sums(*wanted, stack=False):
    arrays = []
    for terms in wanted:
        for array, _ in terms:
            if not any(array is a for a in arrays):
                arrays.append(array)
    places = [[(next(k for k, a in enumerate(arrays) if a is array), at) for array, at in terms] for terms in wanted]
    shapes = [out(*jax.eval_shape(lambda a, at=terms[0][1]: a[at], terms[0][0]).shape) for terms in wanted]
    made = [out(sum(s.shape[0] for s in shapes), *shapes[0].shape[1:])] if stack else shapes
    ends = [sum(s.shape[0] for s in shapes[: n + 1]) for n in range(len(shapes))]

    def kernel(*refs):
        ins, outs = refs[: len(arrays)], refs[len(arrays) :]
        for n, terms in enumerate(places):
            total = None
            for k, at in terms:
                value = ins[k][at].astype(F32)
                total = value if total is None else total + value
            if stack:
                outs[0][ends[n] - shapes[n].shape[0] : ends[n]] = total.astype(BF16)
            else:
                outs[n][...] = total.astype(BF16)

    return call(kernel, arrays, [VMEM] * len(arrays), made, [VMEM] * len(made))


def out(*shape, dtype=BF16):
    return jax.ShapeDtypeStruct(shape, dtype)


def dot(a, b, contract=(1, 0)):
    return lax.dot_general(a, b, (((contract[0],), (contract[1],)), ((), ())), preferred_element_type=F32)


def moments(value):
    mean = jnp.mean(value, axis=-1, keepdims=True)
    centered = value - mean
    inverse = 1.0 / jnp.sqrt(jnp.mean(centered * centered, axis=-1, keepdims=True) + 1e-05)
    return centered * inverse, inverse


def normalize(ours, theirs, scale):
    rows = ours.shape[0]

    def kernel(ours, theirs, scale, *outs):
        gain, bias = scale[0:1], scale[1:2]
        for k, value in enumerate((ours, theirs)):
            standard, _ = moments(value[...].astype(F32))
            normed = (standard * gain + bias).astype(BF16)
            for (start, size), out_ref in zip(ROW_CHUNKS, outs):
                out_ref[k] = normed[:, start : start + size]

    shapes = [out(2, rows, size) for _, size in ROW_CHUNKS]
    return call(kernel, [ours, theirs, scale], [VMEM] * 3, shapes, [VMEM] * len(shapes))


def normalize_backward(ours, theirs, scale, parts):
    count = len(parts)

    def kernel(ours, theirs, scale, *refs):
        gain = scale[0:1]
        for k, value in enumerate((ours, theirs)):
            standard, inverse = moments(value[...].astype(F32))
            total = refs[0][k].astype(F32)
            for ref in refs[1:count]:
                total = total + ref[k].astype(F32)
            scaled = total * gain
            hidden = inverse * (
                scaled
                - jnp.mean(scaled, axis=-1, keepdims=True)
                - standard * jnp.mean(scaled * standard, axis=-1, keepdims=True)
            )
            refs[count + k][...] = hidden.astype(BF16)

    shapes = [out(*ours.shape)] * 2
    return call(kernel, [ours, theirs, scale, *parts], [VMEM] * (3 + count), shapes, [VMEM] * 2)


def both_taps(index, ours, theirs):
    def kernel(index, ours, theirs, result, sems):
        copies = Copies(sems)
        copies.start((ours, result.at[index[0]]), (theirs, result.at[1 - index[0]]))
        wait(copies.all)

    shape = out(2, *ours.shape)
    return call(
        kernel, [index, ours, theirs], [SMEM, VMEM, VMEM], [shape], [ANY], [pltpu.SemaphoreType.DMA((2,))]
    )[0]


def weight_grad_blocks(index, normed, grads, wanted):
    rows = normed[0].shape[-1]
    half = rows // 2
    part = grads[0].shape[1] // 4
    shapes = [out(half, blocks * part) for _, _, blocks in wanted]

    def kernel(index, *refs):
        ins, gs, outs, turned = refs[:4], refs[4:8], refs[8:-1], refs[-1]
        for t in range(4):
            for k in range(2):
                at = pl.multiple_of((4 * k + index[SLOTS + t]) * 128, 128)
                turned[:, pl.ds(at, 128)] = ins[t][k].T
        for (h, first, blocks), out_ref in zip(wanted, outs):
            mine = turned[h * half : (h + 1) * half]
            total = None
            for p in range(4):
                term = dot(mine[:, 256 * p : 256 * (p + 1)], gs[p][:, first * part : (first + blocks) * part])
                total = term if total is None else total + term
            out_ref[...] = total.astype(BF16)

    return call(
        kernel,
        [index, *normed, *grads],
        [SMEM] + [VMEM] * 8,
        shapes,
        [VMEM] * len(shapes),
        [pltpu.VMEM((rows, 1024), BF16)],
    )


def take_tap(index, proj_weight):
    width, cols = proj_weight.shape[0] // 2, proj_weight.shape[1]
    step = width // 8

    def kernel(index, weight, result, sems):
        copies = Copies(sems)
        for n in range(8):
            rows = pl.ds(pl.multiple_of(index[0] * width + n * step, step), step)
            copies.start((weight.at[rows], result.at[n * step : (n + 1) * step]))
        wait(copies.all)

    return call(
        kernel,
        [index, proj_weight],
        [SMEM, ANY],
        [out(width, cols)],
        [VMEM],
        [pltpu.SemaphoreType.DMA((8,))],
    )[0]


def row_gradients(index, grads, weight):
    width, cols = weight.shape
    part = cols // 4
    tile = 256

    def kernel(index, *refs):
        gs, w, outs, held, acc = refs[:4], refs[4], refs[5:9], refs[9], refs[10]
        for j in range(4):
            at = pl.multiple_of(index[AROUND + j] * part, part)
            for n in range(4):
                held[256 * n : 256 * (n + 1), pl.ds(at, part)] = gs[n][:, j * part : (j + 1) * part]
        for i in range(width // tile):
            here = slice(i * tile, (i + 1) * tile)
            acc[:, here] = dot(held[...], w[here], (1, 1)).astype(BF16)
        for t in range(4):
            for k in range(2):
                at = pl.multiple_of((4 * k + index[SLOTS + t]) * 128, 128)
                outs[t][k] = acc[pl.ds(at, 128)]

    return call(
        kernel,
        [index, *grads, weight],
        [SMEM] + [VMEM] * 5,
        [out(2, 128, width)] * 4,
        [VMEM] * 4,
        [pltpu.VMEM((1024, cols), BF16), pltpu.VMEM((1024, width), BF16)],
    )


def project(index, chunks, weight):
    width, cols = weight.shape
    part = cols // 4
    flat = [piece for chunk in chunks for piece in chunk]
    count = len(flat)

    def kernel(index, *refs):
        ins, w, own, other, held = refs[:count], refs[count], refs[count + 1], refs[count + 2], refs[count + 3]
        for m, (first, size) in enumerate(ROW_CHUNKS):
            for t in range(4):
                for k in range(2):
                    at = pl.multiple_of((4 * k + index[SLOTS + t]) * 128, 128)
                    held[pl.ds(at, 128), first : first + size] = ins[4 * m + t][k]
        for i in range(4):
            here = slice(i * part, (i + 1) * part)
            other[:, here] = dot(held[512:], w[:, here]).astype(BF16)
            own[:, here] = dot(held[:512], w[:, here]).astype(BF16)

    return call(
        kernel,
        [index, *flat, weight],
        [SMEM] + [VMEM] * (count + 1),
        [out(512, cols)] * 2,
        [VMEM] * 2,
        [pltpu.VMEM((1024, width), BF16)],
    )


EVERY = slice(None)


def add_first(next_a, next_b, got_a, got_b):
    part = next_a.shape[1]
    left, right = (EVERY, slice(0, part)), (EVERY, slice(part, 2 * part))
    return sums([(next_a, (EVERY, EVERY)), (got_a, right)], [(next_b, (EVERY, EVERY)), (got_b, left)])


def add_second(keep_a, keep_b, got_a, got_b, more_a, more_b):
    part = keep_a.shape[1]
    whole, left, right = (EVERY, EVERY), (EVERY, slice(0, part)), (EVERY, slice(part, 2 * part))
    return sums(
        [(keep_a, whole), (got_a, left), (more_a, whole)],
        [(keep_b, whole), (got_b, right), (more_b, whole)],
        stack=True,
    )[0]


def add_third(keep, other):
    half = keep.shape[0] // 2
    top, bottom = (slice(0, half), EVERY), (slice(half, 2 * half), EVERY)
    return sums([(keep, top), (other, top)], [(keep, bottom), (other, bottom)])


def join(left_a, left_b, right_a, right_b):
    half, part = left_a.shape

    def kernel(left_a, left_b, right_a, right_b, out_a, out_b, both):
        for n, (left, right, single) in enumerate(((left_a, right_a, out_a), (left_b, right_b, out_b))):
            rows = slice(n * half, (n + 1) * half)
            for source, here in ((left, slice(0, part)), (right, slice(part, 2 * part))):
                value = source[...]
                single[:, here] = value
                both[rows, here] = value

    return call(
        kernel,
        [left_a, left_b, right_a, right_b],
        [VMEM] * 4,
        [out(half, 2 * part), out(half, 2 * part), out(2 * half, 2 * part)],
        [VMEM] * 3,
    )


def below(top, bottom):
    rows = top.shape[0]

    def kernel(top, bottom, both):
        both[:rows] = top[...]
        both[rows:] = bottom[...]

    return call(kernel, [top, bottom], [VMEM] * 2, [out(2 * rows, top.shape[1])], [VMEM])[0]


def place(index, pieces, start, width, cols, into):
    part = cols // 4
    half = next(size for first, size in ROW_CHUNKS if first == start) // 2
    arrays = []
    for piece in pieces:
        if not any(piece[0] is a for a in arrays):
            arrays.append(piece[0])
    which = [next(k for k, a in enumerate(arrays) if a is piece[0]) for piece in pieces]
    count = len(arrays)

    def kernel(index, *refs):
        sources, result, sems = refs[:count], refs[-2], refs[-1]
        copies = Copies(sems)
        for k, (_, row, other, h, js) in zip(which, pieces):
            tap = 1 - index[0] if other else index[0]
            rows = pl.ds(pl.multiple_of(tap * width + start + h * half, 64), half)
            for n, j in enumerate(js):
                at = pl.ds(pl.multiple_of(index[AROUND + j] * part, part), part)
                copies.start((sources[k].at[row : row + half, n * part : (n + 1) * part], result.at[rows, at]))
        wait(copies.all)

    operands = [index, *arrays] + ([] if into is None else [into])
    return call(
        kernel,
        operands,
        [SMEM] + [VMEM] * count + ([] if into is None else [ANY]),
        [out(2 * width, cols)],
        [ANY],
        [pltpu.SemaphoreType.DMA((2 * len(pieces),))],
        {} if into is None else {count + 1: 0},
    )[0]


class Phases:
    def __init__(self):
        self.here, self.away = {}, {}

    def __getitem__(self, name):
        return self.here[name]

    def __setitem__(self, name, value):
        self.here[name] = value

    def send(self, name, source, pairs, axis="dp"):
        self.away[name] = swap(self.here[source], pairs, axis)

    def land(self, *names):
        for name in names:
            self.here[name] = self.away.pop(name)

    def end(self, *drop):
        for name in drop:
            del self.here[name]
        self.here = lax.optimization_barrier(self.here)


def body(features, layer_norm_gain, layer_norm_bias, proj_weight, cotangent):
    width = layer_norm_gain.shape[1]
    cols = proj_weight.shape[1]
    half = ROW_CHUNKS[0][1] // 2
    wanted = ((0, 1, 2), (1, 2, 2), (0, 3, 1), (1, 1, 1), (0, 0, 1), (1, 0, 1))
    v = Phases()

    def near(n):
        return [v["n%d" % n], *(v["x%d%d" % (n, k)] for k in (1, 3, 2))]

    def grads():
        return [v["mine"], v["away"], v["mine_c"], v["away_c"]]

    def products(t):
        names = "send_a", "send_b", "next_a", "next_b", "keep_a", "keep_b"
        for name, value in zip(names, weight_grad_blocks(v["index"], near(t), grads(), wanted)):
            v[name + str(t)] = value

    def spread(t):
        v["a%d" % t], v["b%d" % t], v["ab%d" % t] = join(*(v[n + str(t)] for n in ("da", "db", "ga", "gb")))

    def finish(t, early, late):
        pieces = []
        for arrays, places in ((early, ((0, 3), (0, 1))), (late, ((1, 2), (3, 2)))):
            for n, array in enumerate(arrays):
                if len(arrays) == 2:
                    pieces += [(array, h * half, n == 1, h, places[h]) for h in range(2)]
                else:
                    pieces.append((array, 0, n > 1, n % 2, places[n % 2]))
        v["weight_grad"] = place(v["index"], pieces, ROW_CHUNKS[t][0], width, cols, v.here.get("weight_grad"))

    v["ours"], v["theirs"], v["mine"], v["scale"], v["index"] = prepare(
        features, cotangent, layer_norm_gain, layer_norm_bias
    )
    v.end()

    v.send("away", "mine", SECTION, "section")
    v.send("rows", "theirs", CORE)
    v.send("mine_c", "mine", CORE)
    v.land("rows")
    v["n0"], v["n1"] = normalize(v["ours"], v["rows"], v["scale"])
    v.land("mine_c")
    v.end("theirs")

    for k in (1, 3, 2):
        v.send("x0%d" % k, "n0", shift(-k), "tensor")
    v["weight"] = take_tap(v["index"], proj_weight)
    v.land("x01", "x03", "x02", "away")
    v.end()

    v.send("away_c", "away", CORE)
    v.send("x11", "n1", shift(-1), "tensor")
    v.send("x13", "n1", shift(-3), "tensor")
    v.land("away_c")
    v.end()

    products(0)
    v.land("x11", "x13")
    v.end()

    v.send("got_a0", "send_a0", Y1)
    v.send("got_b0", "send_b0", Y3)
    v.send("x12", "n1", shift(-2), "tensor")
    for k, part in zip((0, 1, 3, 2), row_gradients(v["index"], grads(), v["weight"])):
        v["r%d" % k] = part
    v.land("got_a0", "got_b0", "x12")
    v.end("send_a0", "send_b0")

    v["n_a0"], v["n_b0"] = add_first(v["next_a0"], v["next_b0"], v["got_a0"], v["got_b0"])
    v.end("next_a0", "next_b0")

    v.send("more_a0", "n_a0", Y3)
    v.send("more_b0", "n_b0", Y1)
    products(1)
    v.land("more_a0", "more_b0")
    v.end("n_a0", "n_b0", "mine", "away", "mine_c", "away_c")

    v["keep0"] = add_second(*(v[n + "0"] for n in ("keep_a", "keep_b", "got_a", "got_b", "more_a", "more_b")))
    v.end("keep_a0", "keep_b0", "got_a0", "got_b0", "more_a0", "more_b0")

    v.send("got_a1", "send_a1", Y1)
    v.send("got_b1", "send_b1", Y3)
    v.send("other0", "keep0", ZLO)
    v.send("s2", "r2", shift(2), "tensor")
    v["own"], v["other"] = project(v["index"], [near(0), near(1)], v["weight"])
    v.land("got_a1", "got_b1", "other0", "s2")
    v.end("r2", "send_a1", "send_b1", "x01", "x03", "x02", "x11", "x13", "x12", "n0", "n1")

    v["n_a1"], v["n_b1"] = add_first(v["next_a1"], v["next_b1"], v["got_a1"], v["got_b1"])
    v["da0"], v["db0"] = add_third(v["keep0"], v["other0"])
    v.end("next_a1", "next_b1", "keep0", "other0")

    v.send("more_a1", "n_a1", Y3)
    v.send("more_b1", "n_b1", Y1)
    v.send("ga0", "da0", Y3)
    v.send("gb0", "db0", Y1)
    v.send("other_c", "other", CORE)
    v.land("more_a1", "more_b1", "ga0", "gb0", "other_c")
    v.end("n_a1", "n_b1", "other")

    v["keep1"] = add_second(*(v[n + "1"] for n in ("keep_a", "keep_b", "got_a", "got_b", "more_a", "more_b")))
    spread(0)
    v.end("keep_a1", "keep_b1", "got_a1", "got_b1", "more_a1", "more_b1", "da0", "db0", "ga0", "gb0")

    v.send("other1", "keep1", ZLO)
    v.send("la0", "a0", Y1)
    v.send("lb0", "b0", Y3)
    v.send("s1", "r1", shift(1), "tensor")
    v.send("s3", "r3", shift(3), "tensor")
    rows = [slice(0, 112), slice(112, 256), slice(256, 368), slice(368, 512)]
    v["up0"], v["up1"] = sums(*([(v["own"], (r, EVERY)), (v["other_c"], (r, EVERY))] for r in rows[2:]))
    v.land("other1", "la0", "lb0")
    v.end("a0", "b0", "r1", "r3")

    v["da1"], v["db1"] = add_third(v["keep1"], v["other1"])
    v["lab0"] = below(v["la0"], v["lb0"])
    v.land("s1", "s3")
    v.end("keep1", "other1", "la0", "lb0")

    v.send("ga1", "da1", Y3)
    v.send("gb1", "db1", Y1)
    v.send("back0", "up0", SECTION, "section")
    v.send("ab0_c", "ab0", CORE)
    v.send("lab0_c", "lab0", CORE)
    v["own_rows"], v["hidden"] = normalize_backward(
        v["ours"], v["rows"], v["scale"], [v["r0"], v["s1"], v["s3"], v["s2"]]
    )
    v.land("ga1", "gb1", "ab0_c", "lab0_c", "back0")
    v.end("up0", "r0", "s1", "s3", "s2")

    spread(1)
    v.end("da1", "db1", "ga1", "gb1")

    v.send("la1", "a1", Y1)
    v.send("lb1", "b1", Y3)
    v.send("ab1_c", "ab1", CORE)
    v.send("hidden_c", "hidden", CORE)
    v.send("back1", "up1", SECTION, "section")
    finish(0, [v["ab0"], v["ab0_c"]], [v["lab0"], v["lab0_c"]])
    v.land("ab1_c", "hidden_c")
    finish(1, [v["ab1"], v["ab1_c"]], [])
    v["result"] = both_taps(v["index"], v["own_rows"], v["hidden_c"])
    v.land("la1", "lb1", "back1")
    v.end("a1", "b1", "ab0", "ab0_c", "ab1", "ab1_c", "lab0", "lab0_c", "own_rows", "hidden", "hidden_c", "up1")

    v.send("la1_c", "la1", CORE)
    v.send("lb1_c", "lb1", CORE)
    projected = sums(
        *(
            [(v["own"], (r, EVERY)), (v["other_c"], (r, EVERY)), (v[back], (EVERY, EVERY))]
            for r, back in zip(rows, ("back0", "back1"))
        ),
        stack=True,
    )[0]
    v.land("la1_c", "lb1_c")
    finish(1, [], [v["la1"], v["lb1"], v["la1_c"], v["lb1_c"]])
    return (projected[None], v["weight_grad"], v["result"])


def solution(mesh):
    return jax.shard_map(
        body,
        mesh=mesh,
        in_specs=(
            P("section", ("dp", "tensor"), None),
            P("section", None),
            P("section", None),
            P("section", "tensor"),
            P("dp", "section", "tensor"),
        ),
        out_specs=(
            P("dp", "section", "tensor"),
            P("section", "tensor"),
            P("section", ("dp", "tensor"), None),
        ),
        check_vma=False,
    )
```

time: 436 us -> 171 us (0.39)
  waiting for transfers between devices: 374 us -> 70.3 us
  starting transfers between devices: 0.2 us -> 54.5 us
  Pallas kernels: 0 us -> 37.5 us
  matrix products: 31.3 us -> 0 us
  between operations: 13.8 us -> 1.03 us
  other arithmetic: 4.75 us -> 0 us
    psum x1 -> x0, waiting for transfers between devices: 238 us -> none  [body(): summed = lax.psum(partial_value.astype(jnp.bfloat16), 'dp')]
    all_gather x2 -> x0, waiting for transfers between devices: 77.2 us -> none  [the longest x1 42.3 us: body(): grads = lax.all_gather(cotangent, 'section', axis=1, tiled=True)[0]]
    ppermute x0 -> x40, waiting for transfers between devices: none -> 70.3 us  [swap(): return lax.ppermute(value, axis, pairs)]
    reduce_scatter x2 -> x0, waiting for transfers between devices: 58 us -> none  [the longest x1 31.8 us: body(): lax.psum_scatter(jnp.einsum('ro,lco->rlc', rows, weight, preferred_elemen...]
    ppermute x0 -> x40, starting transfers between devices: none -> 54.5 us  [swap(): return lax.ppermute(value, axis, pairs)]
    pallas_call x0 -> x23, Pallas kernels: none -> 37.5 us  [call(): pl.pallas_call(kernel, in_specs=in_specs, out_specs=out_specs, out_shape=...]
    dot_general x3 -> x0, matrix products: 31.3 us -> none  [the longest x1 11.3 us: body(): jnp.einsum('lrc,lco->ro', rows, weight, preferred_element_type=jnp.float32)]
    unnamed x9 -> x10, local copies, waits for them, and re-layouts: 11.3 us -> 7.69 us
  transfers between devices with their start and end apart: 5 -> 40, of which waited for: 5 -> 22; matrix products, arithmetic and copies ran while one was open for 2% -> 0% of each run, Pallas kernels for 0% -> 19%
where the time goes in v3:
time: 171 us
  waiting for transfers between devices  70.3 us (41%)
  starting transfers between devices  54.5 us (32%)
  Pallas kernels  37.5 us (22%)
  local copies, waits for them, and re-layouts  7.69 us (4%)
    ppermute x40, waiting for transfers between devices, swap(): return lax.ppermute(value, axis, pairs)  70.3 us
    ppermute x40, starting transfers between devices, swap(): return lax.ppermute(value, axis, pairs)  54.5 us
    pallas_call x23, Pallas kernels, call(): pl.pallas_call(kernel, in_specs=in_specs, out_specs=out_specs, out_shape=...  37.5 us
    unnamed x10, local copies, waits for them, and re-layouts  7.69 us
  transfers between devices with their start and end apart: 40, of which 22 were waited for; matrix products, arithmetic and copies ran while one was open for 0% of the time, Pallas kernels for 19%

profile of v3, /device:TPU:1, one launch (start us, length us, event | category | flops | bytes accessed | tf_op | source)
XLA Modules:
  0.0 171.0 jit_solution(6839683276895376474)
XLA Ops:
  6.9 3.7 %collective-permute-start = (bf16[256,2048]{1,0:T(8,128)(2,1)S(1)}, bf16[256,2048]{1,0:T(8,128)(2,1)S(1)}, u32[]{:S(2)}, u32[]{:S(2)}) collective-permute-start(bf16[256,2048]{1,0:T(8,128)(2,1)S(1)} %get-tuple-element.470.refs_4_.refs_0_), channel_id=1, source_target_pairs={{0,64},{64,0},{1,65},{65,1},{2,66},{66,2},{3,67},{67,3},{4,68},{68... | collective-permute-start | bytes 3145736 | tf_op jit(solution)/shard_map/ppermute | solution.py:32
  14.0 2.5 %collective-permute-start.4 = (bf16[2,128,640]{2,1,0:T(8,128)(2,1)S(1)}, bf16[2,128,640]{2,1,0:T(8,128)(2,1)S(1)}, u32[]{:S(2)}, u32[]{:S(2)}) collective-permute-start(bf16[2,128,640]{2,1,0:T(8,128)(2,1)S(1)} %get-tuple-element.532.refs_0_), channel_id=1, source_target_pairs={{0,2},{1,3},{2,0},{3,1},{4,6},{5,7},{6,4},{7,5},{8,10},{9,11},{10,... | collective-permute-start | bytes 983048 | tf_op jit(solution)/shard_map/ppermute | solution.py:32
  17.6 4.0 %copy-done = bf16[2560,2048]{1,0:T(8,128)(2,1)S(1)} copy-done((bf16[2560,2048]{1,0:T(8,128)(2,1)S(1)}, bf16[2560,2048]{1,0:T(8,128)(2,1)}, u32[]{:S(2)}) %copy-start) | copy-done | bytes 10485784
  21.6 2.3 %shard_map.78.refs_4_.refs_8_ = bf16[1280,2048]{1,0:T(8,128)(2,1)S(1)} custom-call(s32[13]{0:T(128)S(1)} %get-tuple-element.700.index, bf16[2560,2048]{1,0:T(8,128)(2,1)S(1)} %copy-done), custom_call_target="tpu_custom_call" | custom-call | flops 1 | bytes 1 | tf_op jit(solution)/shard_map/pallas_call | solution.py:60
  23.9 10.1 %collective-permute-done.refs_5_.refs_1_ = bf16[256,2048]{1,0:T(8,128)(2,1)S(1)} collective-permute-done((bf16[256,2048]{1,0:T(8,128)(2,1)S(1)}, bf16[256,2048]{1,0:T(8,128)(2,1)S(1)}, u32[]{:S(2)}, u32[]{:S(2)}) %collective-permute-start) | collective-permute-done | bytes 1048608 | tf_op jit(solution)/shard_map/ppermute | solution.py:32
  37.4 3.9 %shard_map.79 = (bf16[320,1024]{1,0:T(8,128)(2,1)S(1)}, bf16[320,1024]{1,0:T(8,128)(2,1)S(1)}, bf16[320,512]{1,0:T(8,128)(2,1)S(1)}, bf16[320,512]{1,0:T(8,128)(...) custom-call(s32[13]{0:T(128)S(1)} %get-tuple-element.700.index, ...), custom_call_target="tpu_custom_call" | custom-call | flops 1 | bytes 1 | tf_op jit(solution)/shard_map/pallas_call | solution.py:60
  41.3 3.9 %collective-permute-done.8.refs_2_.refs_6_ = bf16[2,128,640]{2,1,0:T(8,128)(2,1)S(1)} collective-permute-done((bf16[2,128,640]{2,1,0:T(8,128)(2,1)S(1)}, bf16[2,128,640]{2,1,0:T(8,128)(2,1)S(1)}, u32[]{:S(2)}, u32[]{:S(2)}) %collective-permute-start.8) | collective-permute-done | bytes 327712 | tf_op jit(solution)/shard_map/ppermute | solution.py:32
  50.5 6.8 %shard_map.80 = (bf16[2,128,1280]{2,1,0:T(8,128)(2,1)S(1)}, bf16[2,128,1280]{2,1,0:T(8,128)(2,1)S(1)}, bf16[2,128,1280]{2,1,0:T(8,128)(2,1)S(1)}, bf16[2,128,1280]{2,1,0:T(8,128)(2,1)S(1)}) custom-call(s32[13]{0:T(128)S(1)} %get-tuple-element.700.index, bf16[256,2048]{1,0:T(8,128)(2,1)S(1)} %get-tuple-element.470.refs_4_.refs_0_, ...), custom_call_target="tpu_custom_call" | custom-call | flops 1 | bytes 1 | tf_op jit(solution)/shard_map/pallas_call | solution.py:60
  57.7 2.9 %collective-permute-done.9.refs_1_ = bf16[320,1024]{1,0:T(8,128)(2,1)S(1)} collective-permute-done((bf16[320,1024]{1,0:T(8,128)(2,1)S(1)}, bf16[320,1024]{1,0:T(8,128)(2,1)S(1)}, u32[]{:S(2)}, u32[]{:S(2)}) %collective-permute-start.9) | collective-permute-done | bytes 655392 | tf_op jit(solution)/shard_map/ppermute | solution.py:32
  60.6 2.2 %collective-permute-done.10.refs_3_.refs_4_ = bf16[320,1024]{1,0:T(8,128)(2,1)S(1)} collective-permute-done((bf16[320,1024]{1,0:T(8,128)(2,1)S(1)}, bf16[320,1024]{1,0:T(8,128)(2,1)S(1)}, u32[]{:S(2)}, u32[]{:S(2)}) %collective-permute-start.10) | collective-permute-done | bytes 655392 | tf_op jit(solution)/shard_map/ppermute | solution.py:32
  65.0 3.9 %shard_map.82 = (bf16[320,1024]{1,0:T(8,128)(2,1)S(1)}, bf16[320,1024]{1,0:T(8,128)(2,1)S(1)}, bf16[320,512]{1,0:T(8,128)(2,1)S(1)}, bf16[320,512]{1,0:T(8,128)(...) custom-call(s32[13]{0:T(128)S(1)} %get-tuple-element.700.index, ...), custom_call_target="tpu_custom_call" | custom-call | flops 1 | bytes 1 | tf_op jit(solution)/shard_map/pallas_call | solution.py:60
  68.8 2.6 %collective-permute-done.12.refs_2_ = bf16[320,512]{1,0:T(8,128)(2,1)S(1)} collective-permute-done((bf16[320,512]{1,0:T(8,128)(2,1)S(1)}, bf16[320,512]{1,0:T(8,128)(2,1)S(1)}, u32[]{:S(2)}, u32[]{:S(2)}) %collective-permute-start.12) | collective-permute-done | bytes 327712 | tf_op jit(solution)/shard_map/ppermute | solution.py:32
  76.2 6.3 %shard_map.84 = (bf16[512,2048]{1,0:T(8,128)(2,1)S(1)}, bf16[512,2048]{1,0:T(8,128)(2,1)S(1)}) custom-call(s32[13]{0:T(128)S(1)} %get-tuple-element.700.index, bf16[2,128,640]{2,1,0:T(8,128)(2,1)S(1)} %get-tuple-element.532.refs_0_, bf16[2,128,640]{2,1,0:T(8,128)(2,1)S(1)} %collective-permute-done.3.refs_1_, ...), custom_call_target="tpu_custom_call" | custom-call | flops 1 | bytes 1 | tf_op jit(solution)/shard_map/pallas_call | solution.py:60
  82.6 2.5 %collective-permute-done.14.refs_1_ = bf16[320,1024]{1,0:T(8,128)(2,1)S(1)} collective-permute-done((bf16[320,1024]{1,0:T(8,128)(2,1)S(1)}, bf16[320,1024]{1,0:T(8,128)(2,1)S(1)}, u32[]{:S(2)}, u32[]{:S(2)}) %collective-permute-start.14) | collective-permute-done | bytes 655392 | tf_op jit(solution)/shard_map/ppermute | solution.py:32
  88.5 4.3 %collective-permute-start.22 = (bf16[512,2048]{1,0:T(8,128)(2,1)S(1)}, bf16[512,2048]{1,0:T(8,128)(2,1)S(1)}, u32[]{:S(2)}, u32[]{:S(2)}) collective-permute-start(bf16[512,2048]{1,0:T(8,128)(2,1)S(1)} %get-tuple-element.581), channel_id=1, source_target_pairs={{0,4},{4,0},{8,12},{12,8},{16,20},{20,16},{24,28},{28,24},{32,36},... | collective-permute-start | bytes 6291464 | tf_op jit(solution)/shard_map/ppermute | solution.py:32
  96.3 6.9 %collective-permute-done.20.refs_2_ = bf16[320,512]{1,0:T(8,128)(2,1)S(1)} collective-permute-done((bf16[320,512]{1,0:T(8,128)(2,1)S(1)}, bf16[320,512]{1,0:T(8,128)(2,1)S(1)}, u32[]{:S(2)}, u32[]{:S(2)}) %collective-permute-start.20) | collective-permute-done | bytes 327712 | tf_op jit(solution)/shard_map/ppermute | solution.py:32
  103.3 7.0 %collective-permute-done.18.right_a = bf16[320,512]{1,0:T(8,128)(2,1)S(1)} collective-permute-done((bf16[320,512]{1,0:T(8,128)(2,1)S(1)}, bf16[320,512]{1,0:T(8,128)(2,1)S(1)}, u32[]{:S(2)}, u32[]{:S(2)}) %collective-permute-start.18) | collective-permute-done | bytes 327712 | tf_op jit(solution)/shard_map/ppermute | solution.py:32
  116.2 9.8 %collective-permute-done.23.top = bf16[320,1024]{1,0:T(8,128)(2,1)S(1)} collective-permute-done((bf16[320,1024]{1,0:T(8,128)(2,1)S(1)}, bf16[320,1024]{1,0:T(8,128)(2,1)S(1)}, u32[]{:S(2)}, u32[]{:S(2)}) %collective-permute-start.23) | collective-permute-done | bytes 655392 | tf_op jit(solution)/shard_map/ppermute | solution.py:32
  128.9 2.8 %collective-permute-start.28 = (bf16[640,1024]{1,0:T(8,128)(2,1)S(1)}, bf16[640,1024]{1,0:T(8,128)(2,1)S(1)}, u32[]{:S(2)}, u32[]{:S(2)}) collective-permute-start(bf16[640,1024]{1,0:T(8,128)(2,1)S(1)} %get-tuple-element.692.refs_0_), channel_id=1, source_target_pairs={{0,4},{4,0},{8,12},{12,8},{16,20},{20,16},{24,28},{28,24},{32,36},... | collective-permute-start | bytes 3932168 | tf_op jit(solution)/shard_map/ppermute | solution.py:32
  131.7 3.3 %collective-permute-start.29 = (bf16[112,2048]{1,0:T(8,128)(2,1)S(1)}, bf16[112,2048]{1,0:T(8,128)(2,1)S(1)}, u32[]{:S(2)}, u32[]{:S(2)}) collective-permute-start(bf16[112,2048]{1,0:T(8,128)(2,1)S(1)} %get-tuple-element.647), channel_id=1, source_target_pairs={{0,64},{64,0},{1,65},{65,1},{2,66},{66,2},{3,67},{67,3},{4,68},{68... | collective-permute-start | bytes 1376264 | tf_op jit(solution)/shard_map/ppermute | solution.py:32
  137.5 7.1 %collective-permute-done.30.right_a = bf16[320,512]{1,0:T(8,128)(2,1)S(1)} collective-permute-done((bf16[320,512]{1,0:T(8,128)(2,1)S(1)}, bf16[320,512]{1,0:T(8,128)(2,1)S(1)}, u32[]{:S(2)}, u32[]{:S(2)}) %collective-permute-start.30) | collective-permute-done | bytes 327712 | tf_op jit(solution)/shard_map/ppermute | solution.py:32
  148.8 3.0 %collective-permute-start.33 = (bf16[144,2048]{1,0:T(8,128)(2,1)S(1)}, bf16[144,2048]{1,0:T(8,128)(2,1)S(1)}, u32[]{:S(2)}, u32[]{:S(2)}) collective-permute-start(bf16[144,2048]{1,0:T(8,128)(2,1)S(1)} %get-tuple-element.683), channel_id=1, source_target_pairs={{0,64},{64,0},{1,65},{65,1},{2,66},{66,2},{3,67},{67,3},{4,68},{68... | collective-permute-start | bytes 1769480 | tf_op jit(solution)/shard_map/ppermute | solution.py:32
  152.7 3.0 %shard_map.95.refs_2_ = bf16[2560,2048]{1,0:T(8,128)(2,1)} custom-call(s32[13]{0:T(128)S(1)} %get-tuple-element.700.index, bf16[640,1024]{1,0:T(8,128)(2,1)S(1)} %get-tuple-element.692.refs_0_, bf16[640,1024]{1,0:T(8,128)(2,1)S(1)} %collective-permute-done.28.refs_1_, bf16[640,1024]{1,0:T(8,128)(2,1)S(1)} %shard_map.91.refs_2_, ...), custom_call_target="tpu_custom_call" | custom-call | flops 1 | bytes 1 | tf_op jit(solution)/shard_map/pallas_call | solution.py:60
  159.2 5.3 %collective-permute-done.33.refs_3_ = bf16[144,2048]{1,0:T(8,128)(2,1)S(1)} collective-permute-done((bf16[144,2048]{1,0:T(8,128)(2,1)S(1)}, bf16[144,2048]{1,0:T(8,128)(2,1)S(1)}, u32[]{:S(2)}, u32[]{:S(2)}) %collective-permute-start.33) | collective-permute-done | bytes 589856 | tf_op jit(solution)/shard_map/ppermute | solution.py:32
  (89 shorter events, 60.0 us)
Async XLA Ops:
  6.9 27.1 %collective-permute-start = (bf16[256,2048]{1,0:T(8,128)(2,1)S(1)}, bf16[256,2048]{1,0:T(8,128)(2,1)S(1)}, u32[]{:S(2)}, u32[]{:S(2)}) collective-permute-start(bf16[256,2048]{1,0:T(8,128)(2,1)S(1)} %get-tuple-element.470.refs_4_.refs_0_), channel_id=1, source_target_pairs={{0,64},{64,0},{1,65},{65,1},{2,66},{66,2},{3,67},{67,3},{4,68},{68... | collective-permute-start | bytes 3145736 | tf_op jit(solution)/shard_map/ppermute | solution.py:32
  12.7 21.3 %collective-permute-start.5 = (bf16[2,128,640]{2,1,0:T(8,128)(2,1)S(1)}, bf16[2,128,640]{2,1,0:T(8,128)(2,1)S(1)}, u32[]{:S(2)}, u32[]{:S(2)}) collective-permute-start(bf16[2,128,640]{2,1,0:T(8,128)(2,1)S(1)} %get-tuple-element.532.refs_0_), channel_id=1, source_target_pairs={{0,1},{1,2},{2,3},{3,0},{4,5},{5,6},{6,7},{7,4},{8,9},{9,10},{10,1... | collective-permute-start | bytes 983048 | tf_op jit(solution)/shard_map/ppermute | solution.py:32
  14.0 20.0 %collective-permute-start.4 = (bf16[2,128,640]{2,1,0:T(8,128)(2,1)S(1)}, bf16[2,128,640]{2,1,0:T(8,128)(2,1)S(1)}, u32[]{:S(2)}, u32[]{:S(2)}) collective-permute-start(bf16[2,128,640]{2,1,0:T(8,128)(2,1)S(1)} %get-tuple-element.532.refs_0_), channel_id=1, source_target_pairs={{0,2},{1,3},{2,0},{3,1},{4,6},{5,7},{6,4},{7,5},{8,10},{9,11},{10,... | collective-permute-start | bytes 983048 | tf_op jit(solution)/shard_map/ppermute | solution.py:32
  16.4 17.6 %collective-permute-start.3 = (bf16[2,128,640]{2,1,0:T(8,128)(2,1)S(1)}, bf16[2,128,640]{2,1,0:T(8,128)(2,1)S(1)}, u32[]{:S(2)}, u32[]{:S(2)}) collective-permute-start(bf16[2,128,640]{2,1,0:T(8,128)(2,1)S(1)} %get-tuple-element.532.refs_0_), channel_id=1, source_target_pairs={{0,3},{1,0},{2,1},{3,2},{4,7},{5,4},{6,5},{7,6},{8,11},{9,8},{10,9... | collective-permute-start | bytes 983048 | tf_op jit(solution)/shard_map/ppermute | solution.py:32
  45.2 15.4 %collective-permute-start.9 = (bf16[320,1024]{1,0:T(8,128)(2,1)S(1)}, bf16[320,1024]{1,0:T(8,128)(2,1)S(1)}, u32[]{:S(2)}, u32[]{:S(2)}) collective-permute-start(bf16[320,1024]{1,0:T(8,128)(2,1)S(1)} %get-tuple-element.409), channel_id=1, source_target_pairs={{0,16},{4,20},{8,24},{12,28},{16,0},{20,4},{24,8},{28,12},{32,48},... | collective-permute-start | bytes 1966088 | tf_op jit(solution)/shard_map/ppermute | solution.py:32
  46.5 16.3 %collective-permute-start.10 = (bf16[320,1024]{1,0:T(8,128)(2,1)S(1)}, bf16[320,1024]{1,0:T(8,128)(2,1)S(1)}, u32[]{:S(2)}, u32[]{:S(2)}) collective-permute-start(bf16[320,1024]{1,0:T(8,128)(2,1)S(1)} %get-tuple-element.410), channel_id=1, source_target_pairs={{0,48},{4,52},{8,56},{12,60},{16,32},{20,36},{24,40},{28,44},{32,1... | collective-permute-start | bytes 1966088 | tf_op jit(solution)/shard_map/ppermute | solution.py:32
  72.1 13.0 %collective-permute-start.14 = (bf16[320,1024]{1,0:T(8,128)(2,1)S(1)}, bf16[320,1024]{1,0:T(8,128)(2,1)S(1)}, u32[]{:S(2)}, u32[]{:S(2)}) collective-permute-start(bf16[320,1024]{1,0:T(8,128)(2,1)S(1)} %get-tuple-element.524), channel_id=1, source_target_pairs={{0,16},{4,20},{8,24},{12,28},{16,0},{20,4},{24,8},{28,12},{32,48},... | collective-permute-start | bytes 1966088 | tf_op jit(solution)/shard_map/ppermute | solution.py:32
  72.4 14.2 %collective-permute-start.15 = (bf16[320,1024]{1,0:T(8,128)(2,1)S(1)}, bf16[320,1024]{1,0:T(8,128)(2,1)S(1)}, u32[]{:S(2)}, u32[]{:S(2)}) collective-permute-start(bf16[320,1024]{1,0:T(8,128)(2,1)S(1)} %get-tuple-element.525), channel_id=1, source_target_pairs={{0,48},{4,52},{8,56},{12,60},{16,32},{20,36},{24,40},{28,44},{32,1... | collective-permute-start | bytes 1966088 | tf_op jit(solution)/shard_map/ppermute | solution.py:32
  73.7 14.5 %collective-permute-start.17 = (bf16[2,128,1280]{2,1,0:T(8,128)(2,1)S(1)}, bf16[2,128,1280]{2,1,0:T(8,128)(2,1)S(1)}, u32[]{:S(2)}, u32[]{:S(2)}) collective-permute-start(bf16[2,128,1280]{2,1,0:T(8,128)(2,1)S(1)} %get-tuple-element.548), channel_id=1, source_target_pairs={{0,2},{1,3},{2,0},{3,1},{4,6},{5,7},{6,4},{7,5},{8,10},{9,11},{10,... | collective-permute-start | bytes 1966088 | tf_op jit(solution)/shard_map/ppermute | solution.py:32
  75.2 13.0 %collective-permute-start.16 = (bf16[640,512]{1,0:T(8,128)(2,1)S(1)}, bf16[640,512]{1,0:T(8,128)(2,1)S(1)}, u32[]{:S(2)}, u32[]{:S(2)}) collective-permute-start(bf16[640,512]{1,0:T(8,128)(2,1)S(1)} %shard_map.83.refs_0_), channel_id=1, source_target_pairs={{0,8},{4,12},{8,0},{12,4},{16,24},{20,28},{24,16},{28,20},{32,40},... | collective-permute-start | bytes 1966088 | tf_op jit(solution)/shard_map/ppermute | solution.py:32
  88.5 21.8 %collective-permute-start.22 = (bf16[512,2048]{1,0:T(8,128)(2,1)S(1)}, bf16[512,2048]{1,0:T(8,128)(2,1)S(1)}, u32[]{:S(2)}, u32[]{:S(2)}) collective-permute-start(bf16[512,2048]{1,0:T(8,128)(2,1)S(1)} %get-tuple-element.581), channel_id=1, source_target_pairs={{0,4},{4,0},{8,12},{12,8},{16,20},{20,16},{24,28},{28,24},{32,36},... | collective-permute-start | bytes 6291464 | tf_op jit(solution)/shard_map/ppermute | solution.py:32
  94.2 16.1 %collective-permute-start.18 = (bf16[320,512]{1,0:T(8,128)(2,1)S(1)}, bf16[320,512]{1,0:T(8,128)(2,1)S(1)}, u32[]{:S(2)}, u32[]{:S(2)}) collective-permute-start(bf16[320,512]{1,0:T(8,128)(2,1)S(1)} %get-tuple-element.590.left_a), channel_id=1, source_target_pairs={{0,48},{4,52},{8,56},{12,60},{16,32},{20,36},{24,40},{28,44},{32,1... | collective-permute-start | bytes 983048 | tf_op jit(solution)/shard_map/ppermute | solution.py:32
  95.6 14.6 %collective-permute-start.19 = (bf16[320,512]{1,0:T(8,128)(2,1)S(1)}, bf16[320,512]{1,0:T(8,128)(2,1)S(1)}, u32[]{:S(2)}, u32[]{:S(2)}) collective-permute-start(bf16[320,512]{1,0:T(8,128)(2,1)S(1)} %get-tuple-element.591.left_b), channel_id=1, source_target_pairs={{0,16},{4,20},{8,24},{12,28},{16,0},{20,4},{24,8},{28,12},{32,48},... | collective-permute-start | bytes 983048 | tf_op jit(solution)/shard_map/ppermute | solution.py:32
  110.7 15.3 %collective-permute-start.23 = (bf16[320,1024]{1,0:T(8,128)(2,1)S(1)}, bf16[320,1024]{1,0:T(8,128)(2,1)S(1)}, u32[]{:S(2)}, u32[]{:S(2)}) collective-permute-start(bf16[320,1024]{1,0:T(8,128)(2,1)S(1)} %get-tuple-element.616), channel_id=1, source_target_pairs={{0,16},{4,20},{8,24},{12,28},{16,0},{20,4},{24,8},{28,12},{32,48},... | collective-permute-start | bytes 1966088 | tf_op jit(solution)/shard_map/ppermute | solution.py:32
  110.8 16.3 %collective-permute-start.24 = (bf16[320,1024]{1,0:T(8,128)(2,1)S(1)}, bf16[320,1024]{1,0:T(8,128)(2,1)S(1)}, u32[]{:S(2)}, u32[]{:S(2)}) collective-permute-start(bf16[320,1024]{1,0:T(8,128)(2,1)S(1)} %get-tuple-element.617), channel_id=1, source_target_pairs={{0,48},{4,52},{8,56},{12,60},{16,32},{20,36},{24,40},{28,44},{32,1... | collective-permute-start | bytes 1966088 | tf_op jit(solution)/shard_map/ppermute | solution.py:32
  112.3 14.8 %collective-permute-start.25 = (bf16[640,512]{1,0:T(8,128)(2,1)S(1)}, bf16[640,512]{1,0:T(8,128)(2,1)S(1)}, u32[]{:S(2)}, u32[]{:S(2)}) collective-permute-start(bf16[640,512]{1,0:T(8,128)(2,1)S(1)} %shard_map.88.refs_0_), channel_id=1, source_target_pairs={{0,8},{4,12},{8,0},{12,4},{16,24},{20,28},{24,16},{28,20},{32,40},... | collective-permute-start | bytes 1966088 | tf_op jit(solution)/shard_map/ppermute | solution.py:32
  113.3 15.6 %collective-permute-start.26 = (bf16[2,128,1280]{2,1,0:T(8,128)(2,1)S(1)}, bf16[2,128,1280]{2,1,0:T(8,128)(2,1)S(1)}, u32[]{:S(2)}, u32[]{:S(2)}) collective-permute-start(bf16[2,128,1280]{2,1,0:T(8,128)(2,1)S(1)} %get-tuple-element.640), channel_id=1, source_target_pairs={{0,1},{1,2},{2,3},{3,0},{4,5},{5,6},{6,7},{7,4},{8,9},{9,10},{10,1... | collective-permute-start | bytes 1966088 | tf_op jit(solution)/shard_map/ppermute | solution.py:32
  114.1 14.8 %collective-permute-start.27 = (bf16[2,128,1280]{2,1,0:T(8,128)(2,1)S(1)}, bf16[2,128,1280]{2,1,0:T(8,128)(2,1)S(1)}, u32[]{:S(2)}, u32[]{:S(2)}) collective-permute-start(bf16[2,128,1280]{2,1,0:T(8,128)(2,1)S(1)} %get-tuple-element.642), channel_id=1, source_target_pairs={{0,3},{1,0},{2,1},{3,2},{4,7},{5,4},{6,5},{7,6},{8,11},{9,8},{10,9... | collective-permute-start | bytes 1966088 | tf_op jit(solution)/shard_map/ppermute | solution.py:32
  128.9 16.5 %collective-permute-start.28 = (bf16[640,1024]{1,0:T(8,128)(2,1)S(1)}, bf16[640,1024]{1,0:T(8,128)(2,1)S(1)}, u32[]{:S(2)}, u32[]{:S(2)}) collective-permute-start(bf16[640,1024]{1,0:T(8,128)(2,1)S(1)} %get-tuple-element.692.refs_0_), channel_id=1, source_target_pairs={{0,4},{4,0},{8,12},{12,8},{16,20},{20,16},{24,28},{28,24},{32,36},... | collective-permute-start | bytes 3932168 | tf_op jit(solution)/shard_map/ppermute | solution.py:32
  131.7 13.7 %collective-permute-start.32 = (bf16[640,1024]{1,0:T(8,128)(2,1)S(1)}, bf16[640,1024]{1,0:T(8,128)(2,1)S(1)}, u32[]{:S(2)}, u32[]{:S(2)}) collective-permute-start(bf16[640,1024]{1,0:T(8,128)(2,1)S(1)} %shard_map.91.refs_2_), channel_id=1, source_target_pairs={{0,4},{4,0},{8,12},{12,8},{16,20},{20,16},{24,28},{28,24},{32,36},... | collective-permute-start | bytes 3932168 | tf_op jit(solution)/shard_map/ppermute | solution.py:32
  131.7 13.7 %collective-permute-start.29 = (bf16[112,2048]{1,0:T(8,128)(2,1)S(1)}, bf16[112,2048]{1,0:T(8,128)(2,1)S(1)}, u32[]{:S(2)}, u32[]{:S(2)}) collective-permute-start(bf16[112,2048]{1,0:T(8,128)(2,1)S(1)} %get-tuple-element.647), channel_id=1, source_target_pairs={{0,64},{64,0},{1,65},{65,1},{2,66},{66,2},{3,67},{67,3},{4,68},{68... | collective-permute-start | bytes 1376264 | tf_op jit(solution)/shard_map/ppermute | solution.py:32
  146.7 17.8 %collective-permute-start.34 = (bf16[320,1024]{1,0:T(8,128)(2,1)S(1)}, bf16[320,1024]{1,0:T(8,128)(2,1)S(1)}, u32[]{:S(2)}, u32[]{:S(2)}) collective-permute-start(bf16[320,1024]{1,0:T(8,128)(2,1)S(1)} %get-tuple-element.685), channel_id=1, source_target_pairs={{0,16},{4,20},{8,24},{12,28},{16,0},{20,4},{24,8},{28,12},{32,48},... | collective-permute-start | bytes 1966088 | tf_op jit(solution)/shard_map/ppermute | solution.py:32
  147.5 17.2 %collective-permute-start.35 = (bf16[320,1024]{1,0:T(8,128)(2,1)S(1)}, bf16[320,1024]{1,0:T(8,128)(2,1)S(1)}, u32[]{:S(2)}, u32[]{:S(2)}) collective-permute-start(bf16[320,1024]{1,0:T(8,128)(2,1)S(1)} %get-tuple-element.686), channel_id=1, source_target_pairs={{0,48},{4,52},{8,56},{12,60},{16,32},{20,36},{24,40},{28,44},{32,1... | collective-permute-start | bytes 1966088 | tf_op jit(solution)/shard_map/ppermute | solution.py:32
  148.8 15.7 %collective-permute-start.33 = (bf16[144,2048]{1,0:T(8,128)(2,1)S(1)}, bf16[144,2048]{1,0:T(8,128)(2,1)S(1)}, u32[]{:S(2)}, u32[]{:S(2)}) collective-permute-start(bf16[144,2048]{1,0:T(8,128)(2,1)S(1)} %get-tuple-element.683), channel_id=1, source_target_pairs={{0,64},{64,0},{1,65},{65,1},{2,66},{66,2},{3,67},{67,3},{4,68},{68... | collective-permute-start | bytes 1769480 | tf_op jit(solution)/shard_map/ppermute | solution.py:32
  (21 other events, 123.3 us)

commit v4 on v3

--- a/solution.py
+++ b/solution.py
@@ -20,16 +20,19 @@
 Y3 = dp_pairs(fy=lambda y: y ^ 3)
 ZLO = dp_pairs(fz=lambda z: z ^ 1)
 CORE = dp_pairs(fc=lambda c: c ^ 1)
-SECTION = [(0, 1), (1, 0)]
 AROUND, SLOT_OF, SLOTS = 1, 5, 9
 
 
-def shift(step):
-    return [(i, (i + step) % 4) for i in range(4)]
-
-
-def swap(value, pairs, axis="dp"):
-    return lax.ppermute(value, axis, pairs)
+def swap(value, pairs):
+    return lax.ppermute(value, "dp", pairs)
+
+
+def along_x(value, step):
+    return lax.ppermute(value, "tensor", [(i, (i + step) % 4) for i in range(4)])
+
+
+def to_section(value):
+    return lax.ppermute(value, "section", [(0, 1), (1, 0)])
 
 
 ANY = pl.BlockSpec(memory_space=pl.ANY)
@@ -391,26 +394,8 @@
 
 
 class Phases:
-    def __init__(self):
-        self.here, self.away = {}, {}
-
-    def __getitem__(self, name):
-        return self.here[name]
-
-    def __setitem__(self, name, value):
-        self.here[name] = value
-
-    def send(self, name, source, pairs, axis="dp"):
-        self.away[name] = swap(self.here[source], pairs, axis)
-
-    def land(self, *names):
-        for name in names:
-            self.here[name] = self.away.pop(name)
-
-    def end(self, *drop):
-        for name in drop:
-            del self.here[name]
-        self.here = lax.optimization_barrier(self.here)
+    def end(self):
+        self.__dict__ = lax.optimization_barrier(self.__dict__)
 
 
 def body(features, layer_norm_gain, layer_norm_bias, proj_weight, cotangent):
@@ -420,21 +405,10 @@
     wanted = ((0, 1, 2), (1, 2, 2), (0, 3, 1), (1, 1, 1), (0, 0, 1), (1, 0, 1))
     v = Phases()
 
-    def near(n):
-        return [v["n%d" % n], *(v["x%d%d" % (n, k)] for k in (1, 3, 2))]
-
     def grads():
-        return [v["mine"], v["away"], v["mine_c"], v["away_c"]]
-
-    def products(t):
-        names = "send_a", "send_b", "next_a", "next_b", "keep_a", "keep_b"
-        for name, value in zip(names, weight_grad_blocks(v["index"], near(t), grads(), wanted)):
-            v[name + str(t)] = value
-
-    def spread(t):
-        v["a%d" % t], v["b%d" % t], v["ab%d" % t] = join(*(v[n + str(t)] for n in ("da", "db", "ga", "gb")))
-
-    def finish(t, early, late):
+        return [v.mine, v.away, v.mine_c, v.away_c]
+
+    def finish(t, early, late, into):
         pieces = []
         for arrays, places in ((early, ((0, 3), (0, 1))), (late, ((1, 2), (3, 2)))):
             for n, array in enumerate(arrays):
@@ -442,134 +416,158 @@
                     pieces += [(array, h * half, n == 1, h, places[h]) for h in range(2)]
                 else:
                     pieces.append((array, 0, n > 1, n % 2, places[n % 2]))
-        v["weight_grad"] = place(v["index"], pieces, ROW_CHUNKS[t][0], width, cols, v.here.get("weight_grad"))
-
-    v["ours"], v["theirs"], v["mine"], v["scale"], v["index"] = prepare(
+        return place(v.index, pieces, ROW_CHUNKS[t][0], width, cols, into)
+
+    v.ours, v.theirs, v.mine, v.scale, v.index = prepare(
         features, cotangent, layer_norm_gain, layer_norm_bias
     )
     v.end()
 
-    v.send("away", "mine", SECTION, "section")
-    v.send("rows", "theirs", CORE)
-    v.send("mine_c", "mine", CORE)
-    v.land("rows")
-    v["n0"], v["n1"] = normalize(v["ours"], v["rows"], v["scale"])
-    v.land("mine_c")
-    v.end("theirs")
-
-    for k in (1, 3, 2):
-        v.send("x0%d" % k, "n0", shift(-k), "tensor")
-    v["weight"] = take_tap(v["index"], proj_weight)
-    v.land("x01", "x03", "x02", "away")
-    v.end()
-
-    v.send("away_c", "away", CORE)
-    v.send("x11", "n1", shift(-1), "tensor")
-    v.send("x13", "n1", shift(-3), "tensor")
-    v.land("away_c")
-    v.end()
-
-    products(0)
-    v.land("x11", "x13")
-    v.end()
-
-    v.send("got_a0", "send_a0", Y1)
-    v.send("got_b0", "send_b0", Y3)
-    v.send("x12", "n1", shift(-2), "tensor")
-    for k, part in zip((0, 1, 3, 2), row_gradients(v["index"], grads(), v["weight"])):
-        v["r%d" % k] = part
-    v.land("got_a0", "got_b0", "x12")
-    v.end("send_a0", "send_b0")
-
-    v["n_a0"], v["n_b0"] = add_first(v["next_a0"], v["next_b0"], v["got_a0"], v["got_b0"])
-    v.end("next_a0", "next_b0")
-
-    v.send("more_a0", "n_a0", Y3)
-    v.send("more_b0", "n_b0", Y1)
-    products(1)
-    v.land("more_a0", "more_b0")
-    v.end("n_a0", "n_b0", "mine", "away", "mine_c", "away_c")
-
-    v["keep0"] = add_second(*(v[n + "0"] for n in ("keep_a", "keep_b", "got_a", "got_b", "more_a", "more_b")))
-    v.end("keep_a0", "keep_b0", "got_a0", "got_b0", "more_a0", "more_b0")
-
-    v.send("got_a1", "send_a1", Y1)
-    v.send("got_b1", "send_b1", Y3)
-    v.send("other0", "keep0", ZLO)
-    v.send("s2", "r2", shift(2), "tensor")
-    v["own"], v["other"] = project(v["index"], [near(0), near(1)], v["weight"])
-    v.land("got_a1", "got_b1", "other0", "s2")
-    v.end("r2", "send_a1", "send_b1", "x01", "x03", "x02", "x11", "x13", "x12", "n0", "n1")
-
-    v["n_a1"], v["n_b1"] = add_first(v["next_a1"], v["next_b1"], v["got_a1"], v["got_b1"])
-    v["da0"], v["db0"] = add_third(v["keep0"], v["other0"])
-    v.end("next_a1", "next_b1", "keep0", "other0")
-
-    v.send("more_a1", "n_a1", Y3)
-    v.send("more_b1", "n_b1", Y1)
-    v.send("ga0", "da0", Y3)
-    v.send("gb0", "db0", Y1)
-    v.send("other_c", "other", CORE)
-    v.land("more_a1", "more_b1", "ga0", "gb0", "other_c")
-    v.end("n_a1", "n_b1", "other")
-
-    v["keep1"] = add_second(*(v[n + "1"] for n in ("keep_a", "keep_b", "got_a", "got_b", "more_a", "more_b")))
-    spread(0)
-    v.end("keep_a1", "keep_b1", "got_a1", "got_b1", "more_a1", "more_b1", "da0", "db0", "ga0", "gb0")
-
-    v.send("other1", "keep1", ZLO)
-    v.send("la0", "a0", Y1)
-    v.send("lb0", "b0", Y3)
-    v.send("s1", "r1", shift(1), "tensor")
-    v.send("s3", "r3", shift(3), "tensor")
+    away = to_section(v.mine)
+    rows = swap(v.theirs, CORE)
+    mine_c = swap(v.mine, CORE)
+    v.rows = rows
+    v.n0, v.n1 = normalize(v.ours, v.rows, v.scale)
+    v.mine_c = mine_c
+    del v.theirs
+    v.end()
+
+    x01 = along_x(v.n0, -1)
+    x03 = along_x(v.n0, -3)
+    x02 = along_x(v.n0, -2)
+    v.weight = take_tap(v.index, proj_weight)
+    v.x01, v.x03, v.x02, v.away = x01, x03, x02, away
+    v.end()
+
+    away_c = swap(v.away, CORE)
+    x11 = along_x(v.n1, -1)
+    x13 = along_x(v.n1, -3)
+    v.away_c = away_c
+    v.end()
+
+    near0 = [v.n0, v.x01, v.x03, v.x02]
+    v.send_a0, v.send_b0, v.next_a0, v.next_b0, v.keep_a0, v.keep_b0 = weight_grad_blocks(
+        v.index, near0, grads(), wanted
+    )
+    v.x11, v.x13 = x11, x13
+    v.end()
+
+    got_a0 = swap(v.send_a0, Y1)
+    got_b0 = swap(v.send_b0, Y3)
+    x12 = along_x(v.n1, -2)
+    v.r0, v.r1, v.r3, v.r2 = row_gradients(v.index, grads(), v.weight)
+    v.got_a0, v.got_b0, v.x12 = got_a0, got_b0, x12
+    del v.send_a0, v.send_b0
+    v.end()
+
+    v.n_a0, v.n_b0 = add_first(v.next_a0, v.next_b0, v.got_a0, v.got_b0)
+    del v.next_a0, v.next_b0
+    v.end()
+
+    more_a0 = swap(v.n_a0, Y3)
+    more_b0 = swap(v.n_b0, Y1)
+    near1 = [v.n1, v.x11, v.x13, v.x12]
+    v.send_a1, v.send_b1, v.next_a1, v.next_b1, v.keep_a1, v.keep_b1 = weight_grad_blocks(
+        v.index, near1, grads(), wanted
+    )
+    v.more_a0, v.more_b0 = more_a0, more_b0
+    del v.n_a0, v.n_b0, v.mine, v.away, v.mine_c, v.away_c
+    v.end()
+
+    v.keep0 = add_second(
+        v.keep_a0, v.keep_b0, v.got_a0, v.got_b0, v.more_a0, v.more_b0
+    )
+    del v.keep_a0, v.keep_b0, v.got_a0, v.got_b0, v.more_a0, v.more_b0
+    v.end()
+
+    got_a1 = swap(v.send_a1, Y1)
+    got_b1 = swap(v.send_b1, Y3)
+    other0 = swap(v.keep0, ZLO)
+    s2 = along_x(v.r2, 2)
+    v.own, v.other = project(v.index, [[v.n0, v.x01, v.x03, v.x02], [v.n1, v.x11, v.x13, v.x12]], v.weight)
+    v.got_a1, v.got_b1, v.other0, v.s2 = got_a1, got_b1, other0, s2
+    del v.r2, v.send_a1, v.send_b1, v.x01, v.x03, v.x02, v.x11, v.x13, v.x12, v.n0, v.n1
+    v.end()
+
+    v.n_a1, v.n_b1 = add_first(v.next_a1, v.next_b1, v.got_a1, v.got_b1)
+    v.da0, v.db0 = add_third(v.keep0, v.other0)
+    del v.next_a1, v.next_b1, v.keep0, v.other0
+    v.end()
+
+    more_a1 = swap(v.n_a1, Y3)
+    more_b1 = swap(v.n_b1, Y1)
+    ga0 = swap(v.da0, Y3)
+    gb0 = swap(v.db0, Y1)
+    other_c = swap(v.other, CORE)
+    v.more_a1, v.more_b1, v.ga0, v.gb0, v.other_c = more_a1, more_b1, ga0, gb0, other_c
+    del v.n_a1, v.n_b1, v.other
+    v.end()
+
+    v.keep1 = add_second(
+        v.keep_a1, v.keep_b1, v.got_a1, v.got_b1, v.more_a1, v.more_b1
+    )
+    v.a0, v.b0, v.ab0 = join(v.da0, v.db0, v.ga0, v.gb0)
+    del v.keep_a1, v.keep_b1, v.got_a1, v.got_b1, v.more_a1, v.more_b1, v.da0, v.db0, v.ga0, v.gb0
+    v.end()
+
+    other1 = swap(v.keep1, ZLO)
+    la0 = swap(v.a0, Y1)
+    lb0 = swap(v.b0, Y3)
+    s1 = along_x(v.r1, 1)
+    s3 = along_x(v.r3, 3)
     rows = [slice(0, 112), slice(112, 256), slice(256, 368), slice(368, 512)]
-    v["up0"], v["up1"] = sums(*([(v["own"], (r, EVERY)), (v["other_c"], (r, EVERY))] for r in rows[2:]))
-    v.land("other1", "la0", "lb0")
-    v.end("a0", "b0", "r1", "r3")
-
-    v["da1"], v["db1"] = add_third(v["keep1"], v["other1"])
-    v["lab0"] = below(v["la0"], v["lb0"])
-    v.land("s1", "s3")
-    v.end("keep1", "other1", "la0", "lb0")
-
-    v.send("ga1", "da1", Y3)
-    v.send("gb1", "db1", Y1)
-    v.send("back0", "up0", SECTION, "section")
-    v.send("ab0_c", "ab0", CORE)
-    v.send("lab0_c", "lab0", CORE)
-    v["own_rows"], v["hidden"] = normalize_backward(
-        v["ours"], v["rows"], v["scale"], [v["r0"], v["s1"], v["s3"], v["s2"]]
-    )
-    v.land("ga1", "gb1", "ab0_c", "lab0_c", "back0")
-    v.end("up0", "r0", "s1", "s3", "s2")
-
-    spread(1)
-    v.end("da1", "db1", "ga1", "gb1")
-
-    v.send("la1", "a1", Y1)
-    v.send("lb1", "b1", Y3)
-    v.send("ab1_c", "ab1", CORE)
-    v.send("hidden_c", "hidden", CORE)
-    v.send("back1", "up1", SECTION, "section")
-    finish(0, [v["ab0"], v["ab0_c"]], [v["lab0"], v["lab0_c"]])
-    v.land("ab1_c", "hidden_c")
-    finish(1, [v["ab1"], v["ab1_c"]], [])
-    v["result"] = both_taps(v["index"], v["own_rows"], v["hidden_c"])
-    v.land("la1", "lb1", "back1")
-    v.end("a1", "b1", "ab0", "ab0_c", "ab1", "ab1_c", "lab0", "lab0_c", "own_rows", "hidden", "hidden_c", "up1")
-
-    v.send("la1_c", "la1", CORE)
-    v.send("lb1_c", "lb1", CORE)
+    v.up0, v.up1 = sums(*([(v.own, (r, EVERY)), (v.other_c, (r, EVERY))] for r in rows[2:]))
+    v.other1, v.la0, v.lb0 = other1, la0, lb0
+    del v.a0, v.b0, v.r1, v.r3
+    v.end()
+
+    v.da1, v.db1 = add_third(v.keep1, v.other1)
+    v.lab0 = below(v.la0, v.lb0)
+    v.s1, v.s3 = s1, s3
+    del v.keep1, v.other1, v.la0, v.lb0
+    v.end()
+
+    ga1 = swap(v.da1, Y3)
+    gb1 = swap(v.db1, Y1)
+    back0 = to_section(v.up0)
+    ab0_c = swap(v.ab0, CORE)
+    lab0_c = swap(v.lab0, CORE)
+    v.own_rows, v.hidden = normalize_backward(
+        v.ours, v.rows, v.scale, [v.r0, v.s1, v.s3, v.s2]
+    )
+    v.ga1, v.gb1, v.ab0_c, v.lab0_c, v.back0 = ga1, gb1, ab0_c, lab0_c, back0
+    del v.up0, v.r0, v.s1, v.s3, v.s2
+    v.end()
+
+    v.a1, v.b1, v.ab1 = join(v.da1, v.db1, v.ga1, v.gb1)
+    del v.da1, v.db1, v.ga1, v.gb1
+    v.end()
+
+    la1 = swap(v.a1, Y1)
+    lb1 = swap(v.b1, Y3)
+    ab1_c = swap(v.ab1, CORE)
+    hidden_c = swap(v.hidden, CORE)
+    back1 = to_section(v.up1)
+    v.weight_grad = finish(0, [v.ab0, v.ab0_c], [v.lab0, v.lab0_c], None)
+    v.ab1_c, v.hidden_c = ab1_c, hidden_c
+    v.weight_grad = finish(1, [v.ab1, v.ab1_c], [], v.weight_grad)
+    v.result = both_taps(v.index, v.own_rows, v.hidden_c)
+    v.la1, v.lb1, v.back1 = la1, lb1, back1
+    del v.a1, v.b1, v.ab0, v.ab0_c, v.ab1, v.ab1_c, v.lab0, v.lab0_c, v.own_rows, v.hidden, v.hidden_c, v.up1
+    v.end()
+
+    la1_c = swap(v.la1, CORE)
+    lb1_c = swap(v.lb1, CORE)
     projected = sums(
         *(
-            [(v["own"], (r, EVERY)), (v["other_c"], (r, EVERY)), (v[back], (EVERY, EVERY))]
-            for r, back in zip(rows, ("back0", "back1"))
+            [(v.own, (r, EVERY)), (v.other_c, (r, EVERY)), (back, (EVERY, EVERY))]
+            for r, back in zip(rows, (v.back0, v.back1))
         ),
         stack=True,
     )[0]
-    v.land("la1_c", "lb1_c")
-    finish(1, [], [v["la1"], v["lb1"], v["la1_c"], v["lb1_c"]])
-    return (projected[None], v["weight_grad"], v["result"])
+    v.la1_c, v.lb1_c = la1_c, lb1_c
+    v.weight_grad = finish(1, [], [v.la1, v.lb1, v.la1_c, v.lb1_c], v.weight_grad)
+    return (projected[None], v.weight_grad, v.result)
 
 
 def solution(mesh):

time: 171 us -> 171 us (level)
  no operation moved by 1% of the time
where the time goes in v4:
time: 171 us
  waiting for transfers between devices  70.3 us (41%)
  starting transfers between devices  54.5 us (32%)
  Pallas kernels  37.5 us (22%)
  local copies, waits for them, and re-layouts  7.69 us (4%)
    ppermute x28, waiting for transfers between devices, swap(): return lax.ppermute(value, 'dp', pairs)  46.7 us
    pallas_call x23, Pallas kernels, call(): pl.pallas_call(kernel, in_specs=in_specs, out_specs=out_specs, out_shape=...  37.5 us
    ppermute x28, starting transfers between devices, swap(): return lax.ppermute(value, 'dp', pairs)  30.7 us
    ppermute x3, waiting for transfers between devices, to_section(): return lax.ppermute(value, 'section', [(0, 1), (1, 0)])  16.2 us
    ppermute x9, starting transfers between devices, along_x(): lax.ppermute(value, 'tensor', [(i, (i + step) % 4) for i in range(4)])  13.9 us
    ppermute x3, starting transfers between devices, to_section(): return lax.ppermute(value, 'section', [(0, 1), (1, 0)])  9.96 us
    unnamed x10, local copies, waits for them, and re-layouts  7.69 us
    ppermute x9, waiting for transfers between devices, along_x(): lax.ppermute(value, 'tensor', [(i, (i + step) % 4) for i in range(4)])  7.39 us
  transfers between devices with their start and end apart: 40, of which 22 were waited for; matrix products, arithmetic and copies ran while one was open for 0% of the time, Pallas kernels for 19%

profile of v4, /device:TPU:1, one launch (start us, length us, event | category | flops | bytes accessed | tf_op | source)
XLA Modules:
  0.0 171.0 jit_solution(6839683276895376474)
XLA Ops:
  6.9 3.7 %collective-permute-start = (bf16[256,2048]{1,0:T(8,128)(2,1)S(1)}, bf16[256,2048]{1,0:T(8,128)(2,1)S(1)}, u32[]{:S(2)}, u32[]{:S(2)}) collective-permute-start(bf16[256,2048]{1,0:T(8,128)(2,1)S(1)} %get-tuple-element.470.refs_4_.refs_0_), channel_id=1, source_target_pairs={{0,64},{64,0},{1,65},{65,1},{2,66},{66,2},{3,67},{67,3},{4,68},{68... | collective-permute-start | bytes 3145736 | tf_op jit(solution)/shard_map/ppermute | solution.py:35
  14.0 2.5 %collective-permute-start.4 = (bf16[2,128,640]{2,1,0:T(8,128)(2,1)S(1)}, bf16[2,128,640]{2,1,0:T(8,128)(2,1)S(1)}, u32[]{:S(2)}, u32[]{:S(2)}) collective-permute-start(bf16[2,128,640]{2,1,0:T(8,128)(2,1)S(1)} %get-tuple-element.532.refs_0_), channel_id=1, source_target_pairs={{0,2},{1,3},{2,0},{3,1},{4,6},{5,7},{6,4},{7,5},{8,10},{9,11},{10,... | collective-permute-start | bytes 983048 | tf_op jit(solution)/shard_map/ppermute | solution.py:31
  17.6 4.0 %copy-done = bf16[2560,2048]{1,0:T(8,128)(2,1)S(1)} copy-done((bf16[2560,2048]{1,0:T(8,128)(2,1)S(1)}, bf16[2560,2048]{1,0:T(8,128)(2,1)}, u32[]{:S(2)}) %copy-start) | copy-done | bytes 10485784
  21.6 2.3 %shard_map.78.refs_4_.refs_8_ = bf16[1280,2048]{1,0:T(8,128)(2,1)S(1)} custom-call(s32[13]{0:T(128)S(1)} %get-tuple-element.700.index, bf16[2560,2048]{1,0:T(8,128)(2,1)S(1)} %copy-done), custom_call_target="tpu_custom_call" | custom-call | flops 1 | bytes 1 | tf_op jit(solution)/shard_map/pallas_call | solution.py:63
  23.9 10.1 %collective-permute-done.refs_5_.refs_1_ = bf16[256,2048]{1,0:T(8,128)(2,1)S(1)} collective-permute-done((bf16[256,2048]{1,0:T(8,128)(2,1)S(1)}, bf16[256,2048]{1,0:T(8,128)(2,1)S(1)}, u32[]{:S(2)}, u32[]{:S(2)}) %collective-permute-start) | collective-permute-done | bytes 1048608 | tf_op jit(solution)/shard_map/ppermute | solution.py:35
  37.4 3.9 %shard_map.79 = (bf16[320,1024]{1,0:T(8,128)(2,1)S(1)}, bf16[320,1024]{1,0:T(8,128)(2,1)S(1)}, bf16[320,512]{1,0:T(8,128)(2,1)S(1)}, bf16[320,512]{1,0:T(8,128)(...) custom-call(s32[13]{0:T(128)S(1)} %get-tuple-element.700.index, ...), custom_call_target="tpu_custom_call" | custom-call | flops 1 | bytes 1 | tf_op jit(solution)/shard_map/pallas_call | solution.py:63
  41.3 3.9 %collective-permute-done.8.refs_2_.refs_6_ = bf16[2,128,640]{2,1,0:T(8,128)(2,1)S(1)} collective-permute-done((bf16[2,128,640]{2,1,0:T(8,128)(2,1)S(1)}, bf16[2,128,640]{2,1,0:T(8,128)(2,1)S(1)}, u32[]{:S(2)}, u32[]{:S(2)}) %collective-permute-start.8) | collective-permute-done | bytes 327712 | tf_op jit(solution)/shard_map/ppermute | solution.py:31
  50.5 6.8 %shard_map.80 = (bf16[2,128,1280]{2,1,0:T(8,128)(2,1)S(1)}, bf16[2,128,1280]{2,1,0:T(8,128)(2,1)S(1)}, bf16[2,128,1280]{2,1,0:T(8,128)(2,1)S(1)}, bf16[2,128,1280]{2,1,0:T(8,128)(2,1)S(1)}) custom-call(s32[13]{0:T(128)S(1)} %get-tuple-element.700.index, bf16[256,2048]{1,0:T(8,128)(2,1)S(1)} %get-tuple-element.470.refs_4_.refs_0_, ...), custom_call_target="tpu_custom_call" | custom-call | flops 1 | bytes 1 | tf_op jit(solution)/shard_map/pallas_call | solution.py:63
  57.7 2.9 %collective-permute-done.9.refs_1_ = bf16[320,1024]{1,0:T(8,128)(2,1)S(1)} collective-permute-done((bf16[320,1024]{1,0:T(8,128)(2,1)S(1)}, bf16[320,1024]{1,0:T(8,128)(2,1)S(1)}, u32[]{:S(2)}, u32[]{:S(2)}) %collective-permute-start.9) | collective-permute-done | bytes 655392 | tf_op jit(solution)/shard_map/ppermute | solution.py:27
  60.6 2.2 %collective-permute-done.10.refs_3_.refs_4_ = bf16[320,1024]{1,0:T(8,128)(2,1)S(1)} collective-permute-done((bf16[320,1024]{1,0:T(8,128)(2,1)S(1)}, bf16[320,1024]{1,0:T(8,128)(2,1)S(1)}, u32[]{:S(2)}, u32[]{:S(2)}) %collective-permute-start.10) | collective-permute-done | bytes 655392 | tf_op jit(solution)/shard_map/ppermute | solution.py:27
  65.0 3.9 %shard_map.82 = (bf16[320,1024]{1,0:T(8,128)(2,1)S(1)}, bf16[320,1024]{1,0:T(8,128)(2,1)S(1)}, bf16[320,512]{1,0:T(8,128)(2,1)S(1)}, bf16[320,512]{1,0:T(8,128)(...) custom-call(s32[13]{0:T(128)S(1)} %get-tuple-element.700.index, ...), custom_call_target="tpu_custom_call" | custom-call | flops 1 | bytes 1 | tf_op jit(solution)/shard_map/pallas_call | solution.py:63
  68.8 2.6 %collective-permute-done.12.refs_2_ = bf16[320,512]{1,0:T(8,128)(2,1)S(1)} collective-permute-done((bf16[320,512]{1,0:T(8,128)(2,1)S(1)}, bf16[320,512]{1,0:T(8,128)(2,1)S(1)}, u32[]{:S(2)}, u32[]{:S(2)}) %collective-permute-start.12) | collective-permute-done | bytes 327712 | tf_op jit(solution)/shard_map/ppermute | solution.py:27
  76.2 6.3 %shard_map.84 = (bf16[512,2048]{1,0:T(8,128)(2,1)S(1)}, bf16[512,2048]{1,0:T(8,128)(2,1)S(1)}) custom-call(s32[13]{0:T(128)S(1)} %get-tuple-element.700.index, bf16[2,128,640]{2,1,0:T(8,128)(2,1)S(1)} %get-tuple-element.532.refs_0_, bf16[2,128,640]{2,1,0:T(8,128)(2,1)S(1)} %collective-permute-done.3.refs_1_, ...), custom_call_target="tpu_custom_call" | custom-call | flops 1 | bytes 1 | tf_op jit(solution)/shard_map/pallas_call | solution.py:63
  82.6 2.5 %collective-permute-done.14.refs_1_ = bf16[320,1024]{1,0:T(8,128)(2,1)S(1)} collective-permute-done((bf16[320,1024]{1,0:T(8,128)(2,1)S(1)}, bf16[320,1024]{1,0:T(8,128)(2,1)S(1)}, u32[]{:S(2)}, u32[]{:S(2)}) %collective-permute-start.14) | collective-permute-done | bytes 655392 | tf_op jit(solution)/shard_map/ppermute | solution.py:27
  88.5 4.3 %collective-permute-start.22 = (bf16[512,2048]{1,0:T(8,128)(2,1)S(1)}, bf16[512,2048]{1,0:T(8,128)(2,1)S(1)}, u32[]{:S(2)}, u32[]{:S(2)}) collective-permute-start(bf16[512,2048]{1,0:T(8,128)(2,1)S(1)} %get-tuple-element.581), channel_id=1, source_target_pairs={{0,4},{4,0},{8,12},{12,8},{16,20},{20,16},{24,28},{28,24},{32,36},... | collective-permute-start | bytes 6291464 | tf_op jit(solution)/shard_map/ppermute | solution.py:27
  96.3 6.9 %collective-permute-done.20.refs_2_ = bf16[320,512]{1,0:T(8,128)(2,1)S(1)} collective-permute-done((bf16[320,512]{1,0:T(8,128)(2,1)S(1)}, bf16[320,512]{1,0:T(8,128)(2,1)S(1)}, u32[]{:S(2)}, u32[]{:S(2)}) %collective-permute-start.20) | collective-permute-done | bytes 327712 | tf_op jit(solution)/shard_map/ppermute | solution.py:27
  103.3 7.0 %collective-permute-done.18.right_a = bf16[320,512]{1,0:T(8,128)(2,1)S(1)} collective-permute-done((bf16[320,512]{1,0:T(8,128)(2,1)S(1)}, bf16[320,512]{1,0:T(8,128)(2,1)S(1)}, u32[]{:S(2)}, u32[]{:S(2)}) %collective-permute-start.18) | collective-permute-done | bytes 327712 | tf_op jit(solution)/shard_map/ppermute | solution.py:27
  116.2 9.8 %collective-permute-done.23.top = bf16[320,1024]{1,0:T(8,128)(2,1)S(1)} collective-permute-done((bf16[320,1024]{1,0:T(8,128)(2,1)S(1)}, bf16[320,1024]{1,0:T(8,128)(2,1)S(1)}, u32[]{:S(2)}, u32[]{:S(2)}) %collective-permute-start.23) | collective-permute-done | bytes 655392 | tf_op jit(solution)/shard_map/ppermute | solution.py:27
  128.9 2.8 %collective-permute-start.28 = (bf16[640,1024]{1,0:T(8,128)(2,1)S(1)}, bf16[640,1024]{1,0:T(8,128)(2,1)S(1)}, u32[]{:S(2)}, u32[]{:S(2)}) collective-permute-start(bf16[640,1024]{1,0:T(8,128)(2,1)S(1)} %get-tuple-element.692.refs_0_), channel_id=1, source_target_pairs={{0,4},{4,0},{8,12},{12,8},{16,20},{20,16},{24,28},{28,24},{32,36},... | collective-permute-start | bytes 3932168 | tf_op jit(solution)/shard_map/ppermute | solution.py:27
  131.7 3.3 %collective-permute-start.29 = (bf16[112,2048]{1,0:T(8,128)(2,1)S(1)}, bf16[112,2048]{1,0:T(8,128)(2,1)S(1)}, u32[]{:S(2)}, u32[]{:S(2)}) collective-permute-start(bf16[112,2048]{1,0:T(8,128)(2,1)S(1)} %get-tuple-element.647), channel_id=1, source_target_pairs={{0,64},{64,0},{1,65},{65,1},{2,66},{66,2},{3,67},{67,3},{4,68},{68... | collective-permute-start | bytes 1376264 | tf_op jit(solution)/shard_map/ppermute | solution.py:35
  137.5 7.1 %collective-permute-done.30.right_a = bf16[320,512]{1,0:T(8,128)(2,1)S(1)} collective-permute-done((bf16[320,512]{1,0:T(8,128)(2,1)S(1)}, bf16[320,512]{1,0:T(8,128)(2,1)S(1)}, u32[]{:S(2)}, u32[]{:S(2)}) %collective-permute-start.30) | collective-permute-done | bytes 327712 | tf_op jit(solution)/shard_map/ppermute | solution.py:27
  148.8 3.0 %collective-permute-start.33 = (bf16[144,2048]{1,0:T(8,128)(2,1)S(1)}, bf16[144,2048]{1,0:T(8,128)(2,1)S(1)}, u32[]{:S(2)}, u32[]{:S(2)}) collective-permute-start(bf16[144,2048]{1,0:T(8,128)(2,1)S(1)} %get-tuple-element.683), channel_id=1, source_target_pairs={{0,64},{64,0},{1,65},{65,1},{2,66},{66,2},{3,67},{67,3},{4,68},{68... | collective-permute-start | bytes 1769480 | tf_op jit(solution)/shard_map/ppermute | solution.py:35
  152.7 3.0 %shard_map.95.refs_2_ = bf16[2560,2048]{1,0:T(8,128)(2,1)} custom-call(s32[13]{0:T(128)S(1)} %get-tuple-element.700.index, bf16[640,1024]{1,0:T(8,128)(2,1)S(1)} %get-tuple-element.692.refs_0_, bf16[640,1024]{1,0:T(8,128)(2,1)S(1)} %collective-permute-done.28.refs_1_, bf16[640,1024]{1,0:T(8,128)(2,1)S(1)} %shard_map.91.refs_2_, ...), custom_call_target="tpu_custom_call" | custom-call | flops 1 | bytes 1 | tf_op jit(solution)/shard_map/pallas_call | solution.py:63
  159.2 5.3 %collective-permute-done.33.refs_3_ = bf16[144,2048]{1,0:T(8,128)(2,1)S(1)} collective-permute-done((bf16[144,2048]{1,0:T(8,128)(2,1)S(1)}, bf16[144,2048]{1,0:T(8,128)(2,1)S(1)}, u32[]{:S(2)}, u32[]{:S(2)}) %collective-permute-start.33) | collective-permute-done | bytes 589856 | tf_op jit(solution)/shard_map/ppermute | solution.py:35
  (89 shorter events, 60.0 us)
Async XLA Ops:
  6.9 27.1 %collective-permute-start = (bf16[256,2048]{1,0:T(8,128)(2,1)S(1)}, bf16[256,2048]{1,0:T(8,128)(2,1)S(1)}, u32[]{:S(2)}, u32[]{:S(2)}) collective-permute-start(bf16[256,2048]{1,0:T(8,128)(2,1)S(1)} %get-tuple-element.470.refs_4_.refs_0_), channel_id=1, source_target_pairs={{0,64},{64,0},{1,65},{65,1},{2,66},{66,2},{3,67},{67,3},{4,68},{68... | collective-permute-start | bytes 3145736 | tf_op jit(solution)/shard_map/ppermute | solution.py:35
  12.7 21.3 %collective-permute-start.5 = (bf16[2,128,640]{2,1,0:T(8,128)(2,1)S(1)}, bf16[2,128,640]{2,1,0:T(8,128)(2,1)S(1)}, u32[]{:S(2)}, u32[]{:S(2)}) collective-permute-start(bf16[2,128,640]{2,1,0:T(8,128)(2,1)S(1)} %get-tuple-element.532.refs_0_), channel_id=1, source_target_pairs={{0,1},{1,2},{2,3},{3,0},{4,5},{5,6},{6,7},{7,4},{8,9},{9,10},{10,1... | collective-permute-start | bytes 983048 | tf_op jit(solution)/shard_map/ppermute | solution.py:31
  14.0 20.0 %collective-permute-start.4 = (bf16[2,128,640]{2,1,0:T(8,128)(2,1)S(1)}, bf16[2,128,640]{2,1,0:T(8,128)(2,1)S(1)}, u32[]{:S(2)}, u32[]{:S(2)}) collective-permute-start(bf16[2,128,640]{2,1,0:T(8,128)(2,1)S(1)} %get-tuple-element.532.refs_0_), channel_id=1, source_target_pairs={{0,2},{1,3},{2,0},{3,1},{4,6},{5,7},{6,4},{7,5},{8,10},{9,11},{10,... | collective-permute-start | bytes 983048 | tf_op jit(solution)/shard_map/ppermute | solution.py:31
  16.4 17.6 %collective-permute-start.3 = (bf16[2,128,640]{2,1,0:T(8,128)(2,1)S(1)}, bf16[2,128,640]{2,1,0:T(8,128)(2,1)S(1)}, u32[]{:S(2)}, u32[]{:S(2)}) collective-permute-start(bf16[2,128,640]{2,1,0:T(8,128)(2,1)S(1)} %get-tuple-element.532.refs_0_), channel_id=1, source_target_pairs={{0,3},{1,0},{2,1},{3,2},{4,7},{5,4},{6,5},{7,6},{8,11},{9,8},{10,9... | collective-permute-start | bytes 983048 | tf_op jit(solution)/shard_map/ppermute | solution.py:31
  45.2 15.4 %collective-permute-start.9 = (bf16[320,1024]{1,0:T(8,128)(2,1)S(1)}, bf16[320,1024]{1,0:T(8,128)(2,1)S(1)}, u32[]{:S(2)}, u32[]{:S(2)}) collective-permute-start(bf16[320,1024]{1,0:T(8,128)(2,1)S(1)} %get-tuple-element.409), channel_id=1, source_target_pairs={{0,16},{4,20},{8,24},{12,28},{16,0},{20,4},{24,8},{28,12},{32,48},... | collective-permute-start | bytes 1966088 | tf_op jit(solution)/shard_map/ppermute | solution.py:27
  46.5 16.3 %collective-permute-start.10 = (bf16[320,1024]{1,0:T(8,128)(2,1)S(1)}, bf16[320,1024]{1,0:T(8,128)(2,1)S(1)}, u32[]{:S(2)}, u32[]{:S(2)}) collective-permute-start(bf16[320,1024]{1,0:T(8,128)(2,1)S(1)} %get-tuple-element.410), channel_id=1, source_target_pairs={{0,48},{4,52},{8,56},{12,60},{16,32},{20,36},{24,40},{28,44},{32,1... | collective-permute-start | bytes 1966088 | tf_op jit(solution)/shard_map/ppermute | solution.py:27
  72.1 13.0 %collective-permute-start.14 = (bf16[320,1024]{1,0:T(8,128)(2,1)S(1)}, bf16[320,1024]{1,0:T(8,128)(2,1)S(1)}, u32[]{:S(2)}, u32[]{:S(2)}) collective-permute-start(bf16[320,1024]{1,0:T(8,128)(2,1)S(1)} %get-tuple-element.524), channel_id=1, source_target_pairs={{0,16},{4,20},{8,24},{12,28},{16,0},{20,4},{24,8},{28,12},{32,48},... | collective-permute-start | bytes 1966088 | tf_op jit(solution)/shard_map/ppermute | solution.py:27
  72.4 14.2 %collective-permute-start.15 = (bf16[320,1024]{1,0:T(8,128)(2,1)S(1)}, bf16[320,1024]{1,0:T(8,128)(2,1)S(1)}, u32[]{:S(2)}, u32[]{:S(2)}) collective-permute-start(bf16[320,1024]{1,0:T(8,128)(2,1)S(1)} %get-tuple-element.525), channel_id=1, source_target_pairs={{0,48},{4,52},{8,56},{12,60},{16,32},{20,36},{24,40},{28,44},{32,1... | collective-permute-start | bytes 1966088 | tf_op jit(solution)/shard_map/ppermute | solution.py:27
  73.7 14.5 %collective-permute-start.17 = (bf16[2,128,1280]{2,1,0:T(8,128)(2,1)S(1)}, bf16[2,128,1280]{2,1,0:T(8,128)(2,1)S(1)}, u32[]{:S(2)}, u32[]{:S(2)}) collective-permute-start(bf16[2,128,1280]{2,1,0:T(8,128)(2,1)S(1)} %get-tuple-element.548), channel_id=1, source_target_pairs={{0,2},{1,3},{2,0},{3,1},{4,6},{5,7},{6,4},{7,5},{8,10},{9,11},{10,... | collective-permute-start | bytes 1966088 | tf_op jit(solution)/shard_map/ppermute | solution.py:31
  75.2 13.0 %collective-permute-start.16 = (bf16[640,512]{1,0:T(8,128)(2,1)S(1)}, bf16[640,512]{1,0:T(8,128)(2,1)S(1)}, u32[]{:S(2)}, u32[]{:S(2)}) collective-permute-start(bf16[640,512]{1,0:T(8,128)(2,1)S(1)} %shard_map.83.refs_0_), channel_id=1, source_target_pairs={{0,8},{4,12},{8,0},{12,4},{16,24},{20,28},{24,16},{28,20},{32,40},... | collective-permute-start | bytes 1966088 | tf_op jit(solution)/shard_map/ppermute | solution.py:27
  88.5 21.8 %collective-permute-start.22 = (bf16[512,2048]{1,0:T(8,128)(2,1)S(1)}, bf16[512,2048]{1,0:T(8,128)(2,1)S(1)}, u32[]{:S(2)}, u32[]{:S(2)}) collective-permute-start(bf16[512,2048]{1,0:T(8,128)(2,1)S(1)} %get-tuple-element.581), channel_id=1, source_target_pairs={{0,4},{4,0},{8,12},{12,8},{16,20},{20,16},{24,28},{28,24},{32,36},... | collective-permute-start | bytes 6291464 | tf_op jit(solution)/shard_map/ppermute | solution.py:27
  94.2 16.1 %collective-permute-start.18 = (bf16[320,512]{1,0:T(8,128)(2,1)S(1)}, bf16[320,512]{1,0:T(8,128)(2,1)S(1)}, u32[]{:S(2)}, u32[]{:S(2)}) collective-permute-start(bf16[320,512]{1,0:T(8,128)(2,1)S(1)} %get-tuple-element.590.left_a), channel_id=1, source_target_pairs={{0,48},{4,52},{8,56},{12,60},{16,32},{20,36},{24,40},{28,44},{32,1... | collective-permute-start | bytes 983048 | tf_op jit(solution)/shard_map/ppermute | solution.py:27
  95.6 14.6 %collective-permute-start.19 = (bf16[320,512]{1,0:T(8,128)(2,1)S(1)}, bf16[320,512]{1,0:T(8,128)(2,1)S(1)}, u32[]{:S(2)}, u32[]{:S(2)}) collective-permute-start(bf16[320,512]{1,0:T(8,128)(2,1)S(1)} %get-tuple-element.591.left_b), channel_id=1, source_target_pairs={{0,16},{4,20},{8,24},{12,28},{16,0},{20,4},{24,8},{28,12},{32,48},... | collective-permute-start | bytes 983048 | tf_op jit(solution)/shard_map/ppermute | solution.py:27
  110.7 15.3 %collective-permute-start.23 = (bf16[320,1024]{1,0:T(8,128)(2,1)S(1)}, bf16[320,1024]{1,0:T(8,128)(2,1)S(1)}, u32[]{:S(2)}, u32[]{:S(2)}) collective-permute-start(bf16[320,1024]{1,0:T(8,128)(2,1)S(1)} %get-tuple-element.616), channel_id=1, source_target_pairs={{0,16},{4,20},{8,24},{12,28},{16,0},{20,4},{24,8},{28,12},{32,48},... | collective-permute-start | bytes 1966088 | tf_op jit(solution)/shard_map/ppermute | solution.py:27
  110.8 16.3 %collective-permute-start.24 = (bf16[320,1024]{1,0:T(8,128)(2,1)S(1)}, bf16[320,1024]{1,0:T(8,128)(2,1)S(1)}, u32[]{:S(2)}, u32[]{:S(2)}) collective-permute-start(bf16[320,1024]{1,0:T(8,128)(2,1)S(1)} %get-tuple-element.617), channel_id=1, source_target_pairs={{0,48},{4,52},{8,56},{12,60},{16,32},{20,36},{24,40},{28,44},{32,1... | collective-permute-start | bytes 1966088 | tf_op jit(solution)/shard_map/ppermute | solution.py:27
  112.3 14.8 %collective-permute-start.25 = (bf16[640,512]{1,0:T(8,128)(2,1)S(1)}, bf16[640,512]{1,0:T(8,128)(2,1)S(1)}, u32[]{:S(2)}, u32[]{:S(2)}) collective-permute-start(bf16[640,512]{1,0:T(8,128)(2,1)S(1)} %shard_map.88.refs_0_), channel_id=1, source_target_pairs={{0,8},{4,12},{8,0},{12,4},{16,24},{20,28},{24,16},{28,20},{32,40},... | collective-permute-start | bytes 1966088 | tf_op jit(solution)/shard_map/ppermute | solution.py:27
  113.3 15.6 %collective-permute-start.26 = (bf16[2,128,1280]{2,1,0:T(8,128)(2,1)S(1)}, bf16[2,128,1280]{2,1,0:T(8,128)(2,1)S(1)}, u32[]{:S(2)}, u32[]{:S(2)}) collective-permute-start(bf16[2,128,1280]{2,1,0:T(8,128)(2,1)S(1)} %get-tuple-element.640), channel_id=1, source_target_pairs={{0,1},{1,2},{2,3},{3,0},{4,5},{5,6},{6,7},{7,4},{8,9},{9,10},{10,1... | collective-permute-start | bytes 1966088 | tf_op jit(solution)/shard_map/ppermute | solution.py:31
  114.1 14.8 %collective-permute-start.27 = (bf16[2,128,1280]{2,1,0:T(8,128)(2,1)S(1)}, bf16[2,128,1280]{2,1,0:T(8,128)(2,1)S(1)}, u32[]{:S(2)}, u32[]{:S(2)}) collective-permute-start(bf16[2,128,1280]{2,1,0:T(8,128)(2,1)S(1)} %get-tuple-element.642), channel_id=1, source_target_pairs={{0,3},{1,0},{2,1},{3,2},{4,7},{5,4},{6,5},{7,6},{8,11},{9,8},{10,9... | collective-permute-start | bytes 1966088 | tf_op jit(solution)/shard_map/ppermute | solution.py:31
  128.9 16.5 %collective-permute-start.28 = (bf16[640,1024]{1,0:T(8,128)(2,1)S(1)}, bf16[640,1024]{1,0:T(8,128)(2,1)S(1)}, u32[]{:S(2)}, u32[]{:S(2)}) collective-permute-start(bf16[640,1024]{1,0:T(8,128)(2,1)S(1)} %get-tuple-element.692.refs_0_), channel_id=1, source_target_pairs={{0,4},{4,0},{8,12},{12,8},{16,20},{20,16},{24,28},{28,24},{32,36},... | collective-permute-start | bytes 3932168 | tf_op jit(solution)/shard_map/ppermute | solution.py:27
  131.7 13.7 %collective-permute-start.32 = (bf16[640,1024]{1,0:T(8,128)(2,1)S(1)}, bf16[640,1024]{1,0:T(8,128)(2,1)S(1)}, u32[]{:S(2)}, u32[]{:S(2)}) collective-permute-start(bf16[640,1024]{1,0:T(8,128)(2,1)S(1)} %shard_map.91.refs_2_), channel_id=1, source_target_pairs={{0,4},{4,0},{8,12},{12,8},{16,20},{20,16},{24,28},{28,24},{32,36},... | collective-permute-start | bytes 3932168 | tf_op jit(solution)/shard_map/ppermute | solution.py:27
  131.7 13.7 %collective-permute-start.29 = (bf16[112,2048]{1,0:T(8,128)(2,1)S(1)}, bf16[112,2048]{1,0:T(8,128)(2,1)S(1)}, u32[]{:S(2)}, u32[]{:S(2)}) collective-permute-start(bf16[112,2048]{1,0:T(8,128)(2,1)S(1)} %get-tuple-element.647), channel_id=1, source_target_pairs={{0,64},{64,0},{1,65},{65,1},{2,66},{66,2},{3,67},{67,3},{4,68},{68... | collective-permute-start | bytes 1376264 | tf_op jit(solution)/shard_map/ppermute | solution.py:35
  146.7 17.8 %collective-permute-start.34 = (bf16[320,1024]{1,0:T(8,128)(2,1)S(1)}, bf16[320,1024]{1,0:T(8,128)(2,1)S(1)}, u32[]{:S(2)}, u32[]{:S(2)}) collective-permute-start(bf16[320,1024]{1,0:T(8,128)(2,1)S(1)} %get-tuple-element.685), channel_id=1, source_target_pairs={{0,16},{4,20},{8,24},{12,28},{16,0},{20,4},{24,8},{28,12},{32,48},... | collective-permute-start | bytes 1966088 | tf_op jit(solution)/shard_map/ppermute | solution.py:27
  147.5 17.2 %collective-permute-start.35 = (bf16[320,1024]{1,0:T(8,128)(2,1)S(1)}, bf16[320,1024]{1,0:T(8,128)(2,1)S(1)}, u32[]{:S(2)}, u32[]{:S(2)}) collective-permute-start(bf16[320,1024]{1,0:T(8,128)(2,1)S(1)} %get-tuple-element.686), channel_id=1, source_target_pairs={{0,48},{4,52},{8,56},{12,60},{16,32},{20,36},{24,40},{28,44},{32,1... | collective-permute-start | bytes 1966088 | tf_op jit(solution)/shard_map/ppermute | solution.py:27
  148.8 15.7 %collective-permute-start.33 = (bf16[144,2048]{1,0:T(8,128)(2,1)S(1)}, bf16[144,2048]{1,0:T(8,128)(2,1)S(1)}, u32[]{:S(2)}, u32[]{:S(2)}) collective-permute-start(bf16[144,2048]{1,0:T(8,128)(2,1)S(1)} %get-tuple-element.683), channel_id=1, source_target_pairs={{0,64},{64,0},{1,65},{65,1},{2,66},{66,2},{3,67},{67,3},{4,68},{68... | collective-permute-start | bytes 1769480 | tf_op jit(solution)/shard_map/ppermute | solution.py:35
  (21 other events, 123.3 us)

commit v5 on v4

--- a/solution.py
+++ b/solution.py
@@ -72,12 +72,12 @@
     )(*operands)
 
 
-def prepare(features, cotangent, gain, bias):
+def prepare(features, cotangent):
     _, rows, width = features.shape
     _, tokens, cols = cotangent.shape
     part = cols // 4
 
-    def kernel(features, cotangent, gain, bias, ours_out, theirs_out, mine_out, scale_out, index_out, sems):
+    def kernel(features, cotangent, ours_out, theirs_out, mine_out, index_out, sems):
         s, d, x = lax.axis_index("section"), lax.axis_index("dp"), lax.axis_index("tensor")
         y, c = d // 4, d % 2
         around = (y, y + 1 - 2 * (y % 2), (y + 2) % 4, 3 - y)
@@ -93,16 +93,14 @@
             index_out[SLOT_OF + t] = (s if t < 2 else 1 - s) * 2 + t % 2
         for n, t in enumerate((x, (x + 1) % 4, (x + 3) % 4, (x + 2) % 4)):
             index_out[SLOTS + n] = ((t // 2 + s) % 2) * 2 + t % 2
-        scale_out[0:1] = gain[pl.ds(c, 1)]
-        scale_out[1:2] = bias[pl.ds(c, 1)]
         wait(copies.all)
 
     return call(
         kernel,
-        [features, cotangent, gain, bias],
-        [ANY, ANY, VMEM, VMEM],
-        [out(rows, width), out(rows, width), out(tokens, cols), out(2, width, dtype=F32), out(13, dtype=jnp.int32)],
-        [VMEM, VMEM, VMEM, VMEM, SMEM],
+        [features, cotangent],
+        [ANY, ANY],
+        [out(rows, width), out(rows, width), out(tokens, cols), out(13, dtype=jnp.int32)],
+        [VMEM, VMEM, VMEM, SMEM],
         [pltpu.SemaphoreType.DMA((6,))],
     )
 
@@ -148,11 +146,11 @@
     return centered * inverse, inverse
 
 
-def normalize(ours, theirs, scale):
+def normalize(index, ours, theirs, gain, bias):
     rows = ours.shape[0]
 
-    def kernel(ours, theirs, scale, *outs):
-        gain, bias = scale[0:1], scale[1:2]
+    def kernel(index, ours, theirs, gain, bias, *outs):
+        gain, bias = gain[pl.ds(index[0], 1)], bias[pl.ds(index[0], 1)]
         for k, value in enumerate((ours, theirs)):
             standard, _ = moments(value[...].astype(F32))
             normed = (standard * gain + bias).astype(BF16)
@@ -160,14 +158,14 @@
                 out_ref[k] = normed[:, start : start + size]
 
     shapes = [out(2, rows, size) for _, size in ROW_CHUNKS]
-    return call(kernel, [ours, theirs, scale], [VMEM] * 3, shapes, [VMEM] * len(shapes))
-
-
-def normalize_backward(ours, theirs, scale, parts):
+    return call(kernel, [index, ours, theirs, gain, bias], [SMEM] + [VMEM] * 4, shapes, [VMEM] * len(shapes))
+
+
+def normalize_backward(index, ours, theirs, gain, parts):
     count = len(parts)
 
-    def kernel(ours, theirs, scale, *refs):
-        gain = scale[0:1]
+    def kernel(index, ours, theirs, gain, *refs):
+        gain = gain[pl.ds(index[0], 1)]
         for k, value in enumerate((ours, theirs)):
             standard, inverse = moments(value[...].astype(F32))
             total = refs[0][k].astype(F32)
@@ -182,7 +180,7 @@
             refs[count + k][...] = hidden.astype(BF16)
 
     shapes = [out(*ours.shape)] * 2
-    return call(kernel, [ours, theirs, scale, *parts], [VMEM] * (3 + count), shapes, [VMEM] * 2)
+    return call(kernel, [index, ours, theirs, gain, *parts], [SMEM] + [VMEM] * (3 + count), shapes, [VMEM] * 2)
 
 
 def both_taps(index, ours, theirs):
@@ -418,16 +416,14 @@
                     pieces.append((array, 0, n > 1, n % 2, places[n % 2]))
         return place(v.index, pieces, ROW_CHUNKS[t][0], width, cols, into)
 
-    v.ours, v.theirs, v.mine, v.scale, v.index = prepare(
-        features, cotangent, layer_norm_gain, layer_norm_bias
-    )
+    v.ours, v.theirs, v.mine, v.index = prepare(features, cotangent)
     v.end()
 
     away = to_section(v.mine)
     rows = swap(v.theirs, CORE)
     mine_c = swap(v.mine, CORE)
     v.rows = rows
-    v.n0, v.n1 = normalize(v.ours, v.rows, v.scale)
+    v.n0, v.n1 = normalize(v.index, v.ours, v.rows, layer_norm_gain, layer_norm_bias)
     v.mine_c = mine_c
     del v.theirs
     v.end()
@@ -440,8 +436,7 @@
     v.end()
 
     away_c = swap(v.away, CORE)
-    x11 = along_x(v.n1, -1)
-    x13 = along_x(v.n1, -3)
+    x12 = along_x(v.n1, -2)
     v.away_c = away_c
     v.end()
 
@@ -449,14 +444,15 @@
     v.send_a0, v.send_b0, v.next_a0, v.next_b0, v.keep_a0, v.keep_b0 = weight_grad_blocks(
         v.index, near0, grads(), wanted
     )
-    v.x11, v.x13 = x11, x13
+    v.x12 = x12
     v.end()
 
     got_a0 = swap(v.send_a0, Y1)
     got_b0 = swap(v.send_b0, Y3)
-    x12 = along_x(v.n1, -2)
+    x11 = along_x(v.n1, -1)
+    x13 = along_x(v.n1, -3)
     v.r0, v.r1, v.r3, v.r2 = row_gradients(v.index, grads(), v.weight)
-    v.got_a0, v.got_b0, v.x12 = got_a0, got_b0, x12
+    v.got_a0, v.got_b0, v.x11, v.x13 = got_a0, got_b0, x11, x13
     del v.send_a0, v.send_b0
     v.end()
 
@@ -533,7 +529,7 @@
     ab0_c = swap(v.ab0, CORE)
     lab0_c = swap(v.lab0, CORE)
     v.own_rows, v.hidden = normalize_backward(
-        v.ours, v.rows, v.scale, [v.r0, v.s1, v.s3, v.s2]
+        v.index, v.ours, v.rows, layer_norm_gain, [v.r0, v.s1, v.s3, v.s2]
     )
     v.ga1, v.gb1, v.ab0_c, v.lab0_c, v.back0 = ga1, gb1, ab0_c, lab0_c, back0
     del v.up0, v.r0, v.s1, v.s3, v.s2

time: 171 us -> 171 us (level)
  waiting for transfers between devices: 70.3 us -> 67.1 us
  starting transfers between devices: 54.5 us -> 56.7 us
    ppermute x3, waiting for transfers between devices: 16.2 us -> 14.2 us  [to_section(): return lax.ppermute(value, 'section', [(0, 1), (1, 0)])]
    ppermute x9, starting transfers between devices: 13.9 us -> 15.7 us  [along_x(): lax.ppermute(value, 'tensor', [(i, (i + step) % 4) for i in range(4)])]
    unnamed x10 -> x12, local copies, waits for them, and re-layouts: 7.69 us -> 7.69 us
  transfers between devices with their start and end apart: 40 -> 40, of which waited for: 22 -> 22; matrix products, arithmetic and copies ran while one was open for 0% -> 0% of each run, Pallas kernels for 19% -> 20%
where the time goes in v5:
time: 171 us
  waiting for transfers between devices  67.1 us (39%)
  starting transfers between devices  56.7 us (33%)
  Pallas kernels  38.5 us (23%)
  local copies, waits for them, and re-layouts  7.69 us (4%)
    ppermute x28, waiting for transfers between devices, swap(): return lax.ppermute(value, 'dp', pairs)  45.6 us
    pallas_call x23, Pallas kernels, call(): pl.pallas_call(kernel, in_specs=in_specs, out_specs=out_specs, out_shape=...  38.5 us
    ppermute x28, starting transfers between devices, swap(): return lax.ppermute(value, 'dp', pairs)  31 us
    ppermute x9, starting transfers between devices, along_x(): lax.ppermute(value, 'tensor', [(i, (i + step) % 4) for i in range(4)])  15.7 us
    ppermute x3, waiting for transfers between devices, to_section(): return lax.ppermute(value, 'section', [(0, 1), (1, 0)])  14.2 us
    ppermute x3, starting transfers between devices, to_section(): return lax.ppermute(value, 'section', [(0, 1), (1, 0)])  9.96 us
    unnamed x12, local copies, waits for them, and re-layouts  7.69 us
    ppermute x9, waiting for transfers between devices, along_x(): lax.ppermute(value, 'tensor', [(i, (i + step) % 4) for i in range(4)])  7.25 us
  transfers between devices with their start and end apart: 40, of which 22 were waited for; matrix products, arithmetic and copies ran while one was open for 0% of the time, Pallas kernels for 20%

profile of v5, /device:TPU:1, one launch (start us, length us, event | category | flops | bytes accessed | tf_op | source)
XLA Modules:
  0.0 171.1 jit_solution(8843916925059949063)
XLA Ops:
  5.5 3.7 %collective-permute-start = (bf16[256,2048]{1,0:T(8,128)(2,1)S(1)}, bf16[256,2048]{1,0:T(8,128)(2,1)S(1)}, u32[]{:S(2)}, u32[]{:S(2)}) collective-permute-start(bf16[256,2048]{1,0:T(8,128)(2,1)S(1)} %get-tuple-element.445.refs_4_.refs_0_), channel_id=1, source_target_pairs={{0,64},{64,0},{1,65},{65,1},{2,66},{66,2},{3,67},{67,3},{4,68},{68... | collective-permute-start | bytes 3145736 | tf_op jit(solution)/shard_map/ppermute | solution.py:35
  14.5 2.5 %collective-permute-start.4 = (bf16[2,128,640]{2,1,0:T(8,128)(2,1)S(1)}, bf16[2,128,640]{2,1,0:T(8,128)(2,1)S(1)}, u32[]{:S(2)}, u32[]{:S(2)}) collective-permute-start(bf16[2,128,640]{2,1,0:T(8,128)(2,1)S(1)} %get-tuple-element.505.refs_0_), channel_id=1, source_target_pairs={{0,2},{1,3},{2,0},{3,1},{4,6},{5,7},{6,4},{7,5},{8,10},{9,11},{10,... | collective-permute-start | bytes 983048 | tf_op jit(solution)/shard_map/ppermute | solution.py:31
  18.1 4.0 %copy-done = bf16[2560,2048]{1,0:T(8,128)(2,1)S(1)} copy-done((bf16[2560,2048]{1,0:T(8,128)(2,1)S(1)}, bf16[2560,2048]{1,0:T(8,128)(2,1)}, u32[]{:S(2)}) %copy-start) | copy-done | bytes 10485784
  24.4 8.2 %collective-permute-done.refs_5_.refs_1_ = bf16[256,2048]{1,0:T(8,128)(2,1)S(1)} collective-permute-done((bf16[256,2048]{1,0:T(8,128)(2,1)S(1)}, bf16[256,2048]{1,0:T(8,128)(2,1)S(1)}, u32[]{:S(2)}, u32[]{:S(2)}) %collective-permute-start) | collective-permute-done | bytes 1048608 | tf_op jit(solution)/shard_map/ppermute | solution.py:35
  33.3 2.8 %collective-permute-start.7 = (bf16[2,128,640]{2,1,0:T(8,128)(2,1)S(1)}, bf16[2,128,640]{2,1,0:T(8,128)(2,1)S(1)}, u32[]{:S(2)}, u32[]{:S(2)}) collective-permute-start(bf16[2,128,640]{2,1,0:T(8,128)(2,1)S(1)} %get-tuple-element.509.refs_0_.refs_4_), channel_id=1, source_target_pairs={{0,2},{1,3},{2,0},{3,1},{4,6},{5,7},{6,4},{7,5},{8,10},{9,11},{10,... | collective-permute-start | bytes 983048 | tf_op jit(solution)/shard_map/ppermute | solution.py:31
  36.1 3.9 %shard_map.79 = (bf16[320,1024]{1,0:T(8,128)(2,1)S(1)}, bf16[320,1024]{1,0:T(8,128)(2,1)S(1)}, bf16[320,512]{1,0:T(8,128)(2,1)S(1)}, bf16[320,512]{1,0:T(8,128)(...) custom-call(s32[13]{0:T(128)S(1)} %get-tuple-element.666.index, ...), custom_call_target="tpu_custom_call" | custom-call | flops 1 | bytes 1 | tf_op jit(solution)/shard_map/pallas_call | solution.py:63
  40.0 4.1 %collective-permute-done.7.refs_3_.refs_7_ = bf16[2,128,640]{2,1,0:T(8,128)(2,1)S(1)} collective-permute-done((bf16[2,128,640]{2,1,0:T(8,128)(2,1)S(1)}, bf16[2,128,640]{2,1,0:T(8,128)(2,1)S(1)}, u32[]{:S(2)}, u32[]{:S(2)}) %collective-permute-start.7) | collective-permute-done | bytes 327712 | tf_op jit(solution)/shard_map/ppermute | solution.py:31
  50.0 6.8 %shard_map.80 = (bf16[2,128,1280]{2,1,0:T(8,128)(2,1)S(1)}, bf16[2,128,1280]{2,1,0:T(8,128)(2,1)S(1)}, bf16[2,128,1280]{2,1,0:T(8,128)(2,1)S(1)}, bf16[2,128,1280]{2,1,0:T(8,128)(2,1)S(1)}) custom-call(s32[13]{0:T(128)S(1)} %get-tuple-element.666.index, bf16[256,2048]{1,0:T(8,128)(2,1)S(1)} %get-tuple-element.445.refs_4_.refs_0_, ...), custom_call_target="tpu_custom_call" | custom-call | flops 1 | bytes 1 | tf_op jit(solution)/shard_map/pallas_call | solution.py:63
  56.8 2.7 %collective-permute-done.8.refs_1_ = bf16[320,1024]{1,0:T(8,128)(2,1)S(1)} collective-permute-done((bf16[320,1024]{1,0:T(8,128)(2,1)S(1)}, bf16[320,1024]{1,0:T(8,128)(2,1)S(1)}, u32[]{:S(2)}, u32[]{:S(2)}) %collective-permute-start.8) | collective-permute-done | bytes 655392 | tf_op jit(solution)/shard_map/ppermute | solution.py:27
  63.8 3.9 %shard_map.82 = (bf16[320,1024]{1,0:T(8,128)(2,1)S(1)}, bf16[320,1024]{1,0:T(8,128)(2,1)S(1)}, bf16[320,512]{1,0:T(8,128)(2,1)S(1)}, bf16[320,512]{1,0:T(8,128)(...) custom-call(s32[13]{0:T(128)S(1)} %get-tuple-element.666.index, ...), custom_call_target="tpu_custom_call" | custom-call | flops 1 | bytes 1 | tf_op jit(solution)/shard_map/pallas_call | solution.py:63
  67.7 2.6 %collective-permute-done.12.refs_2_ = bf16[320,512]{1,0:T(8,128)(2,1)S(1)} collective-permute-done((bf16[320,512]{1,0:T(8,128)(2,1)S(1)}, bf16[320,512]{1,0:T(8,128)(2,1)S(1)}, u32[]{:S(2)}, u32[]{:S(2)}) %collective-permute-start.12) | collective-permute-done | bytes 327712 | tf_op jit(solution)/shard_map/ppermute | solution.py:27
  72.6 2.7 %collective-permute-start.17 = (bf16[2,128,1280]{2,1,0:T(8,128)(2,1)S(1)}, bf16[2,128,1280]{2,1,0:T(8,128)(2,1)S(1)}, u32[]{:S(2)}, u32[]{:S(2)}) collective-permute-start(bf16[2,128,1280]{2,1,0:T(8,128)(2,1)S(1)} %get-tuple-element.521), channel_id=1, source_target_pairs={{0,2},{1,3},{2,0},{3,1},{4,6},{5,7},{6,4},{7,5},{8,10},{9,11},{10,... | collective-permute-start | bytes 1966088 | tf_op jit(solution)/shard_map/ppermute | solution.py:31
  76.3 6.3 %shard_map.84 = (bf16[512,2048]{1,0:T(8,128)(2,1)S(1)}, bf16[512,2048]{1,0:T(8,128)(2,1)S(1)}) custom-call(s32[13]{0:T(128)S(1)} %get-tuple-element.666.index, bf16[2,128,640]{2,1,0:T(8,128)(2,1)S(1)} %get-tuple-element.505.refs_0_, bf16[2,128,640]{2,1,0:T(8,128)(2,1)S(1)} %collective-permute-done.3.refs_1_, ...), custom_call_target="tpu_custom_call" | custom-call | flops 1 | bytes 1 | tf_op jit(solution)/shard_map/pallas_call | solution.py:63
  88.3 4.6 %collective-permute-start.22 = (bf16[512,2048]{1,0:T(8,128)(2,1)S(1)}, bf16[512,2048]{1,0:T(8,128)(2,1)S(1)}, u32[]{:S(2)}, u32[]{:S(2)}) collective-permute-start(bf16[512,2048]{1,0:T(8,128)(2,1)S(1)} %get-tuple-element.552), channel_id=1, source_target_pairs={{0,4},{4,0},{8,12},{12,8},{16,20},{20,16},{24,28},{28,24},{32,36},... | collective-permute-start | bytes 6291464 | tf_op jit(solution)/shard_map/ppermute | solution.py:27
  96.4 6.9 %collective-permute-done.20.refs_2_ = bf16[320,512]{1,0:T(8,128)(2,1)S(1)} collective-permute-done((bf16[320,512]{1,0:T(8,128)(2,1)S(1)}, bf16[320,512]{1,0:T(8,128)(2,1)S(1)}, u32[]{:S(2)}, u32[]{:S(2)}) %collective-permute-start.20) | collective-permute-done | bytes 327712 | tf_op jit(solution)/shard_map/ppermute | solution.py:27
  103.4 7.0 %collective-permute-done.18.right_a = bf16[320,512]{1,0:T(8,128)(2,1)S(1)} collective-permute-done((bf16[320,512]{1,0:T(8,128)(2,1)S(1)}, bf16[320,512]{1,0:T(8,128)(2,1)S(1)}, u32[]{:S(2)}, u32[]{:S(2)}) %collective-permute-start.18) | collective-permute-done | bytes 327712 | tf_op jit(solution)/shard_map/ppermute | solution.py:27
  113.7 2.4 %collective-permute-start.27 = (bf16[2,128,1280]{2,1,0:T(8,128)(2,1)S(1)}, bf16[2,128,1280]{2,1,0:T(8,128)(2,1)S(1)}, u32[]{:S(2)}, u32[]{:S(2)}) collective-permute-start(bf16[2,128,1280]{2,1,0:T(8,128)(2,1)S(1)} %get-tuple-element.610), channel_id=1, source_target_pairs={{0,3},{1,0},{2,1},{3,2},{4,7},{5,4},{6,5},{7,6},{8,11},{9,8},{10,9... | collective-permute-start | bytes 1966088 | tf_op jit(solution)/shard_map/ppermute | solution.py:31
  116.3 9.8 %collective-permute-done.23.top = bf16[320,1024]{1,0:T(8,128)(2,1)S(1)} collective-permute-done((bf16[320,1024]{1,0:T(8,128)(2,1)S(1)}, bf16[320,1024]{1,0:T(8,128)(2,1)S(1)}, u32[]{:S(2)}, u32[]{:S(2)}) %collective-permute-start.23) | collective-permute-done | bytes 655392 | tf_op jit(solution)/shard_map/ppermute | solution.py:27
  128.9 2.8 %collective-permute-start.28 = (bf16[640,1024]{1,0:T(8,128)(2,1)S(1)}, bf16[640,1024]{1,0:T(8,128)(2,1)S(1)}, u32[]{:S(2)}, u32[]{:S(2)}) collective-permute-start(bf16[640,1024]{1,0:T(8,128)(2,1)S(1)} %get-tuple-element.658.refs_0_), channel_id=1, source_target_pairs={{0,4},{4,0},{8,12},{12,8},{16,20},{20,16},{24,28},{28,24},{32,36},... | collective-permute-start | bytes 3932168 | tf_op jit(solution)/shard_map/ppermute | solution.py:27
  131.7 3.3 %collective-permute-start.29 = (bf16[112,2048]{1,0:T(8,128)(2,1)S(1)}, bf16[112,2048]{1,0:T(8,128)(2,1)S(1)}, u32[]{:S(2)}, u32[]{:S(2)}) collective-permute-start(bf16[112,2048]{1,0:T(8,128)(2,1)S(1)} %get-tuple-element.614), channel_id=1, source_target_pairs={{0,64},{64,0},{1,65},{65,1},{2,66},{66,2},{3,67},{67,3},{4,68},{68... | collective-permute-start | bytes 1376264 | tf_op jit(solution)/shard_map/ppermute | solution.py:35
  138.2 6.5 %collective-permute-done.30.right_a = bf16[320,512]{1,0:T(8,128)(2,1)S(1)} collective-permute-done((bf16[320,512]{1,0:T(8,128)(2,1)S(1)}, bf16[320,512]{1,0:T(8,128)(2,1)S(1)}, u32[]{:S(2)}, u32[]{:S(2)}) %collective-permute-start.30) | collective-permute-done | bytes 327712 | tf_op jit(solution)/shard_map/ppermute | solution.py:27
  148.9 3.0 %collective-permute-start.33 = (bf16[144,2048]{1,0:T(8,128)(2,1)S(1)}, bf16[144,2048]{1,0:T(8,128)(2,1)S(1)}, u32[]{:S(2)}, u32[]{:S(2)}) collective-permute-start(bf16[144,2048]{1,0:T(8,128)(2,1)S(1)} %get-tuple-element.649), channel_id=1, source_target_pairs={{0,64},{64,0},{1,65},{65,1},{2,66},{66,2},{3,67},{67,3},{4,68},{68... | collective-permute-start | bytes 1769480 | tf_op jit(solution)/shard_map/ppermute | solution.py:35
  152.8 3.0 %shard_map.95.refs_2_ = bf16[2560,2048]{1,0:T(8,128)(2,1)} custom-call(s32[13]{0:T(128)S(1)} %get-tuple-element.666.index, bf16[640,1024]{1,0:T(8,128)(2,1)S(1)} %get-tuple-element.658.refs_0_, bf16[640,1024]{1,0:T(8,128)(2,1)S(1)} %collective-permute-done.28.refs_1_, bf16[640,1024]{1,0:T(8,128)(2,1)S(1)} %shard_map.91.refs_2_, ...), custom_call_target="tpu_custom_call" | custom-call | flops 1 | bytes 1 | tf_op jit(solution)/shard_map/pallas_call | solution.py:63
  159.3 5.3 %collective-permute-done.33.refs_3_ = bf16[144,2048]{1,0:T(8,128)(2,1)S(1)} collective-permute-done((bf16[144,2048]{1,0:T(8,128)(2,1)S(1)}, bf16[144,2048]{1,0:T(8,128)(2,1)S(1)}, u32[]{:S(2)}, u32[]{:S(2)}) %collective-permute-start.33) | collective-permute-done | bytes 589856 | tf_op jit(solution)/shard_map/ppermute | solution.py:35
  (91 shorter events, 61.4 us)
Async XLA Ops:
  5.5 27.1 %collective-permute-start = (bf16[256,2048]{1,0:T(8,128)(2,1)S(1)}, bf16[256,2048]{1,0:T(8,128)(2,1)S(1)}, u32[]{:S(2)}, u32[]{:S(2)}) collective-permute-start(bf16[256,2048]{1,0:T(8,128)(2,1)S(1)} %get-tuple-element.445.refs_4_.refs_0_), channel_id=1, source_target_pairs={{0,64},{64,0},{1,65},{65,1},{2,66},{66,2},{3,67},{67,3},{4,68},{68... | collective-permute-start | bytes 3145736 | tf_op jit(solution)/shard_map/ppermute | solution.py:35
  13.2 19.3 %collective-permute-start.5 = (bf16[2,128,640]{2,1,0:T(8,128)(2,1)S(1)}, bf16[2,128,640]{2,1,0:T(8,128)(2,1)S(1)}, u32[]{:S(2)}, u32[]{:S(2)}) collective-permute-start(bf16[2,128,640]{2,1,0:T(8,128)(2,1)S(1)} %get-tuple-element.505.refs_0_), channel_id=1, source_target_pairs={{0,1},{1,2},{2,3},{3,0},{4,5},{5,6},{6,7},{7,4},{8,9},{9,10},{10,1... | collective-permute-start | bytes 983048 | tf_op jit(solution)/shard_map/ppermute | solution.py:31
  14.5 18.1 %collective-permute-start.4 = (bf16[2,128,640]{2,1,0:T(8,128)(2,1)S(1)}, bf16[2,128,640]{2,1,0:T(8,128)(2,1)S(1)}, u32[]{:S(2)}, u32[]{:S(2)}) collective-permute-start(bf16[2,128,640]{2,1,0:T(8,128)(2,1)S(1)} %get-tuple-element.505.refs_0_), channel_id=1, source_target_pairs={{0,2},{1,3},{2,0},{3,1},{4,6},{5,7},{6,4},{7,5},{8,10},{9,11},{10,... | collective-permute-start | bytes 983048 | tf_op jit(solution)/shard_map/ppermute | solution.py:31
  17.0 15.6 %collective-permute-start.3 = (bf16[2,128,640]{2,1,0:T(8,128)(2,1)S(1)}, bf16[2,128,640]{2,1,0:T(8,128)(2,1)S(1)}, u32[]{:S(2)}, u32[]{:S(2)}) collective-permute-start(bf16[2,128,640]{2,1,0:T(8,128)(2,1)S(1)} %get-tuple-element.505.refs_0_), channel_id=1, source_target_pairs={{0,3},{1,0},{2,1},{3,2},{4,7},{5,4},{6,5},{7,6},{8,11},{9,8},{10,9... | collective-permute-start | bytes 983048 | tf_op jit(solution)/shard_map/ppermute | solution.py:31
  44.1 15.4 %collective-permute-start.8 = (bf16[320,1024]{1,0:T(8,128)(2,1)S(1)}, bf16[320,1024]{1,0:T(8,128)(2,1)S(1)}, u32[]{:S(2)}, u32[]{:S(2)}) collective-permute-start(bf16[320,1024]{1,0:T(8,128)(2,1)S(1)} %get-tuple-element.387), channel_id=1, source_target_pairs={{0,16},{4,20},{8,24},{12,28},{16,0},{20,4},{24,8},{28,12},{32,48},... | collective-permute-start | bytes 1966088 | tf_op jit(solution)/shard_map/ppermute | solution.py:27
  45.4 16.3 %collective-permute-start.9 = (bf16[320,1024]{1,0:T(8,128)(2,1)S(1)}, bf16[320,1024]{1,0:T(8,128)(2,1)S(1)}, u32[]{:S(2)}, u32[]{:S(2)}) collective-permute-start(bf16[320,1024]{1,0:T(8,128)(2,1)S(1)} %get-tuple-element.388), channel_id=1, source_target_pairs={{0,48},{4,52},{8,56},{12,60},{16,32},{20,36},{24,40},{28,44},{32,1... | collective-permute-start | bytes 1966088 | tf_op jit(solution)/shard_map/ppermute | solution.py:27
  70.9 13.0 %collective-permute-start.14 = (bf16[320,1024]{1,0:T(8,128)(2,1)S(1)}, bf16[320,1024]{1,0:T(8,128)(2,1)S(1)}, u32[]{:S(2)}, u32[]{:S(2)}) collective-permute-start(bf16[320,1024]{1,0:T(8,128)(2,1)S(1)} %get-tuple-element.497), channel_id=1, source_target_pairs={{0,16},{4,20},{8,24},{12,28},{16,0},{20,4},{24,8},{28,12},{32,48},... | collective-permute-start | bytes 1966088 | tf_op jit(solution)/shard_map/ppermute | solution.py:27
  71.3 14.2 %collective-permute-start.15 = (bf16[320,1024]{1,0:T(8,128)(2,1)S(1)}, bf16[320,1024]{1,0:T(8,128)(2,1)S(1)}, u32[]{:S(2)}, u32[]{:S(2)}) collective-permute-start(bf16[320,1024]{1,0:T(8,128)(2,1)S(1)} %get-tuple-element.498), channel_id=1, source_target_pairs={{0,48},{4,52},{8,56},{12,60},{16,32},{20,36},{24,40},{28,44},{32,1... | collective-permute-start | bytes 1966088 | tf_op jit(solution)/shard_map/ppermute | solution.py:27
  72.6 14.5 %collective-permute-start.17 = (bf16[2,128,1280]{2,1,0:T(8,128)(2,1)S(1)}, bf16[2,128,1280]{2,1,0:T(8,128)(2,1)S(1)}, u32[]{:S(2)}, u32[]{:S(2)}) collective-permute-start(bf16[2,128,1280]{2,1,0:T(8,128)(2,1)S(1)} %get-tuple-element.521), channel_id=1, source_target_pairs={{0,2},{1,3},{2,0},{3,1},{4,6},{5,7},{6,4},{7,5},{8,10},{9,11},{10,... | collective-permute-start | bytes 1966088 | tf_op jit(solution)/shard_map/ppermute | solution.py:31
  75.3 12.7 %collective-permute-start.16 = (bf16[640,512]{1,0:T(8,128)(2,1)S(1)}, bf16[640,512]{1,0:T(8,128)(2,1)S(1)}, u32[]{:S(2)}, u32[]{:S(2)}) collective-permute-start(bf16[640,512]{1,0:T(8,128)(2,1)S(1)} %shard_map.83.refs_0_), channel_id=1, source_target_pairs={{0,8},{4,12},{8,0},{12,4},{16,24},{20,28},{24,16},{28,20},{32,40},... | collective-permute-start | bytes 1966088 | tf_op jit(solution)/shard_map/ppermute | solution.py:27
  88.3 22.1 %collective-permute-start.22 = (bf16[512,2048]{1,0:T(8,128)(2,1)S(1)}, bf16[512,2048]{1,0:T(8,128)(2,1)S(1)}, u32[]{:S(2)}, u32[]{:S(2)}) collective-permute-start(bf16[512,2048]{1,0:T(8,128)(2,1)S(1)} %get-tuple-element.552), channel_id=1, source_target_pairs={{0,4},{4,0},{8,12},{12,8},{16,20},{20,16},{24,28},{28,24},{32,36},... | collective-permute-start | bytes 6291464 | tf_op jit(solution)/shard_map/ppermute | solution.py:27
  94.3 16.1 %collective-permute-start.18 = (bf16[320,512]{1,0:T(8,128)(2,1)S(1)}, bf16[320,512]{1,0:T(8,128)(2,1)S(1)}, u32[]{:S(2)}, u32[]{:S(2)}) collective-permute-start(bf16[320,512]{1,0:T(8,128)(2,1)S(1)} %get-tuple-element.560.left_a), channel_id=1, source_target_pairs={{0,48},{4,52},{8,56},{12,60},{16,32},{20,36},{24,40},{28,44},{32,1... | collective-permute-start | bytes 983048 | tf_op jit(solution)/shard_map/ppermute | solution.py:27
  95.7 14.6 %collective-permute-start.19 = (bf16[320,512]{1,0:T(8,128)(2,1)S(1)}, bf16[320,512]{1,0:T(8,128)(2,1)S(1)}, u32[]{:S(2)}, u32[]{:S(2)}) collective-permute-start(bf16[320,512]{1,0:T(8,128)(2,1)S(1)} %get-tuple-element.561.left_b), channel_id=1, source_target_pairs={{0,16},{4,20},{8,24},{12,28},{16,0},{20,4},{24,8},{28,12},{32,48},... | collective-permute-start | bytes 983048 | tf_op jit(solution)/shard_map/ppermute | solution.py:27
  110.8 15.3 %collective-permute-start.23 = (bf16[320,1024]{1,0:T(8,128)(2,1)S(1)}, bf16[320,1024]{1,0:T(8,128)(2,1)S(1)}, u32[]{:S(2)}, u32[]{:S(2)}) collective-permute-start(bf16[320,1024]{1,0:T(8,128)(2,1)S(1)} %get-tuple-element.585), channel_id=1, source_target_pairs={{0,16},{4,20},{8,24},{12,28},{16,0},{20,4},{24,8},{28,12},{32,48},... | collective-permute-start | bytes 1966088 | tf_op jit(solution)/shard_map/ppermute | solution.py:27
  110.9 16.3 %collective-permute-start.24 = (bf16[320,1024]{1,0:T(8,128)(2,1)S(1)}, bf16[320,1024]{1,0:T(8,128)(2,1)S(1)}, u32[]{:S(2)}, u32[]{:S(2)}) collective-permute-start(bf16[320,1024]{1,0:T(8,128)(2,1)S(1)} %get-tuple-element.586), channel_id=1, source_target_pairs={{0,48},{4,52},{8,56},{12,60},{16,32},{20,36},{24,40},{28,44},{32,1... | collective-permute-start | bytes 1966088 | tf_op jit(solution)/shard_map/ppermute | solution.py:27
  112.3 14.8 %collective-permute-start.25 = (bf16[640,512]{1,0:T(8,128)(2,1)S(1)}, bf16[640,512]{1,0:T(8,128)(2,1)S(1)}, u32[]{:S(2)}, u32[]{:S(2)}) collective-permute-start(bf16[640,512]{1,0:T(8,128)(2,1)S(1)} %shard_map.88.refs_0_), channel_id=1, source_target_pairs={{0,8},{4,12},{8,0},{12,4},{16,24},{20,28},{24,16},{28,20},{32,40},... | collective-permute-start | bytes 1966088 | tf_op jit(solution)/shard_map/ppermute | solution.py:27
  113.4 15.6 %collective-permute-start.26 = (bf16[2,128,1280]{2,1,0:T(8,128)(2,1)S(1)}, bf16[2,128,1280]{2,1,0:T(8,128)(2,1)S(1)}, u32[]{:S(2)}, u32[]{:S(2)}) collective-permute-start(bf16[2,128,1280]{2,1,0:T(8,128)(2,1)S(1)} %get-tuple-element.608), channel_id=1, source_target_pairs={{0,1},{1,2},{2,3},{3,0},{4,5},{5,6},{6,7},{7,4},{8,9},{9,10},{10,1... | collective-permute-start | bytes 1966088 | tf_op jit(solution)/shard_map/ppermute | solution.py:31
  113.7 15.3 %collective-permute-start.27 = (bf16[2,128,1280]{2,1,0:T(8,128)(2,1)S(1)}, bf16[2,128,1280]{2,1,0:T(8,128)(2,1)S(1)}, u32[]{:S(2)}, u32[]{:S(2)}) collective-permute-start(bf16[2,128,1280]{2,1,0:T(8,128)(2,1)S(1)} %get-tuple-element.610), channel_id=1, source_target_pairs={{0,3},{1,0},{2,1},{3,2},{4,7},{5,4},{6,5},{7,6},{8,11},{9,8},{10,9... | collective-permute-start | bytes 1966088 | tf_op jit(solution)/shard_map/ppermute | solution.py:31
  128.9 16.5 %collective-permute-start.28 = (bf16[640,1024]{1,0:T(8,128)(2,1)S(1)}, bf16[640,1024]{1,0:T(8,128)(2,1)S(1)}, u32[]{:S(2)}, u32[]{:S(2)}) collective-permute-start(bf16[640,1024]{1,0:T(8,128)(2,1)S(1)} %get-tuple-element.658.refs_0_), channel_id=1, source_target_pairs={{0,4},{4,0},{8,12},{12,8},{16,20},{20,16},{24,28},{28,24},{32,36},... | collective-permute-start | bytes 3932168 | tf_op jit(solution)/shard_map/ppermute | solution.py:27
  131.7 13.7 %collective-permute-start.32 = (bf16[640,1024]{1,0:T(8,128)(2,1)S(1)}, bf16[640,1024]{1,0:T(8,128)(2,1)S(1)}, u32[]{:S(2)}, u32[]{:S(2)}) collective-permute-start(bf16[640,1024]{1,0:T(8,128)(2,1)S(1)} %shard_map.91.refs_2_), channel_id=1, source_target_pairs={{0,4},{4,0},{8,12},{12,8},{16,20},{20,16},{24,28},{28,24},{32,36},... | collective-permute-start | bytes 3932168 | tf_op jit(solution)/shard_map/ppermute | solution.py:27
  131.7 13.7 %collective-permute-start.29 = (bf16[112,2048]{1,0:T(8,128)(2,1)S(1)}, bf16[112,2048]{1,0:T(8,128)(2,1)S(1)}, u32[]{:S(2)}, u32[]{:S(2)}) collective-permute-start(bf16[112,2048]{1,0:T(8,128)(2,1)S(1)} %get-tuple-element.614), channel_id=1, source_target_pairs={{0,64},{64,0},{1,65},{65,1},{2,66},{66,2},{3,67},{67,3},{4,68},{68... | collective-permute-start | bytes 1376264 | tf_op jit(solution)/shard_map/ppermute | solution.py:35
  146.8 17.8 %collective-permute-start.34 = (bf16[320,1024]{1,0:T(8,128)(2,1)S(1)}, bf16[320,1024]{1,0:T(8,128)(2,1)S(1)}, u32[]{:S(2)}, u32[]{:S(2)}) collective-permute-start(bf16[320,1024]{1,0:T(8,128)(2,1)S(1)} %get-tuple-element.651), channel_id=1, source_target_pairs={{0,16},{4,20},{8,24},{12,28},{16,0},{20,4},{24,8},{28,12},{32,48},... | collective-permute-start | bytes 1966088 | tf_op jit(solution)/shard_map/ppermute | solution.py:27
  147.6 17.2 %collective-permute-start.35 = (bf16[320,1024]{1,0:T(8,128)(2,1)S(1)}, bf16[320,1024]{1,0:T(8,128)(2,1)S(1)}, u32[]{:S(2)}, u32[]{:S(2)}) collective-permute-start(bf16[320,1024]{1,0:T(8,128)(2,1)S(1)} %get-tuple-element.652), channel_id=1, source_target_pairs={{0,48},{4,52},{8,56},{12,60},{16,32},{20,36},{24,40},{28,44},{32,1... | collective-permute-start | bytes 1966088 | tf_op jit(solution)/shard_map/ppermute | solution.py:27
  148.9 15.7 %collective-permute-start.33 = (bf16[144,2048]{1,0:T(8,128)(2,1)S(1)}, bf16[144,2048]{1,0:T(8,128)(2,1)S(1)}, u32[]{:S(2)}, u32[]{:S(2)}) collective-permute-start(bf16[144,2048]{1,0:T(8,128)(2,1)S(1)} %get-tuple-element.649), channel_id=1, source_target_pairs={{0,64},{64,0},{1,65},{65,1},{2,66},{66,2},{3,67},{67,3},{4,68},{68... | collective-permute-start | bytes 1769480 | tf_op jit(solution)/shard_map/ppermute | solution.py:35
  (22 other events, 145.0 us)

commit v6 on v5

--- a/solution.py
+++ b/solution.py
@@ -481,12 +481,13 @@
     other0 = swap(v.keep0, ZLO)
     s2 = along_x(v.r2, 2)
     v.own, v.other = project(v.index, [[v.n0, v.x01, v.x03, v.x02], [v.n1, v.x11, v.x13, v.x12]], v.weight)
-    v.got_a1, v.got_b1, v.other0, v.s2 = got_a1, got_b1, other0, s2
+    v.got_a1, v.got_b1, v.other0 = got_a1, got_b1, other0
     del v.r2, v.send_a1, v.send_b1, v.x01, v.x03, v.x02, v.x11, v.x13, v.x12, v.n0, v.n1
     v.end()
 
     v.n_a1, v.n_b1 = add_first(v.next_a1, v.next_b1, v.got_a1, v.got_b1)
     v.da0, v.db0 = add_third(v.keep0, v.other0)
+    v.s2 = s2
     del v.next_a1, v.next_b1, v.keep0, v.other0
     v.end()
 
@@ -548,7 +549,7 @@
     v.ab1_c, v.hidden_c = ab1_c, hidden_c
     v.weight_grad = finish(1, [v.ab1, v.ab1_c], [], v.weight_grad)
     v.result = both_taps(v.index, v.own_rows, v.hidden_c)
-    v.la1, v.lb1, v.back1 = la1, lb1, back1
+    v.la1, v.lb1 = la1, lb1
     del v.a1, v.b1, v.ab0, v.ab0_c, v.ab1, v.ab1_c, v.lab0, v.lab0_c, v.own_rows, v.hidden, v.hidden_c, v.up1
     v.end()
 
@@ -557,7 +558,7 @@
     projected = sums(
         *(
             [(v.own, (r, EVERY)), (v.other_c, (r, EVERY)), (back, (EVERY, EVERY))]
-            for r, back in zip(rows, (v.back0, v.back1))
+            for r, back in zip(rows, (v.back0, back1))
         ),
         stack=True,
     )[0]

time: 171 us -> 184 us (1.076)
  waiting for transfers between devices: 67.1 us -> 81.4 us
    ppermute x3, waiting for transfers between devices: 14.2 us -> 21.5 us  [to_section(): return lax.ppermute(value, 'section', [(0, 1), (1, 0)])]
    ppermute x28, waiting for transfers between devices: 45.6 us -> 52.8 us  [swap(): return lax.ppermute(value, 'dp', pairs)]
  transfers between devices with their start and end apart: 40 -> 40, of which waited for: 22 -> 21; matrix products, arithmetic and copies ran while one was open for 0% -> 0% of each run, Pallas kernels for 20% -> 19%
where the time goes in v6:
time: 184 us
  waiting for transfers between devices  81.4 us (44%)
  starting transfers between devices  55.3 us (30%)
  Pallas kernels  38.5 us (21%)
  local copies, waits for them, and re-layouts  7.69 us (4%)
    ppermute x28, waiting for transfers between devices, swap(): return lax.ppermute(value, 'dp', pairs)  52.8 us
    pallas_call x23, Pallas kernels, call(): pl.pallas_call(kernel, in_specs=in_specs, out_specs=out_specs, out_shape=...  38.5 us
    ppermute x28, starting transfers between devices, swap(): return lax.ppermute(value, 'dp', pairs)  30 us
    ppermute x3, waiting for transfers between devices, to_section(): return lax.ppermute(value, 'section', [(0, 1), (1, 0)])  21.5 us
    ppermute x9, starting transfers between devices, along_x(): lax.ppermute(value, 'tensor', [(i, (i + step) % 4) for i in range(4)])  15.7 us
    ppermute x3, starting transfers between devices, to_section(): return lax.ppermute(value, 'section', [(0, 1), (1, 0)])  9.65 us
    unnamed x12, local copies, waits for them, and re-layouts  7.69 us
    ppermute x9, waiting for transfers between devices, along_x(): lax.ppermute(value, 'tensor', [(i, (i + step) % 4) for i in range(4)])  7 us
  transfers between devices with their start and end apart: 40, of which 21 were waited for; matrix products, arithmetic and copies ran while one was open for 0% of the time, Pallas kernels for 19%

profile of v6, /device:TPU:1, one launch (start us, length us, event | category | flops | bytes accessed | tf_op | source)
XLA Modules:
  0.0 184.0 jit_solution(15897694148411281321)
XLA Ops:
  5.5 3.7 %collective-permute-start = (bf16[256,2048]{1,0:T(8,128)(2,1)S(1)}, bf16[256,2048]{1,0:T(8,128)(2,1)S(1)}, u32[]{:S(2)}, u32[]{:S(2)}) collective-permute-start(bf16[256,2048]{1,0:T(8,128)(2,1)S(1)} %get-tuple-element.443.refs_4_.refs_0_), channel_id=1, source_target_pairs={{0,64},{64,0},{1,65},{65,1},{2,66},{66,2},{3,67},{67,3},{4,68},{68... | collective-permute-start | bytes 3145736 | tf_op jit(solution)/shard_map/ppermute | solution.py:35
  14.5 2.5 %collective-permute-start.4 = (bf16[2,128,640]{2,1,0:T(8,128)(2,1)S(1)}, bf16[2,128,640]{2,1,0:T(8,128)(2,1)S(1)}, u32[]{:S(2)}, u32[]{:S(2)}) collective-permute-start(bf16[2,128,640]{2,1,0:T(8,128)(2,1)S(1)} %get-tuple-element.503.refs_0_), channel_id=1, source_target_pairs={{0,2},{1,3},{2,0},{3,1},{4,6},{5,7},{6,4},{7,5},{8,10},{9,11},{10,... | collective-permute-start | bytes 983048 | tf_op jit(solution)/shard_map/ppermute | solution.py:31
  18.1 4.0 %copy-done = bf16[2560,2048]{1,0:T(8,128)(2,1)S(1)} copy-done((bf16[2560,2048]{1,0:T(8,128)(2,1)S(1)}, bf16[2560,2048]{1,0:T(8,128)(2,1)}, u32[]{:S(2)}) %copy-start) | copy-done | bytes 10485784
  24.4 8.2 %collective-permute-done.refs_5_.refs_1_ = bf16[256,2048]{1,0:T(8,128)(2,1)S(1)} collective-permute-done((bf16[256,2048]{1,0:T(8,128)(2,1)S(1)}, bf16[256,2048]{1,0:T(8,128)(2,1)S(1)}, u32[]{:S(2)}, u32[]{:S(2)}) %collective-permute-start) | collective-permute-done | bytes 1048608 | tf_op jit(solution)/shard_map/ppermute | solution.py:35
  33.3 2.8 %collective-permute-start.7 = (bf16[2,128,640]{2,1,0:T(8,128)(2,1)S(1)}, bf16[2,128,640]{2,1,0:T(8,128)(2,1)S(1)}, u32[]{:S(2)}, u32[]{:S(2)}) collective-permute-start(bf16[2,128,640]{2,1,0:T(8,128)(2,1)S(1)} %get-tuple-element.507.refs_0_.refs_4_), channel_id=1, source_target_pairs={{0,2},{1,3},{2,0},{3,1},{4,6},{5,7},{6,4},{7,5},{8,10},{9,11},{10,... | collective-permute-start | bytes 983048 | tf_op jit(solution)/shard_map/ppermute | solution.py:31
  36.1 3.9 %shard_map.79 = (bf16[320,1024]{1,0:T(8,128)(2,1)S(1)}, bf16[320,1024]{1,0:T(8,128)(2,1)S(1)}, bf16[320,512]{1,0:T(8,128)(2,1)S(1)}, bf16[320,512]{1,0:T(8,128)(...) custom-call(s32[13]{0:T(128)S(1)} %get-tuple-element.662.index, ...), custom_call_target="tpu_custom_call" | custom-call | flops 1 | bytes 1 | tf_op jit(solution)/shard_map/pallas_call | solution.py:63
  40.0 4.1 %collective-permute-done.7.refs_3_.refs_7_ = bf16[2,128,640]{2,1,0:T(8,128)(2,1)S(1)} collective-permute-done((bf16[2,128,640]{2,1,0:T(8,128)(2,1)S(1)}, bf16[2,128,640]{2,1,0:T(8,128)(2,1)S(1)}, u32[]{:S(2)}, u32[]{:S(2)}) %collective-permute-start.7) | collective-permute-done | bytes 327712 | tf_op jit(solution)/shard_map/ppermute | solution.py:31
  50.0 6.8 %shard_map.80 = (bf16[2,128,1280]{2,1,0:T(8,128)(2,1)S(1)}, bf16[2,128,1280]{2,1,0:T(8,128)(2,1)S(1)}, bf16[2,128,1280]{2,1,0:T(8,128)(2,1)S(1)}, bf16[2,128,1280]{2,1,0:T(8,128)(2,1)S(1)}) custom-call(s32[13]{0:T(128)S(1)} %get-tuple-element.662.index, bf16[256,2048]{1,0:T(8,128)(2,1)S(1)} %get-tuple-element.443.refs_4_.refs_0_, ...), custom_call_target="tpu_custom_call" | custom-call | flops 1 | bytes 1 | tf_op jit(solution)/shard_map/pallas_call | solution.py:63
  56.8 2.7 %collective-permute-done.8.refs_1_ = bf16[320,1024]{1,0:T(8,128)(2,1)S(1)} collective-permute-done((bf16[320,1024]{1,0:T(8,128)(2,1)S(1)}, bf16[320,1024]{1,0:T(8,128)(2,1)S(1)}, u32[]{:S(2)}, u32[]{:S(2)}) %collective-permute-start.8) | collective-permute-done | bytes 655392 | tf_op jit(solution)/shard_map/ppermute | solution.py:27
  63.8 3.9 %shard_map.82 = (bf16[320,1024]{1,0:T(8,128)(2,1)S(1)}, bf16[320,1024]{1,0:T(8,128)(2,1)S(1)}, bf16[320,512]{1,0:T(8,128)(2,1)S(1)}, bf16[320,512]{1,0:T(8,128)(...) custom-call(s32[13]{0:T(128)S(1)} %get-tuple-element.662.index, ...), custom_call_target="tpu_custom_call" | custom-call | flops 1 | bytes 1 | tf_op jit(solution)/shard_map/pallas_call | solution.py:63
  67.7 2.6 %collective-permute-done.12.refs_2_ = bf16[320,512]{1,0:T(8,128)(2,1)S(1)} collective-permute-done((bf16[320,512]{1,0:T(8,128)(2,1)S(1)}, bf16[320,512]{1,0:T(8,128)(2,1)S(1)}, u32[]{:S(2)}, u32[]{:S(2)}) %collective-permute-start.12) | collective-permute-done | bytes 327712 | tf_op jit(solution)/shard_map/ppermute | solution.py:27
  73.6 2.7 %collective-permute-start.17 = (bf16[2,128,1280]{2,1,0:T(8,128)(2,1)S(1)}, bf16[2,128,1280]{2,1,0:T(8,128)(2,1)S(1)}, u32[]{:S(2)}, u32[]{:S(2)}) collective-permute-start(bf16[2,128,1280]{2,1,0:T(8,128)(2,1)S(1)} %get-tuple-element.539), channel_id=1, source_target_pairs={{0,2},{1,3},{2,0},{3,1},{4,6},{5,7},{6,4},{7,5},{8,10},{9,11},{10,... | collective-permute-start | bytes 1966088 | tf_op jit(solution)/shard_map/ppermute | solution.py:31
  76.3 6.3 %shard_map.84 = (bf16[512,2048]{1,0:T(8,128)(2,1)S(1)}, bf16[512,2048]{1,0:T(8,128)(2,1)S(1)}) custom-call(s32[13]{0:T(128)S(1)} %get-tuple-element.662.index, bf16[2,128,640]{2,1,0:T(8,128)(2,1)S(1)} %get-tuple-element.503.refs_0_, bf16[2,128,640]{2,1,0:T(8,128)(2,1)S(1)} %collective-permute-done.3.refs_1_, ...), custom_call_target="tpu_custom_call" | custom-call | flops 1 | bytes 1 | tf_op jit(solution)/shard_map/pallas_call | solution.py:63
  87.8 4.5 %collective-permute-start.22 = (bf16[512,2048]{1,0:T(8,128)(2,1)S(1)}, bf16[512,2048]{1,0:T(8,128)(2,1)S(1)}, u32[]{:S(2)}, u32[]{:S(2)}) collective-permute-start(bf16[512,2048]{1,0:T(8,128)(2,1)S(1)} %get-tuple-element.549), channel_id=1, source_target_pairs={{0,4},{4,0},{8,12},{12,8},{16,20},{20,16},{24,28},{28,24},{32,36},... | collective-permute-start | bytes 6291464 | tf_op jit(solution)/shard_map/ppermute | solution.py:27
  95.8 7.0 %collective-permute-done.20.refs_2_ = bf16[320,512]{1,0:T(8,128)(2,1)S(1)} collective-permute-done((bf16[320,512]{1,0:T(8,128)(2,1)S(1)}, bf16[320,512]{1,0:T(8,128)(2,1)S(1)}, u32[]{:S(2)}, u32[]{:S(2)}) %collective-permute-start.20) | collective-permute-done | bytes 327712 | tf_op jit(solution)/shard_map/ppermute | solution.py:27
  102.8 7.0 %collective-permute-done.18.right_a = bf16[320,512]{1,0:T(8,128)(2,1)S(1)} collective-permute-done((bf16[320,512]{1,0:T(8,128)(2,1)S(1)}, bf16[320,512]{1,0:T(8,128)(2,1)S(1)}, u32[]{:S(2)}, u32[]{:S(2)}) %collective-permute-start.18) | collective-permute-done | bytes 327712 | tf_op jit(solution)/shard_map/ppermute | solution.py:27
  115.2 10.5 %collective-permute-done.23.top = bf16[320,1024]{1,0:T(8,128)(2,1)S(1)} collective-permute-done((bf16[320,1024]{1,0:T(8,128)(2,1)S(1)}, bf16[320,1024]{1,0:T(8,128)(2,1)S(1)}, u32[]{:S(2)}, u32[]{:S(2)}) %collective-permute-start.23) | collective-permute-done | bytes 655392 | tf_op jit(solution)/shard_map/ppermute | solution.py:27
  127.9 2.7 %collective-permute-start.28 = (bf16[640,1024]{1,0:T(8,128)(2,1)S(1)}, bf16[640,1024]{1,0:T(8,128)(2,1)S(1)}, u32[]{:S(2)}, u32[]{:S(2)}) collective-permute-start(bf16[640,1024]{1,0:T(8,128)(2,1)S(1)} %get-tuple-element.654.refs_0_), channel_id=1, source_target_pairs={{0,4},{4,0},{8,12},{12,8},{16,20},{20,16},{24,28},{28,24},{32,36},... | collective-permute-start | bytes 3932168 | tf_op jit(solution)/shard_map/ppermute | solution.py:27
  130.6 3.0 %collective-permute-start.29 = (bf16[112,2048]{1,0:T(8,128)(2,1)S(1)}, bf16[112,2048]{1,0:T(8,128)(2,1)S(1)}, u32[]{:S(2)}, u32[]{:S(2)}) collective-permute-start(bf16[112,2048]{1,0:T(8,128)(2,1)S(1)} %get-tuple-element.611), channel_id=1, source_target_pairs={{0,64},{64,0},{1,65},{65,1},{2,66},{66,2},{3,67},{67,3},{4,68},{68... | collective-permute-start | bytes 1376264 | tf_op jit(solution)/shard_map/ppermute | solution.py:35
  136.7 6.5 %collective-permute-done.30.right_a = bf16[320,512]{1,0:T(8,128)(2,1)S(1)} collective-permute-done((bf16[320,512]{1,0:T(8,128)(2,1)S(1)}, bf16[320,512]{1,0:T(8,128)(2,1)S(1)}, u32[]{:S(2)}, u32[]{:S(2)}) %collective-permute-start.30) | collective-permute-done | bytes 327712 | tf_op jit(solution)/shard_map/ppermute | solution.py:27
  148.1 3.0 %shard_map.95.refs_2_ = bf16[2560,2048]{1,0:T(8,128)(2,1)} custom-call(s32[13]{0:T(128)S(1)} %get-tuple-element.662.index, bf16[640,1024]{1,0:T(8,128)(2,1)S(1)} %get-tuple-element.654.refs_0_, bf16[640,1024]{1,0:T(8,128)(2,1)S(1)} %collective-permute-done.28.refs_1_, bf16[640,1024]{1,0:T(8,128)(2,1)S(1)} %shard_map.91.refs_2_, ...), custom_call_target="tpu_custom_call" | custom-call | flops 1 | bytes 1 | tf_op jit(solution)/shard_map/pallas_call | solution.py:63
  154.6 7.0 %collective-permute-done.33.refs_0_ = bf16[320,1024]{1,0:T(8,128)(2,1)S(1)} collective-permute-done((bf16[320,1024]{1,0:T(8,128)(2,1)S(1)}, bf16[320,1024]{1,0:T(8,128)(2,1)S(1)}, u32[]{:S(2)}, u32[]{:S(2)}) %collective-permute-start.33) | collective-permute-done | bytes 655392 | tf_op jit(solution)/shard_map/ppermute | solution.py:27
  164.5 3.0 %collective-permute-start.37 = (bf16[144,2048]{1,0:T(8,128)(2,1)S(1)}, bf16[144,2048]{1,0:T(8,128)(2,1)S(1)}, u32[]{:S(2)}, u32[]{:S(2)}) collective-permute-start(bf16[144,2048]{1,0:T(8,128)(2,1)S(1)} %get-tuple-element.661), channel_id=1, source_target_pairs={{0,64},{64,0},{1,65},{65,1},{2,66},{66,2},{3,67},{67,3},{4,68},{68... | collective-permute-start | bytes 1769480 | tf_op jit(solution)/shard_map/ppermute | solution.py:35
  167.5 12.9 %collective-permute-done.37.refs_3_ = bf16[144,2048]{1,0:T(8,128)(2,1)S(1)} collective-permute-done((bf16[144,2048]{1,0:T(8,128)(2,1)S(1)}, bf16[144,2048]{1,0:T(8,128)(2,1)S(1)}, u32[]{:S(2)}, u32[]{:S(2)}) %collective-permute-start.37) | collective-permute-done | bytes 589856 | tf_op jit(solution)/shard_map/ppermute | solution.py:35
  (91 shorter events, 61.8 us)
Async XLA Ops:
  5.5 27.1 %collective-permute-start = (bf16[256,2048]{1,0:T(8,128)(2,1)S(1)}, bf16[256,2048]{1,0:T(8,128)(2,1)S(1)}, u32[]{:S(2)}, u32[]{:S(2)}) collective-permute-start(bf16[256,2048]{1,0:T(8,128)(2,1)S(1)} %get-tuple-element.443.refs_4_.refs_0_), channel_id=1, source_target_pairs={{0,64},{64,0},{1,65},{65,1},{2,66},{66,2},{3,67},{67,3},{4,68},{68... | collective-permute-start | bytes 3145736 | tf_op jit(solution)/shard_map/ppermute | solution.py:35
  13.2 19.3 %collective-permute-start.5 = (bf16[2,128,640]{2,1,0:T(8,128)(2,1)S(1)}, bf16[2,128,640]{2,1,0:T(8,128)(2,1)S(1)}, u32[]{:S(2)}, u32[]{:S(2)}) collective-permute-start(bf16[2,128,640]{2,1,0:T(8,128)(2,1)S(1)} %get-tuple-element.503.refs_0_), channel_id=1, source_target_pairs={{0,1},{1,2},{2,3},{3,0},{4,5},{5,6},{6,7},{7,4},{8,9},{9,10},{10,1... | collective-permute-start | bytes 983048 | tf_op jit(solution)/shard_map/ppermute | solution.py:31
  14.5 18.1 %collective-permute-start.4 = (bf16[2,128,640]{2,1,0:T(8,128)(2,1)S(1)}, bf16[2,128,640]{2,1,0:T(8,128)(2,1)S(1)}, u32[]{:S(2)}, u32[]{:S(2)}) collective-permute-start(bf16[2,128,640]{2,1,0:T(8,128)(2,1)S(1)} %get-tuple-element.503.refs_0_), channel_id=1, source_target_pairs={{0,2},{1,3},{2,0},{3,1},{4,6},{5,7},{6,4},{7,5},{8,10},{9,11},{10,... | collective-permute-start | bytes 983048 | tf_op jit(solution)/shard_map/ppermute | solution.py:31
  17.0 15.6 %collective-permute-start.3 = (bf16[2,128,640]{2,1,0:T(8,128)(2,1)S(1)}, bf16[2,128,640]{2,1,0:T(8,128)(2,1)S(1)}, u32[]{:S(2)}, u32[]{:S(2)}) collective-permute-start(bf16[2,128,640]{2,1,0:T(8,128)(2,1)S(1)} %get-tuple-element.503.refs_0_), channel_id=1, source_target_pairs={{0,3},{1,0},{2,1},{3,2},{4,7},{5,4},{6,5},{7,6},{8,11},{9,8},{10,9... | collective-permute-start | bytes 983048 | tf_op jit(solution)/shard_map/ppermute | solution.py:31
  44.1 15.4 %collective-permute-start.8 = (bf16[320,1024]{1,0:T(8,128)(2,1)S(1)}, bf16[320,1024]{1,0:T(8,128)(2,1)S(1)}, u32[]{:S(2)}, u32[]{:S(2)}) collective-permute-start(bf16[320,1024]{1,0:T(8,128)(2,1)S(1)} %get-tuple-element.385), channel_id=1, source_target_pairs={{0,16},{4,20},{8,24},{12,28},{16,0},{20,4},{24,8},{28,12},{32,48},... | collective-permute-start | bytes 1966088 | tf_op jit(solution)/shard_map/ppermute | solution.py:27
  45.4 16.3 %collective-permute-start.9 = (bf16[320,1024]{1,0:T(8,128)(2,1)S(1)}, bf16[320,1024]{1,0:T(8,128)(2,1)S(1)}, u32[]{:S(2)}, u32[]{:S(2)}) collective-permute-start(bf16[320,1024]{1,0:T(8,128)(2,1)S(1)} %get-tuple-element.386), channel_id=1, source_target_pairs={{0,48},{4,52},{8,56},{12,60},{16,32},{20,36},{24,40},{28,44},{32,1... | collective-permute-start | bytes 1966088 | tf_op jit(solution)/shard_map/ppermute | solution.py:27
  71.3 14.2 %collective-permute-start.15 = (bf16[320,1024]{1,0:T(8,128)(2,1)S(1)}, bf16[320,1024]{1,0:T(8,128)(2,1)S(1)}, u32[]{:S(2)}, u32[]{:S(2)}) collective-permute-start(bf16[320,1024]{1,0:T(8,128)(2,1)S(1)} %get-tuple-element.496), channel_id=1, source_target_pairs={{0,48},{4,52},{8,56},{12,60},{16,32},{20,36},{24,40},{28,44},{32,1... | collective-permute-start | bytes 1966088 | tf_op jit(solution)/shard_map/ppermute | solution.py:27
  73.6 14.2 %collective-permute-start.17 = (bf16[2,128,1280]{2,1,0:T(8,128)(2,1)S(1)}, bf16[2,128,1280]{2,1,0:T(8,128)(2,1)S(1)}, u32[]{:S(2)}, u32[]{:S(2)}) collective-permute-start(bf16[2,128,1280]{2,1,0:T(8,128)(2,1)S(1)} %get-tuple-element.539), channel_id=1, source_target_pairs={{0,2},{1,3},{2,0},{3,1},{4,6},{5,7},{6,4},{7,5},{8,10},{9,11},{10,... | collective-permute-start | bytes 1966088 | tf_op jit(solution)/shard_map/ppermute | solution.py:31
  87.8 22.1 %collective-permute-start.22 = (bf16[512,2048]{1,0:T(8,128)(2,1)S(1)}, bf16[512,2048]{1,0:T(8,128)(2,1)S(1)}, u32[]{:S(2)}, u32[]{:S(2)}) collective-permute-start(bf16[512,2048]{1,0:T(8,128)(2,1)S(1)} %get-tuple-element.549), channel_id=1, source_target_pairs={{0,4},{4,0},{8,12},{12,8},{16,20},{20,16},{24,28},{28,24},{32,36},... | collective-permute-start | bytes 6291464 | tf_op jit(solution)/shard_map/ppermute | solution.py:27
  93.6 16.2 %collective-permute-start.18 = (bf16[320,512]{1,0:T(8,128)(2,1)S(1)}, bf16[320,512]{1,0:T(8,128)(2,1)S(1)}, u32[]{:S(2)}, u32[]{:S(2)}) collective-permute-start(bf16[320,512]{1,0:T(8,128)(2,1)S(1)} %get-tuple-element.557.left_a), channel_id=1, source_target_pairs={{0,48},{4,52},{8,56},{12,60},{16,32},{20,36},{24,40},{28,44},{32,1... | collective-permute-start | bytes 983048 | tf_op jit(solution)/shard_map/ppermute | solution.py:27
  95.1 14.7 %collective-permute-start.19 = (bf16[320,512]{1,0:T(8,128)(2,1)S(1)}, bf16[320,512]{1,0:T(8,128)(2,1)S(1)}, u32[]{:S(2)}, u32[]{:S(2)}) collective-permute-start(bf16[320,512]{1,0:T(8,128)(2,1)S(1)} %get-tuple-element.558.left_b), channel_id=1, source_target_pairs={{0,16},{4,20},{8,24},{12,28},{16,0},{20,4},{24,8},{28,12},{32,48},... | collective-permute-start | bytes 983048 | tf_op jit(solution)/shard_map/ppermute | solution.py:27
  110.3 15.4 %collective-permute-start.23 = (bf16[320,1024]{1,0:T(8,128)(2,1)S(1)}, bf16[320,1024]{1,0:T(8,128)(2,1)S(1)}, u32[]{:S(2)}, u32[]{:S(2)}) collective-permute-start(bf16[320,1024]{1,0:T(8,128)(2,1)S(1)} %get-tuple-element.582), channel_id=1, source_target_pairs={{0,16},{4,20},{8,24},{12,28},{16,0},{20,4},{24,8},{28,12},{32,48},... | collective-permute-start | bytes 1966088 | tf_op jit(solution)/shard_map/ppermute | solution.py:27
  110.4 16.4 %collective-permute-start.24 = (bf16[320,1024]{1,0:T(8,128)(2,1)S(1)}, bf16[320,1024]{1,0:T(8,128)(2,1)S(1)}, u32[]{:S(2)}, u32[]{:S(2)}) collective-permute-start(bf16[320,1024]{1,0:T(8,128)(2,1)S(1)} %get-tuple-element.583), channel_id=1, source_target_pairs={{0,48},{4,52},{8,56},{12,60},{16,32},{20,36},{24,40},{28,44},{32,1... | collective-permute-start | bytes 1966088 | tf_op jit(solution)/shard_map/ppermute | solution.py:27
  111.8 14.9 %collective-permute-start.25 = (bf16[640,512]{1,0:T(8,128)(2,1)S(1)}, bf16[640,512]{1,0:T(8,128)(2,1)S(1)}, u32[]{:S(2)}, u32[]{:S(2)}) collective-permute-start(bf16[640,512]{1,0:T(8,128)(2,1)S(1)} %shard_map.88.refs_0_), channel_id=1, source_target_pairs={{0,8},{4,12},{8,0},{12,4},{16,24},{20,28},{24,16},{28,20},{32,40},... | collective-permute-start | bytes 1966088 | tf_op jit(solution)/shard_map/ppermute | solution.py:27
  112.3 15.6 %collective-permute-start.26 = (bf16[2,128,1280]{2,1,0:T(8,128)(2,1)S(1)}, bf16[2,128,1280]{2,1,0:T(8,128)(2,1)S(1)}, u32[]{:S(2)}, u32[]{:S(2)}) collective-permute-start(bf16[2,128,1280]{2,1,0:T(8,128)(2,1)S(1)} %get-tuple-element.605), channel_id=1, source_target_pairs={{0,1},{1,2},{2,3},{3,0},{4,5},{5,6},{6,7},{7,4},{8,9},{9,10},{10,1... | collective-permute-start | bytes 1966088 | tf_op jit(solution)/shard_map/ppermute | solution.py:31
  113.5 14.4 %collective-permute-start.27 = (bf16[2,128,1280]{2,1,0:T(8,128)(2,1)S(1)}, bf16[2,128,1280]{2,1,0:T(8,128)(2,1)S(1)}, u32[]{:S(2)}, u32[]{:S(2)}) collective-permute-start(bf16[2,128,1280]{2,1,0:T(8,128)(2,1)S(1)} %get-tuple-element.607), channel_id=1, source_target_pairs={{0,3},{1,0},{2,1},{3,2},{4,7},{5,4},{6,5},{7,6},{8,11},{9,8},{10,9... | collective-permute-start | bytes 1966088 | tf_op jit(solution)/shard_map/ppermute | solution.py:31
  127.9 15.8 %collective-permute-start.28 = (bf16[640,1024]{1,0:T(8,128)(2,1)S(1)}, bf16[640,1024]{1,0:T(8,128)(2,1)S(1)}, u32[]{:S(2)}, u32[]{:S(2)}) collective-permute-start(bf16[640,1024]{1,0:T(8,128)(2,1)S(1)} %get-tuple-element.654.refs_0_), channel_id=1, source_target_pairs={{0,4},{4,0},{8,12},{12,8},{16,20},{20,16},{24,28},{28,24},{32,36},... | collective-permute-start | bytes 3932168 | tf_op jit(solution)/shard_map/ppermute | solution.py:27
  130.6 13.1 %collective-permute-start.32 = (bf16[640,1024]{1,0:T(8,128)(2,1)S(1)}, bf16[640,1024]{1,0:T(8,128)(2,1)S(1)}, u32[]{:S(2)}, u32[]{:S(2)}) collective-permute-start(bf16[640,1024]{1,0:T(8,128)(2,1)S(1)} %shard_map.91.refs_2_), channel_id=1, source_target_pairs={{0,4},{4,0},{8,12},{12,8},{16,20},{20,16},{24,28},{28,24},{32,36},... | collective-permute-start | bytes 3932168 | tf_op jit(solution)/shard_map/ppermute | solution.py:27
  130.6 13.1 %collective-permute-start.29 = (bf16[112,2048]{1,0:T(8,128)(2,1)S(1)}, bf16[112,2048]{1,0:T(8,128)(2,1)S(1)}, u32[]{:S(2)}, u32[]{:S(2)}) collective-permute-start(bf16[112,2048]{1,0:T(8,128)(2,1)S(1)} %get-tuple-element.611), channel_id=1, source_target_pairs={{0,64},{64,0},{1,65},{65,1},{2,66},{66,2},{3,67},{67,3},{4,68},{68... | collective-permute-start | bytes 1376264 | tf_op jit(solution)/shard_map/ppermute | solution.py:35
  145.4 16.3 %collective-permute-start.33 = (bf16[320,1024]{1,0:T(8,128)(2,1)S(1)}, bf16[320,1024]{1,0:T(8,128)(2,1)S(1)}, u32[]{:S(2)}, u32[]{:S(2)}) collective-permute-start(bf16[320,1024]{1,0:T(8,128)(2,1)S(1)} %get-tuple-element.647), channel_id=1, source_target_pairs={{0,16},{4,20},{8,24},{12,28},{16,0},{20,4},{24,8},{28,12},{32,48},... | collective-permute-start | bytes 1966088 | tf_op jit(solution)/shard_map/ppermute | solution.py:27
  146.1 17.2 %collective-permute-start.34 = (bf16[320,1024]{1,0:T(8,128)(2,1)S(1)}, bf16[320,1024]{1,0:T(8,128)(2,1)S(1)}, u32[]{:S(2)}, u32[]{:S(2)}) collective-permute-start(bf16[320,1024]{1,0:T(8,128)(2,1)S(1)} %get-tuple-element.648), channel_id=1, source_target_pairs={{0,48},{4,52},{8,56},{12,60},{16,32},{20,36},{24,40},{28,44},{32,1... | collective-permute-start | bytes 1966088 | tf_op jit(solution)/shard_map/ppermute | solution.py:27
  163.3 18.4 %collective-permute-start.38 = (bf16[320,1024]{1,0:T(8,128)(2,1)S(1)}, bf16[320,1024]{1,0:T(8,128)(2,1)S(1)}, u32[]{:S(2)}, u32[]{:S(2)}) collective-permute-start(bf16[320,1024]{1,0:T(8,128)(2,1)S(1)} %collective-permute-done.33.refs_0_), channel_id=1, source_target_pairs={{0,4},{4,0},{8,12},{12,8},{16,20},{20,16},{24,28},{28,24},{32,36},... | collective-permute-start | bytes 1966088 | tf_op jit(solution)/shard_map/ppermute | solution.py:27
  164.5 17.2 %collective-permute-start.39 = (bf16[320,1024]{1,0:T(8,128)(2,1)S(1)}, bf16[320,1024]{1,0:T(8,128)(2,1)S(1)}, u32[]{:S(2)}, u32[]{:S(2)}) collective-permute-start(bf16[320,1024]{1,0:T(8,128)(2,1)S(1)} %collective-permute-done.34.refs_1_), channel_id=1, source_target_pairs={{0,4},{4,0},{8,12},{12,8},{16,20},{20,16},{24,28},{28,24},{32,36},... | collective-permute-start | bytes 1966088 | tf_op jit(solution)/shard_map/ppermute | solution.py:27
  164.5 15.9 %collective-permute-start.37 = (bf16[144,2048]{1,0:T(8,128)(2,1)S(1)}, bf16[144,2048]{1,0:T(8,128)(2,1)S(1)}, u32[]{:S(2)}, u32[]{:S(2)}) collective-permute-start(bf16[144,2048]{1,0:T(8,128)(2,1)S(1)} %get-tuple-element.661), channel_id=1, source_target_pairs={{0,64},{64,0},{1,65},{65,1},{2,66},{66,2},{3,67},{67,3},{4,68},{68... | collective-permute-start | bytes 1769480 | tf_op jit(solution)/shard_map/ppermute | solution.py:35
  (22 other events, 161.8 us)

commit v7 on v5

--- a/solution.py
+++ b/solution.py
@@ -481,12 +481,13 @@
     other0 = swap(v.keep0, ZLO)
     s2 = along_x(v.r2, 2)
     v.own, v.other = project(v.index, [[v.n0, v.x01, v.x03, v.x02], [v.n1, v.x11, v.x13, v.x12]], v.weight)
-    v.got_a1, v.got_b1, v.other0, v.s2 = got_a1, got_b1, other0, s2
+    v.got_a1, v.got_b1, v.other0 = got_a1, got_b1, other0
     del v.r2, v.send_a1, v.send_b1, v.x01, v.x03, v.x02, v.x11, v.x13, v.x12, v.n0, v.n1
     v.end()
 
     v.n_a1, v.n_b1 = add_first(v.next_a1, v.next_b1, v.got_a1, v.got_b1)
     v.da0, v.db0 = add_third(v.keep0, v.other0)
+    v.s2 = s2
     del v.next_a1, v.next_b1, v.keep0, v.other0
     v.end()
 

time: 171 us -> 170 us (level)
  no operation moved by 1% of the time
where the time goes in v7:
time: 170 us
  waiting for transfers between devices  66.4 us (39%)
  starting transfers between devices  55.9 us (33%)
  Pallas kernels  38.5 us (23%)
  local copies, waits for them, and re-layouts  7.69 us (5%)
    ppermute x28, waiting for transfers between devices, swap(): return lax.ppermute(value, 'dp', pairs)  45.5 us
    pallas_call x23, Pallas kernels, call(): pl.pallas_call(kernel, in_specs=in_specs, out_specs=out_specs, out_shape=...  38.5 us
    ppermute x28, starting transfers between devices, swap(): return lax.ppermute(value, 'dp', pairs)  30.5 us
    ppermute x9, starting transfers between devices, along_x(): lax.ppermute(value, 'tensor', [(i, (i + step) % 4) for i in range(4)])  15.7 us
    ppermute x3, waiting for transfers between devices, to_section(): return lax.ppermute(value, 'section', [(0, 1), (1, 0)])  13.9 us
    ppermute x3, starting transfers between devices, to_section(): return lax.ppermute(value, 'section', [(0, 1), (1, 0)])  9.65 us
    unnamed x12, local copies, waits for them, and re-layouts  7.69 us
    ppermute x9, waiting for transfers between devices, along_x(): lax.ppermute(value, 'tensor', [(i, (i + step) % 4) for i in range(4)])  7 us
  transfers between devices with their start and end apart: 40, of which 22 were waited for; matrix products, arithmetic and copies ran while one was open for 0% of the time, Pallas kernels for 20%

profile of v7, /device:TPU:1, one launch (start us, length us, event | category | flops | bytes accessed | tf_op | source)
XLA Modules:
  0.0 169.6 jit_solution(231973928711723088)
XLA Ops:
  5.5 3.7 %collective-permute-start = (bf16[256,2048]{1,0:T(8,128)(2,1)S(1)}, bf16[256,2048]{1,0:T(8,128)(2,1)S(1)}, u32[]{:S(2)}, u32[]{:S(2)}) collective-permute-start(bf16[256,2048]{1,0:T(8,128)(2,1)S(1)} %get-tuple-element.444.refs_4_.refs_0_), channel_id=1, source_target_pairs={{0,64},{64,0},{1,65},{65,1},{2,66},{66,2},{3,67},{67,3},{4,68},{68... | collective-permute-start | bytes 3145736 | tf_op jit(solution)/shard_map/ppermute | solution.py:35
  14.5 2.5 %collective-permute-start.4 = (bf16[2,128,640]{2,1,0:T(8,128)(2,1)S(1)}, bf16[2,128,640]{2,1,0:T(8,128)(2,1)S(1)}, u32[]{:S(2)}, u32[]{:S(2)}) collective-permute-start(bf16[2,128,640]{2,1,0:T(8,128)(2,1)S(1)} %get-tuple-element.504.refs_0_), channel_id=1, source_target_pairs={{0,2},{1,3},{2,0},{3,1},{4,6},{5,7},{6,4},{7,5},{8,10},{9,11},{10,... | collective-permute-start | bytes 983048 | tf_op jit(solution)/shard_map/ppermute | solution.py:31
  18.1 4.0 %copy-done = bf16[2560,2048]{1,0:T(8,128)(2,1)S(1)} copy-done((bf16[2560,2048]{1,0:T(8,128)(2,1)S(1)}, bf16[2560,2048]{1,0:T(8,128)(2,1)}, u32[]{:S(2)}) %copy-start) | copy-done | bytes 10485784
  22.1 2.3 %shard_map.78.refs_4_.refs_8_ = bf16[1280,2048]{1,0:T(8,128)(2,1)S(1)} custom-call(s32[13]{0:T(128)S(1)} %get-tuple-element.664.index, bf16[2560,2048]{1,0:T(8,128)(2,1)S(1)} %copy-done), custom_call_target="tpu_custom_call" | custom-call | flops 1 | bytes 1 | tf_op jit(solution)/shard_map/pallas_call | solution.py:63
  24.4 8.2 %collective-permute-done.refs_5_.refs_1_ = bf16[256,2048]{1,0:T(8,128)(2,1)S(1)} collective-permute-done((bf16[256,2048]{1,0:T(8,128)(2,1)S(1)}, bf16[256,2048]{1,0:T(8,128)(2,1)S(1)}, u32[]{:S(2)}, u32[]{:S(2)}) %collective-permute-start) | collective-permute-done | bytes 1048608 | tf_op jit(solution)/shard_map/ppermute | solution.py:35
  33.3 2.8 %collective-permute-start.7 = (bf16[2,128,640]{2,1,0:T(8,128)(2,1)S(1)}, bf16[2,128,640]{2,1,0:T(8,128)(2,1)S(1)}, u32[]{:S(2)}, u32[]{:S(2)}) collective-permute-start(bf16[2,128,640]{2,1,0:T(8,128)(2,1)S(1)} %get-tuple-element.508.refs_0_.refs_4_), channel_id=1, source_target_pairs={{0,2},{1,3},{2,0},{3,1},{4,6},{5,7},{6,4},{7,5},{8,10},{9,11},{10,... | collective-permute-start | bytes 983048 | tf_op jit(solution)/shard_map/ppermute | solution.py:31
  36.1 3.9 %shard_map.79 = (bf16[320,1024]{1,0:T(8,128)(2,1)S(1)}, bf16[320,1024]{1,0:T(8,128)(2,1)S(1)}, bf16[320,512]{1,0:T(8,128)(2,1)S(1)}, bf16[320,512]{1,0:T(8,128)(...) custom-call(s32[13]{0:T(128)S(1)} %get-tuple-element.664.index, ...), custom_call_target="tpu_custom_call" | custom-call | flops 1 | bytes 1 | tf_op jit(solution)/shard_map/pallas_call | solution.py:63
  40.0 4.1 %collective-permute-done.7.refs_3_.refs_7_ = bf16[2,128,640]{2,1,0:T(8,128)(2,1)S(1)} collective-permute-done((bf16[2,128,640]{2,1,0:T(8,128)(2,1)S(1)}, bf16[2,128,640]{2,1,0:T(8,128)(2,1)S(1)}, u32[]{:S(2)}, u32[]{:S(2)}) %collective-permute-start.7) | collective-permute-done | bytes 327712 | tf_op jit(solution)/shard_map/ppermute | solution.py:31
  50.0 6.8 %shard_map.80 = (bf16[2,128,1280]{2,1,0:T(8,128)(2,1)S(1)}, bf16[2,128,1280]{2,1,0:T(8,128)(2,1)S(1)}, bf16[2,128,1280]{2,1,0:T(8,128)(2,1)S(1)}, bf16[2,128,1280]{2,1,0:T(8,128)(2,1)S(1)}) custom-call(s32[13]{0:T(128)S(1)} %get-tuple-element.664.index, bf16[256,2048]{1,0:T(8,128)(2,1)S(1)} %get-tuple-element.444.refs_4_.refs_0_, ...), custom_call_target="tpu_custom_call" | custom-call | flops 1 | bytes 1 | tf_op jit(solution)/shard_map/pallas_call | solution.py:63
  56.8 2.7 %collective-permute-done.8.refs_1_ = bf16[320,1024]{1,0:T(8,128)(2,1)S(1)} collective-permute-done((bf16[320,1024]{1,0:T(8,128)(2,1)S(1)}, bf16[320,1024]{1,0:T(8,128)(2,1)S(1)}, u32[]{:S(2)}, u32[]{:S(2)}) %collective-permute-start.8) | collective-permute-done | bytes 655392 | tf_op jit(solution)/shard_map/ppermute | solution.py:27
  63.8 3.9 %shard_map.82 = (bf16[320,1024]{1,0:T(8,128)(2,1)S(1)}, bf16[320,1024]{1,0:T(8,128)(2,1)S(1)}, bf16[320,512]{1,0:T(8,128)(2,1)S(1)}, bf16[320,512]{1,0:T(8,128)(...) custom-call(s32[13]{0:T(128)S(1)} %get-tuple-element.664.index, ...), custom_call_target="tpu_custom_call" | custom-call | flops 1 | bytes 1 | tf_op jit(solution)/shard_map/pallas_call | solution.py:63
  67.7 2.6 %collective-permute-done.12.refs_2_ = bf16[320,512]{1,0:T(8,128)(2,1)S(1)} collective-permute-done((bf16[320,512]{1,0:T(8,128)(2,1)S(1)}, bf16[320,512]{1,0:T(8,128)(2,1)S(1)}, u32[]{:S(2)}, u32[]{:S(2)}) %collective-permute-start.12) | collective-permute-done | bytes 327712 | tf_op jit(solution)/shard_map/ppermute | solution.py:27
  73.6 2.7 %collective-permute-start.17 = (bf16[2,128,1280]{2,1,0:T(8,128)(2,1)S(1)}, bf16[2,128,1280]{2,1,0:T(8,128)(2,1)S(1)}, u32[]{:S(2)}, u32[]{:S(2)}) collective-permute-start(bf16[2,128,1280]{2,1,0:T(8,128)(2,1)S(1)} %get-tuple-element.540), channel_id=1, source_target_pairs={{0,2},{1,3},{2,0},{3,1},{4,6},{5,7},{6,4},{7,5},{8,10},{9,11},{10,... | collective-permute-start | bytes 1966088 | tf_op jit(solution)/shard_map/ppermute | solution.py:31
  76.3 6.3 %shard_map.84 = (bf16[512,2048]{1,0:T(8,128)(2,1)S(1)}, bf16[512,2048]{1,0:T(8,128)(2,1)S(1)}) custom-call(s32[13]{0:T(128)S(1)} %get-tuple-element.664.index, bf16[2,128,640]{2,1,0:T(8,128)(2,1)S(1)} %get-tuple-element.504.refs_0_, bf16[2,128,640]{2,1,0:T(8,128)(2,1)S(1)} %collective-permute-done.3.refs_1_, ...), custom_call_target="tpu_custom_call" | custom-call | flops 1 | bytes 1 | tf_op jit(solution)/shard_map/pallas_call | solution.py:63
  87.8 4.5 %collective-permute-start.22 = (bf16[512,2048]{1,0:T(8,128)(2,1)S(1)}, bf16[512,2048]{1,0:T(8,128)(2,1)S(1)}, u32[]{:S(2)}, u32[]{:S(2)}) collective-permute-start(bf16[512,2048]{1,0:T(8,128)(2,1)S(1)} %get-tuple-element.550), channel_id=1, source_target_pairs={{0,4},{4,0},{8,12},{12,8},{16,20},{20,16},{24,28},{28,24},{32,36},... | collective-permute-start | bytes 6291464 | tf_op jit(solution)/shard_map/ppermute | solution.py:27
  95.8 7.0 %collective-permute-done.20.refs_2_ = bf16[320,512]{1,0:T(8,128)(2,1)S(1)} collective-permute-done((bf16[320,512]{1,0:T(8,128)(2,1)S(1)}, bf16[320,512]{1,0:T(8,128)(2,1)S(1)}, u32[]{:S(2)}, u32[]{:S(2)}) %collective-permute-start.20) | collective-permute-done | bytes 327712 | tf_op jit(solution)/shard_map/ppermute | solution.py:27
  102.8 7.0 %collective-permute-done.18.right_a = bf16[320,512]{1,0:T(8,128)(2,1)S(1)} collective-permute-done((bf16[320,512]{1,0:T(8,128)(2,1)S(1)}, bf16[320,512]{1,0:T(8,128)(2,1)S(1)}, u32[]{:S(2)}, u32[]{:S(2)}) %collective-permute-start.18) | collective-permute-done | bytes 327712 | tf_op jit(solution)/shard_map/ppermute | solution.py:27
  115.2 10.5 %collective-permute-done.23.top = bf16[320,1024]{1,0:T(8,128)(2,1)S(1)} collective-permute-done((bf16[320,1024]{1,0:T(8,128)(2,1)S(1)}, bf16[320,1024]{1,0:T(8,128)(2,1)S(1)}, u32[]{:S(2)}, u32[]{:S(2)}) %collective-permute-start.23) | collective-permute-done | bytes 655392 | tf_op jit(solution)/shard_map/ppermute | solution.py:27
  127.9 2.7 %collective-permute-start.28 = (bf16[640,1024]{1,0:T(8,128)(2,1)S(1)}, bf16[640,1024]{1,0:T(8,128)(2,1)S(1)}, u32[]{:S(2)}, u32[]{:S(2)}) collective-permute-start(bf16[640,1024]{1,0:T(8,128)(2,1)S(1)} %get-tuple-element.656.refs_0_), channel_id=1, source_target_pairs={{0,4},{4,0},{8,12},{12,8},{16,20},{20,16},{24,28},{28,24},{32,36},... | collective-permute-start | bytes 3932168 | tf_op jit(solution)/shard_map/ppermute | solution.py:27
  130.6 3.0 %collective-permute-start.29 = (bf16[112,2048]{1,0:T(8,128)(2,1)S(1)}, bf16[112,2048]{1,0:T(8,128)(2,1)S(1)}, u32[]{:S(2)}, u32[]{:S(2)}) collective-permute-start(bf16[112,2048]{1,0:T(8,128)(2,1)S(1)} %get-tuple-element.612), channel_id=1, source_target_pairs={{0,64},{64,0},{1,65},{65,1},{2,66},{66,2},{3,67},{67,3},{4,68},{68... | collective-permute-start | bytes 1376264 | tf_op jit(solution)/shard_map/ppermute | solution.py:35
  136.7 6.5 %collective-permute-done.30.right_a = bf16[320,512]{1,0:T(8,128)(2,1)S(1)} collective-permute-done((bf16[320,512]{1,0:T(8,128)(2,1)S(1)}, bf16[320,512]{1,0:T(8,128)(2,1)S(1)}, u32[]{:S(2)}, u32[]{:S(2)}) %collective-permute-start.30) | collective-permute-done | bytes 327712 | tf_op jit(solution)/shard_map/ppermute | solution.py:27
  147.4 3.0 %collective-permute-start.33 = (bf16[144,2048]{1,0:T(8,128)(2,1)S(1)}, bf16[144,2048]{1,0:T(8,128)(2,1)S(1)}, u32[]{:S(2)}, u32[]{:S(2)}) collective-permute-start(bf16[144,2048]{1,0:T(8,128)(2,1)S(1)} %get-tuple-element.647), channel_id=1, source_target_pairs={{0,64},{64,0},{1,65},{65,1},{2,66},{66,2},{3,67},{67,3},{4,68},{68... | collective-permute-start | bytes 1769480 | tf_op jit(solution)/shard_map/ppermute | solution.py:35
  151.3 3.0 %shard_map.95.refs_2_ = bf16[2560,2048]{1,0:T(8,128)(2,1)} custom-call(s32[13]{0:T(128)S(1)} %get-tuple-element.664.index, bf16[640,1024]{1,0:T(8,128)(2,1)S(1)} %get-tuple-element.656.refs_0_, bf16[640,1024]{1,0:T(8,128)(2,1)S(1)} %collective-permute-done.28.refs_1_, bf16[640,1024]{1,0:T(8,128)(2,1)S(1)} %shard_map.91.refs_2_, ...), custom_call_target="tpu_custom_call" | custom-call | flops 1 | bytes 1 | tf_op jit(solution)/shard_map/pallas_call | solution.py:63
  157.9 5.3 %collective-permute-done.33.refs_3_ = bf16[144,2048]{1,0:T(8,128)(2,1)S(1)} collective-permute-done((bf16[144,2048]{1,0:T(8,128)(2,1)S(1)}, bf16[144,2048]{1,0:T(8,128)(2,1)S(1)}, u32[]{:S(2)}, u32[]{:S(2)}) %collective-permute-start.33) | collective-permute-done | bytes 589856 | tf_op jit(solution)/shard_map/ppermute | solution.py:35
  (91 shorter events, 59.8 us)
Async XLA Ops:
  5.5 27.1 %collective-permute-start = (bf16[256,2048]{1,0:T(8,128)(2,1)S(1)}, bf16[256,2048]{1,0:T(8,128)(2,1)S(1)}, u32[]{:S(2)}, u32[]{:S(2)}) collective-permute-start(bf16[256,2048]{1,0:T(8,128)(2,1)S(1)} %get-tuple-element.444.refs_4_.refs_0_), channel_id=1, source_target_pairs={{0,64},{64,0},{1,65},{65,1},{2,66},{66,2},{3,67},{67,3},{4,68},{68... | collective-permute-start | bytes 3145736 | tf_op jit(solution)/shard_map/ppermute | solution.py:35
  13.2 19.3 %collective-permute-start.5 = (bf16[2,128,640]{2,1,0:T(8,128)(2,1)S(1)}, bf16[2,128,640]{2,1,0:T(8,128)(2,1)S(1)}, u32[]{:S(2)}, u32[]{:S(2)}) collective-permute-start(bf16[2,128,640]{2,1,0:T(8,128)(2,1)S(1)} %get-tuple-element.504.refs_0_), channel_id=1, source_target_pairs={{0,1},{1,2},{2,3},{3,0},{4,5},{5,6},{6,7},{7,4},{8,9},{9,10},{10,1... | collective-permute-start | bytes 983048 | tf_op jit(solution)/shard_map/ppermute | solution.py:31
  14.5 18.1 %collective-permute-start.4 = (bf16[2,128,640]{2,1,0:T(8,128)(2,1)S(1)}, bf16[2,128,640]{2,1,0:T(8,128)(2,1)S(1)}, u32[]{:S(2)}, u32[]{:S(2)}) collective-permute-start(bf16[2,128,640]{2,1,0:T(8,128)(2,1)S(1)} %get-tuple-element.504.refs_0_), channel_id=1, source_target_pairs={{0,2},{1,3},{2,0},{3,1},{4,6},{5,7},{6,4},{7,5},{8,10},{9,11},{10,... | collective-permute-start | bytes 983048 | tf_op jit(solution)/shard_map/ppermute | solution.py:31
  17.0 15.6 %collective-permute-start.3 = (bf16[2,128,640]{2,1,0:T(8,128)(2,1)S(1)}, bf16[2,128,640]{2,1,0:T(8,128)(2,1)S(1)}, u32[]{:S(2)}, u32[]{:S(2)}) collective-permute-start(bf16[2,128,640]{2,1,0:T(8,128)(2,1)S(1)} %get-tuple-element.504.refs_0_), channel_id=1, source_target_pairs={{0,3},{1,0},{2,1},{3,2},{4,7},{5,4},{6,5},{7,6},{8,11},{9,8},{10,9... | collective-permute-start | bytes 983048 | tf_op jit(solution)/shard_map/ppermute | solution.py:31
  44.1 15.4 %collective-permute-start.8 = (bf16[320,1024]{1,0:T(8,128)(2,1)S(1)}, bf16[320,1024]{1,0:T(8,128)(2,1)S(1)}, u32[]{:S(2)}, u32[]{:S(2)}) collective-permute-start(bf16[320,1024]{1,0:T(8,128)(2,1)S(1)} %get-tuple-element.386), channel_id=1, source_target_pairs={{0,16},{4,20},{8,24},{12,28},{16,0},{20,4},{24,8},{28,12},{32,48},... | collective-permute-start | bytes 1966088 | tf_op jit(solution)/shard_map/ppermute | solution.py:27
  45.4 16.3 %collective-permute-start.9 = (bf16[320,1024]{1,0:T(8,128)(2,1)S(1)}, bf16[320,1024]{1,0:T(8,128)(2,1)S(1)}, u32[]{:S(2)}, u32[]{:S(2)}) collective-permute-start(bf16[320,1024]{1,0:T(8,128)(2,1)S(1)} %get-tuple-element.387), channel_id=1, source_target_pairs={{0,48},{4,52},{8,56},{12,60},{16,32},{20,36},{24,40},{28,44},{32,1... | collective-permute-start | bytes 1966088 | tf_op jit(solution)/shard_map/ppermute | solution.py:27
  70.9 13.0 %collective-permute-start.14 = (bf16[320,1024]{1,0:T(8,128)(2,1)S(1)}, bf16[320,1024]{1,0:T(8,128)(2,1)S(1)}, u32[]{:S(2)}, u32[]{:S(2)}) collective-permute-start(bf16[320,1024]{1,0:T(8,128)(2,1)S(1)} %get-tuple-element.496), channel_id=1, source_target_pairs={{0,16},{4,20},{8,24},{12,28},{16,0},{20,4},{24,8},{28,12},{32,48},... | collective-permute-start | bytes 1966088 | tf_op jit(solution)/shard_map/ppermute | solution.py:27
  71.3 14.2 %collective-permute-start.15 = (bf16[320,1024]{1,0:T(8,128)(2,1)S(1)}, bf16[320,1024]{1,0:T(8,128)(2,1)S(1)}, u32[]{:S(2)}, u32[]{:S(2)}) collective-permute-start(bf16[320,1024]{1,0:T(8,128)(2,1)S(1)} %get-tuple-element.497), channel_id=1, source_target_pairs={{0,48},{4,52},{8,56},{12,60},{16,32},{20,36},{24,40},{28,44},{32,1... | collective-permute-start | bytes 1966088 | tf_op jit(solution)/shard_map/ppermute | solution.py:27
  72.6 13.0 %collective-permute-start.16 = (bf16[640,512]{1,0:T(8,128)(2,1)S(1)}, bf16[640,512]{1,0:T(8,128)(2,1)S(1)}, u32[]{:S(2)}, u32[]{:S(2)}) collective-permute-start(bf16[640,512]{1,0:T(8,128)(2,1)S(1)} %shard_map.83.refs_0_), channel_id=1, source_target_pairs={{0,8},{4,12},{8,0},{12,4},{16,24},{20,28},{24,16},{28,20},{32,40},... | collective-permute-start | bytes 1966088 | tf_op jit(solution)/shard_map/ppermute | solution.py:27
  73.6 14.2 %collective-permute-start.17 = (bf16[2,128,1280]{2,1,0:T(8,128)(2,1)S(1)}, bf16[2,128,1280]{2,1,0:T(8,128)(2,1)S(1)}, u32[]{:S(2)}, u32[]{:S(2)}) collective-permute-start(bf16[2,128,1280]{2,1,0:T(8,128)(2,1)S(1)} %get-tuple-element.540), channel_id=1, source_target_pairs={{0,2},{1,3},{2,0},{3,1},{4,6},{5,7},{6,4},{7,5},{8,10},{9,11},{10,... | collective-permute-start | bytes 1966088 | tf_op jit(solution)/shard_map/ppermute | solution.py:31
  87.8 22.1 %collective-permute-start.22 = (bf16[512,2048]{1,0:T(8,128)(2,1)S(1)}, bf16[512,2048]{1,0:T(8,128)(2,1)S(1)}, u32[]{:S(2)}, u32[]{:S(2)}) collective-permute-start(bf16[512,2048]{1,0:T(8,128)(2,1)S(1)} %get-tuple-element.550), channel_id=1, source_target_pairs={{0,4},{4,0},{8,12},{12,8},{16,20},{20,16},{24,28},{28,24},{32,36},... | collective-permute-start | bytes 6291464 | tf_op jit(solution)/shard_map/ppermute | solution.py:27
  93.6 16.2 %collective-permute-start.18 = (bf16[320,512]{1,0:T(8,128)(2,1)S(1)}, bf16[320,512]{1,0:T(8,128)(2,1)S(1)}, u32[]{:S(2)}, u32[]{:S(2)}) collective-permute-start(bf16[320,512]{1,0:T(8,128)(2,1)S(1)} %get-tuple-element.558.left_a), channel_id=1, source_target_pairs={{0,48},{4,52},{8,56},{12,60},{16,32},{20,36},{24,40},{28,44},{32,1... | collective-permute-start | bytes 983048 | tf_op jit(solution)/shard_map/ppermute | solution.py:27
  95.1 14.7 %collective-permute-start.19 = (bf16[320,512]{1,0:T(8,128)(2,1)S(1)}, bf16[320,512]{1,0:T(8,128)(2,1)S(1)}, u32[]{:S(2)}, u32[]{:S(2)}) collective-permute-start(bf16[320,512]{1,0:T(8,128)(2,1)S(1)} %get-tuple-element.559.left_b), channel_id=1, source_target_pairs={{0,16},{4,20},{8,24},{12,28},{16,0},{20,4},{24,8},{28,12},{32,48},... | collective-permute-start | bytes 983048 | tf_op jit(solution)/shard_map/ppermute | solution.py:27
  110.3 15.4 %collective-permute-start.23 = (bf16[320,1024]{1,0:T(8,128)(2,1)S(1)}, bf16[320,1024]{1,0:T(8,128)(2,1)S(1)}, u32[]{:S(2)}, u32[]{:S(2)}) collective-permute-start(bf16[320,1024]{1,0:T(8,128)(2,1)S(1)} %get-tuple-element.583), channel_id=1, source_target_pairs={{0,16},{4,20},{8,24},{12,28},{16,0},{20,4},{24,8},{28,12},{32,48},... | collective-permute-start | bytes 1966088 | tf_op jit(solution)/shard_map/ppermute | solution.py:27
  110.4 16.4 %collective-permute-start.24 = (bf16[320,1024]{1,0:T(8,128)(2,1)S(1)}, bf16[320,1024]{1,0:T(8,128)(2,1)S(1)}, u32[]{:S(2)}, u32[]{:S(2)}) collective-permute-start(bf16[320,1024]{1,0:T(8,128)(2,1)S(1)} %get-tuple-element.584), channel_id=1, source_target_pairs={{0,48},{4,52},{8,56},{12,60},{16,32},{20,36},{24,40},{28,44},{32,1... | collective-permute-start | bytes 1966088 | tf_op jit(solution)/shard_map/ppermute | solution.py:27
  111.8 14.9 %collective-permute-start.25 = (bf16[640,512]{1,0:T(8,128)(2,1)S(1)}, bf16[640,512]{1,0:T(8,128)(2,1)S(1)}, u32[]{:S(2)}, u32[]{:S(2)}) collective-permute-start(bf16[640,512]{1,0:T(8,128)(2,1)S(1)} %shard_map.88.refs_0_), channel_id=1, source_target_pairs={{0,8},{4,12},{8,0},{12,4},{16,24},{20,28},{24,16},{28,20},{32,40},... | collective-permute-start | bytes 1966088 | tf_op jit(solution)/shard_map/ppermute | solution.py:27
  112.3 15.6 %collective-permute-start.26 = (bf16[2,128,1280]{2,1,0:T(8,128)(2,1)S(1)}, bf16[2,128,1280]{2,1,0:T(8,128)(2,1)S(1)}, u32[]{:S(2)}, u32[]{:S(2)}) collective-permute-start(bf16[2,128,1280]{2,1,0:T(8,128)(2,1)S(1)} %get-tuple-element.606), channel_id=1, source_target_pairs={{0,1},{1,2},{2,3},{3,0},{4,5},{5,6},{6,7},{7,4},{8,9},{9,10},{10,1... | collective-permute-start | bytes 1966088 | tf_op jit(solution)/shard_map/ppermute | solution.py:31
  113.5 14.4 %collective-permute-start.27 = (bf16[2,128,1280]{2,1,0:T(8,128)(2,1)S(1)}, bf16[2,128,1280]{2,1,0:T(8,128)(2,1)S(1)}, u32[]{:S(2)}, u32[]{:S(2)}) collective-permute-start(bf16[2,128,1280]{2,1,0:T(8,128)(2,1)S(1)} %get-tuple-element.608), channel_id=1, source_target_pairs={{0,3},{1,0},{2,1},{3,2},{4,7},{5,4},{6,5},{7,6},{8,11},{9,8},{10,9... | collective-permute-start | bytes 1966088 | tf_op jit(solution)/shard_map/ppermute | solution.py:31
  127.9 15.8 %collective-permute-start.28 = (bf16[640,1024]{1,0:T(8,128)(2,1)S(1)}, bf16[640,1024]{1,0:T(8,128)(2,1)S(1)}, u32[]{:S(2)}, u32[]{:S(2)}) collective-permute-start(bf16[640,1024]{1,0:T(8,128)(2,1)S(1)} %get-tuple-element.656.refs_0_), channel_id=1, source_target_pairs={{0,4},{4,0},{8,12},{12,8},{16,20},{20,16},{24,28},{28,24},{32,36},... | collective-permute-start | bytes 3932168 | tf_op jit(solution)/shard_map/ppermute | solution.py:27
  130.6 13.1 %collective-permute-start.32 = (bf16[640,1024]{1,0:T(8,128)(2,1)S(1)}, bf16[640,1024]{1,0:T(8,128)(2,1)S(1)}, u32[]{:S(2)}, u32[]{:S(2)}) collective-permute-start(bf16[640,1024]{1,0:T(8,128)(2,1)S(1)} %shard_map.91.refs_2_), channel_id=1, source_target_pairs={{0,4},{4,0},{8,12},{12,8},{16,20},{20,16},{24,28},{28,24},{32,36},... | collective-permute-start | bytes 3932168 | tf_op jit(solution)/shard_map/ppermute | solution.py:27
  130.6 13.1 %collective-permute-start.29 = (bf16[112,2048]{1,0:T(8,128)(2,1)S(1)}, bf16[112,2048]{1,0:T(8,128)(2,1)S(1)}, u32[]{:S(2)}, u32[]{:S(2)}) collective-permute-start(bf16[112,2048]{1,0:T(8,128)(2,1)S(1)} %get-tuple-element.612), channel_id=1, source_target_pairs={{0,64},{64,0},{1,65},{65,1},{2,66},{66,2},{3,67},{67,3},{4,68},{68... | collective-permute-start | bytes 1376264 | tf_op jit(solution)/shard_map/ppermute | solution.py:35
  145.4 17.8 %collective-permute-start.34 = (bf16[320,1024]{1,0:T(8,128)(2,1)S(1)}, bf16[320,1024]{1,0:T(8,128)(2,1)S(1)}, u32[]{:S(2)}, u32[]{:S(2)}) collective-permute-start(bf16[320,1024]{1,0:T(8,128)(2,1)S(1)} %get-tuple-element.649), channel_id=1, source_target_pairs={{0,16},{4,20},{8,24},{12,28},{16,0},{20,4},{24,8},{28,12},{32,48},... | collective-permute-start | bytes 1966088 | tf_op jit(solution)/shard_map/ppermute | solution.py:27
  146.1 17.2 %collective-permute-start.35 = (bf16[320,1024]{1,0:T(8,128)(2,1)S(1)}, bf16[320,1024]{1,0:T(8,128)(2,1)S(1)}, u32[]{:S(2)}, u32[]{:S(2)}) collective-permute-start(bf16[320,1024]{1,0:T(8,128)(2,1)S(1)} %get-tuple-element.650), channel_id=1, source_target_pairs={{0,48},{4,52},{8,56},{12,60},{16,32},{20,36},{24,40},{28,44},{32,1... | collective-permute-start | bytes 1966088 | tf_op jit(solution)/shard_map/ppermute | solution.py:27
  147.4 15.7 %collective-permute-start.33 = (bf16[144,2048]{1,0:T(8,128)(2,1)S(1)}, bf16[144,2048]{1,0:T(8,128)(2,1)S(1)}, u32[]{:S(2)}, u32[]{:S(2)}) collective-permute-start(bf16[144,2048]{1,0:T(8,128)(2,1)S(1)} %get-tuple-element.647), channel_id=1, source_target_pairs={{0,64},{64,0},{1,65},{65,1},{2,66},{66,2},{3,67},{67,3},{4,68},{68... | collective-permute-start | bytes 1769480 | tf_op jit(solution)/shard_map/ppermute | solution.py:35
  (22 other events, 145.1 us)
